TPU v7x, 256 devices: a whole 4x4x8 slice. The times are simulated.
256 devices in a mesh: row: 8 (over z_lo, x), col: 32 (over y, z_hi, core).
Axes of the slice: x: 4, y: 4, z: 8 (z_hi: 4, z_lo: 2; z = z_hi * 2 + z_lo), core: 2. Of those that a mesh axis runs over, the one named last changes fastest.
Arguments:
- tokens: bfloat16 [4096, 6144], P('row', 'col'), may hold values from -6 to 6
- w_qkvg: bfloat16 [6144, 64, 512], P('row', 'col'), may hold values from -0.078125 to 0.078125
- w_out: bfloat16 [64, 128, 6144], P('col', None, 'row'), may hold values from -0.125 to 0.125
- norm_gain: float32 [64, 128], P('col'), may hold values from 0.1 to 1.9
- decay_index: int32 [64], P('col'), may hold values from 0 to 15
Outputs:
- mixed: bfloat16 [4096, 6144], P('row', 'col')
All inputs are finite; a program needn't handle non-finite values.
Results may differ from a plain program's by a relative error of at most 0.02.
Values may be sent and summed in bfloat16 or wider, within the bound.
No kernel may reach another device: no remote copies, remote signals or barrier semaphores. Data moves between devices by JAX's collectives and lax.ppermute only.
A program may use at most 128 MiB of HBM per device.

v0:
```python
import math

import jax
import jax.numpy as jnp
from jax import lax
from jax.sharding import PartitionSpec as P

NSLOPE = 16


def carried_in(shard, axis, join, neutral):
    place = lax.axis_index(axis)
    gathered = jax.tree.map(
        lambda a, kind: lax.all_gather(a.astype(kind), axis), shard, (jnp.bfloat16, jnp.bfloat16)
    )
    state = jax.tree.map(lambda a, e: jnp.zeros_like(a) + jnp.asarray(e, a.dtype), shard, neutral)

    def one(turn, state):
        return join(
            state,
            jax.tree.map(
                lambda a, own: lax.dynamic_index_in_dim(a, turn, 0, False).astype(own.dtype),
                gathered,
                shard,
            ),
        )

    return lax.fori_loop(0, place, one, state)


def decay_rates(index_vec, total_rows):
    exponent = index_vec.astype(jnp.float32) / (NSLOPE - 1)
    fast_rate = 1.0 / 32.0
    slow_rate = 0.5 / total_rows
    return fast_rate * jnp.exp(exponent * math.log(slow_rate / fast_rate))


def local(tokens, w_qkvg, w_out, norm_gain, decay_index):
    block_rows = tokens.shape[0]
    row_count = lax.axis_size("row")
    local_heads = w_qkvg.shape[1]
    head_size = w_qkvg.shape[2] // 4
    gathered = lax.all_gather(tokens, "col", axis=1, tiled=True)
    portion = lax.all_gather(w_qkvg, "row", axis=0, tiled=True)
    projected = jnp.dot(
        gathered,
        portion.reshape(portion.shape[0], local_heads * 4 * head_size),
        preferred_element_type=jnp.float32,
    )
    projected = projected.astype(jnp.bfloat16).reshape(block_rows, local_heads, 4, head_size)
    activated = jax.nn.silu(projected[:, :, :3].astype(jnp.float32))
    queries = activated[:, :, 0]
    keys_act = activated[:, :, 1]
    values_act = activated[:, :, 2]
    gate_part = projected[:, :, 3].astype(jnp.float32)
    rate_vec = decay_rates(decay_index, block_rows * row_count)
    local_pos = jnp.arange(block_rows, dtype=jnp.float32)
    distance = local_pos[:, None] - local_pos[None, :]
    weight = jnp.where(
        distance[None] >= 0,
        jnp.exp(-rate_vec[:, None, None] * jnp.maximum(distance, 0.0)[None]),
        0.0,
    )
    scores = jnp.einsum("thd,shd->hts", queries, keys_act, precision=lax.Precision.HIGHEST) * weight
    inner_part = jnp.einsum("hts,shd->thd", scores, values_act, precision=lax.Precision.HIGHEST)
    state_weight = jnp.exp(-rate_vec[:, None] * (block_rows - 1.0 - local_pos)[None])
    local_state = jnp.einsum(
        "hs,shd,she->hde", state_weight, keys_act, values_act, precision=lax.Precision.HIGHEST
    )
    block_decay = jnp.exp(-rate_vec * block_rows)

    def combine(earlier, later):
        return (earlier[0] * later[0], later[0][:, None, None] * earlier[1] + later[1])

    identity = (jnp.ones_like(block_decay), jnp.zeros_like(local_state))
    carried = carried_in((block_decay, local_state), "row", combine, identity)[1]
    entry_decay = jnp.exp(-rate_vec[None, :] * (local_pos[:, None] + 1.0))
    carried_part = entry_decay[:, :, None] * jnp.einsum(
        "thd,hde->the", queries, carried, precision=lax.Precision.HIGHEST
    )
    attended = inner_part + carried_part
    mean_square = jnp.mean(attended * attended, axis=-1, keepdims=True)
    normed = attended * lax.rsqrt(mean_square + 1e-06) * norm_gain[None]
    hidden = (normed * jax.nn.sigmoid(gate_part)).astype(jnp.bfloat16)
    partial_terms = jnp.einsum(
        "thd,hdc->tc",
        hidden,
        lax.all_gather(w_out, "row", axis=2, tiled=True),
        preferred_element_type=jnp.float32,
    )
    return lax.psum_scatter(
        partial_terms.astype(jnp.bfloat16), "col", scatter_dimension=1, tiled=True
    )


def solution(mesh):
    in_specs = (
        P("row", "col"),
        P("row", "col", None),
        P("col", None, "row"),
        P("col", None),
        P("col"),
    )
    out_specs = P("row", "col")
    return jax.shard_map(local, mesh=mesh, in_specs=in_specs, out_specs=out_specs, check_vma=False)
```

profile of v0, /device:TPU:4, one launch (start us, length us, event | category | flops | bytes accessed | tf_op | source)
XLA Modules:
  0.0 388.3 jit_solution(10462269563590822355)
XLA Ops:
  6.5 0.7 all-gather.8.cloned.1.call-update
  7.3 0.7 all-gather.6.cloned.1.call-update
  8.1 1.9 copy.25
  10.1 1.2 fusion.16
  11.3 0.2 fusion.17
  11.6 0.6 dynamic-slice
  12.8 0.2 dynamic-update-slice
  13.1 17.1 %all-reduce = bf16[16]{0:T(256)(128)(2,1)S(1)} all-reduce(bf16[16]{0:T(256)(128)(2,1)S(1)} %dynamic-update-slice), channel_id=2, replica_groups=mesh['row'=8,'col'=32] {'row'}, use_global_device_ids=true, to_apply=%add | all-reduce | flops 16 | bytes 64
  30.4 113.0 %all-gather.8.cloned.1.call-done = bf16[6144,2,512]{2,1,0:T(2,128)(2,1)} async-done(((bf16[768,2,512]{2,1,0:T(2,128)(2,1)}), bf16[6144,2,512]{2,1,0:T(2,128)(2,1)}) %all-gather.8.cloned.1.call-update) | async-done | bytes 12582928 | tf_op jit(solution)/shard_map/all_gather | solution.py:44
  143.4 12.6 %copy.33 = bf16[768,8,2,512]{3,1,2,0:T(8,128)(2,1)} copy(bf16[768,8,2,512]{3,2,1,0:T(2,128)(2,1)} %bitcast.52) | data formatting | bytes 25165824
  156.1 60.2 %all-gather.6.cloned.1.call-done = bf16[512,6144]{0,1:T(8,128)(2,1)} async-done(((bf16[512,192]{0,1:T(8,128)(2,1)}), bf16[512,6144]{0,1:T(8,128)(2,1)}) %all-gather.6.cloned.1.call-update) | async-done | bytes 6291472 | tf_op jit(solution)/shard_map/all_gather | solution.py:43
  216.2 11.5 %convolution_convert_fusion = bf16[512,1024]{1,0:T(8,128)(2,1)S(1)} fusion(bf16[512,6144]{0,1:T(8,128)(2,1)} %all-gather.6.cloned.1.call-done, bf16[6144,1024]{1,0:T(8,128)(2,1)} %bitcast.53), kind=kOutput, calls=%fused_computation.13 | convolution fusion | flops 6442975232 | bytes 19922944 | tf_op jit(solution)/shard_map/dot_general | solution.py:45
  227.8 0.8 reshape.95
  228.5 0.6 slice.24
  229.1 0.7 copy.32
  229.8 0.4 convert_multiply_fusion
  230.2 1.2 convolution_convert_fusion.1
  231.4 28.4 %all-gather.1 = bf16[16,128,128]{2,1,0:T(8,128)(2,1)S(1)} all-gather(bf16[2,128,128]{2,1,0:T(8,128)(2,1)S(1)} %convolution_convert_fusion.1), channel_id=3, replica_groups=mesh['row'=8,'col'=32] {'row'}, dimensions={0}, use_global_device_ids=true | all-gather | bytes 589824 | tf_op jit(solution)/shard_map/all_gather | solution.py:14
  259.8 1.8 fusion.21
  261.6 2.9 fusion.8
  264.6 0.3 while.12
  264.8 0.7 multiply_reduce_fusion
  265.6 5.8 %bitcast_convert_fusion.1 = bf16[512,6144]{0,1:T(8,128)(2,1)} fusion(bf16[2,128,6144]{1,2,0:T(8,128)(2,1)} %all-gather.10.cloned.1.call-done, bf16[512,2,1,128]{0,3,1,2:T(8,128)(2,1)S(1)} %copy.32, f32[512,2,128]{0,2,1:T(8,128)S(1)} %get-tuple-element.63, f32[2,128]{1,0:T(2,128)S(1)} %copy-done.1, f32[512,2]{0,1:T(2,128)S(1)} %add_rsqrt_fusion), kind=kOutput, calls=%fused_computation.2 | convolution fusion | flops 1614807040 | bytes 10228736 | tf_op jit(solution)/shard_map/thd,hdc->tc/dot_general | solution.py:85
  271.4 110.4 %reduce-scatter.2.cloned.1.call-done = bf16[512,192]{0,1:T(8,128)(2,1)} async-done(((bf16[512,6144]{0,1:T(8,128)(2,1)}), bf16[512,192]{0,1:T(8,128)(2,1)}) %reduce-scatter.2.cloned.1.call-update) | async-done | bytes 196624 | tf_op jit(solution)/shard_map/reduce_scatter | solution.py:91
  (28 shorter events, 0.7 us)
Async XLA Ops:
  6.5 5.0 %copy-start.3 = (u32[256]{0:T(256)S(1)}, u32[256]{0:T(256)}, u32[]{:S(2)}) copy-start(u32[256]{0:T(256)} %constant.56) | copy-start | bytes 3076
  6.5 5.0 %copy-start.2 = (s32[2]{0:T(128)S(1)}, s32[2]{0:T(128)}, u32[]{:S(2)}) copy-start(s32[2]{0:T(128)} %param.11) | copy-start | bytes 28
  6.5 136.9 %all-gather.8.cloned.1.call-start = ((), (), s32[]{:S(2)}) async-start(), calls=%async_computation.2 | async-start | bytes 14155776 | tf_op jit(solution)/shard_map/all_gather | solution.py:44
  7.3 209.0 %all-gather.6.cloned.1.call-start = ((), (), s32[]{:S(2)}) async-start(), calls=%async_computation.1 | async-start | bytes 6488064 | tf_op jit(solution)/shard_map/all_gather | solution.py:43
  8.0 257.6 %all-gather.10.cloned.1.call-start = ((), (), s32[]{:S(2)}) async-start(), calls=%async_computation.3 | async-start | bytes 3538944 | tf_op jit(solution)/shard_map/all_gather | solution.py:88
  10.0 371.8 %reduce-scatter.2.cloned.1.call-start = ((), (), s32[]{:S(2)}) async-start(), calls=%async_computation.4 | async-start | bytes 6488064 | tf_op jit(solution)/shard_map/reduce_scatter | solution.py:91
  231.4 30.2 %copy-start = (f32[512,512]{1,0:T(8,128)S(1)}, f32[512,512]{1,0:T(8,128)}, u32[]{:S(2)}) copy-start(f32[512,512]{1,0:T(8,128)} %fusion.16) | copy-start | bytes 3145732
  264.5 1.1 copy-start.1
Sparse Core Ops, SparseCore 0:
  9.1 134.2 all-gather.7
  146.0 70.2 all-gather.5
  218.0 46.6 all-gather.9
  271.5 110.2 reduce-scatter.1
where the time goes:
time: 389 us; the launch traced here: 388 us
  waiting for transfers between devices  285 us (73%)
  blocking collectives  45.5 us (12%)
  matrix products  23.9 us (6%)
  local copies, waits for them, and re-layouts  17.5 us (4%)
  between operations  14 us (4%)
    all_gather x1, waiting for transfers between devices, local(): portion = lax.all_gather(w_qkvg, 'row', axis=0, tiled=True)  113 us
    reduce_scatter x1, waiting for transfers between devices, local(): lax.psum_scatter(partial_terms.astype(jnp.bfloat16), 'col', scatter_dimen...  110 us
    all_gather x1, waiting for transfers between devices, local(): gathered = lax.all_gather(tokens, 'col', axis=1, tiled=True)  60.2 us
    all_gather x1, blocking collectives, carried_in(): lax.all_gather(a.astype(kind), axis)  28.4 us
    unnamed x1, blocking collectives  17.1 us
    unnamed x14, local copies, waits for them, and re-layouts  16.1 us
    dot_general x1, matrix products, local(): jnp.dot(gathered, portion.reshape(portion.shape[0], local_heads * 4 * hea...  11.5 us
  transfers between devices with their start and end apart: 4, of which 3 were waited for; matrix products, arithmetic and copies ran while one was open for 10% of the time, Pallas kernels for 0%

commit v1 on v0

v1 whole, which is shorter than its diff:
```python
import math

import jax
import jax.numpy as jnp
import numpy as np
from jax import lax
from jax.sharding import Mesh
from jax.sharding import PartitionSpec as P

NSLOPE = 16
AXES = ("zl", "x", "y", "zh", "core")
SIZES = (2, 4, 4, 4, 2)
BF = jnp.bfloat16
F32 = jnp.float32


def moves(target):
    pairs = []
    for flat in range(int(np.prod(SIZES))):
        place = [int(v) for v in np.unravel_index(flat, SIZES)]
        there = target(*place)
        if there is not None:
            pairs.append((flat, int(np.ravel_multi_index(there, SIZES))))
    return pairs


def send(array, target):
    return lax.ppermute(array, AXES, moves(target))


def along_x(step):
    return lambda zl, x, y, zh, c: (zl, (x + step) % 4, y, zh, c)


def along_y(step):
    return lambda zl, x, y, zh, c: (zl, x, (y + step) % 4, zh, c)


def along_zh(step):
    return lambda zl, x, y, zh, c: (zl, x, y, (zh + step) % 4, c)


def other_zl(zl, x, y, zh, c):
    return (1 - zl, x, y, zh, c)


def other_core(zl, x, y, zh, c):
    return (zl, x, y, zh, 1 - c)


def later_row(step):
    def target(zl, x, y, zh, c):
        row = zl * 4 + x + step
        return (row // 4, row % 4, y, zh, c) if row < 8 else None

    return target


def tokens_to_half(zl, x, y, zh, c):
    half = y // 2
    return (half, x, (zl ^ half) * 2 + y % 2, zh, c)


def w_out_to_columns(zl, x, y, zh, c):
    row = zl * 4 + x
    return (row % 2, y, row // 2, zh, c)


def gather_x(block):
    place = lax.axis_index("x")
    rows, columns = block.shape
    half = rows // 2
    low, high = block[:half], block[half:]
    left_low = send(low, along_x(1))
    right_high = send(high, along_x(-1))
    left_high = send(high, along_x(1))
    right_low = send(low, along_x(-1))
    far_low = send(left_low, along_x(1))
    far_high = send(right_high, along_x(-1))
    whole = jnp.zeros((4 * rows, columns), block.dtype)
    left = (place + 3) % 4 * rows
    right = (place + 1) % 4 * rows
    far = (place + 2) % 4 * rows
    for piece, start in (
        (block, place * rows),
        (left_low, left),
        (left_high, left + half),
        (right_low, right),
        (right_high, right + half),
        (far_low, far),
        (far_high, far + half),
    ):
        whole = lax.dynamic_update_slice(whole, piece, (start, 0))
    return whole


def decay_rates(index_vec, total_rows):
    exponent = index_vec.astype(F32) / (NSLOPE - 1)
    fast_rate = 1.0 / 32.0
    slow_rate = 0.5 / total_rows
    return fast_rate * jnp.exp(exponent * math.log(slow_rate / fast_rate))


def local(tokens, w_qkvg, w_out, norm_gain, decay_index):
    rows = tokens.shape[0]
    heads = w_qkvg.shape[1]
    size = w_qkvg.shape[2] // 4
    core = lax.axis_index("core")
    zh = lax.axis_index("zh")
    y = lax.axis_index("y")

    moved = send(tokens, tokens_to_half)
    gathered = lax.all_gather(moved, ("y", "zh", "core"), axis=1, tiled=True)
    width = gathered.shape[1] // 2
    mine, theirs = gathered[:, :width], gathered[:, width:]

    parts = w_qkvg.reshape(-1, heads, 4, size)
    kv_block = parts[:, :, 1:3].reshape(-1, heads * 2 * size)
    qg_block = jnp.stack([parts[:, :, 0], parts[:, :, 3]], axis=2).reshape(-1, heads * 2 * size)
    weight_cols = gather_x(jnp.concatenate([kv_block, qg_block], axis=1))
    w_kv, w_qg = weight_cols[:, : heads * 2 * size], weight_cols[:, heads * 2 * size :]

    w_out_moved = send(w_out.reshape(heads * size, -1), w_out_to_columns)
    w_out_all = lax.all_gather(w_out_moved, ("zl", "x"), axis=0, tiled=True)

    def half_dot(a, b):
        return jnp.dot(a, b, preferred_element_type=F32)

    kv_sent = send(half_dot(theirs, w_kv).astype(BF), other_zl)
    qg_sent = send(half_dot(theirs, w_qg).astype(BF), other_zl)
    kv = (half_dot(mine, w_kv) + kv_sent.astype(F32)).astype(BF).astype(F32)
    qg = (half_dot(mine, w_qg) + qg_sent.astype(F32)).astype(BF).astype(F32)

    kv = jax.nn.silu(kv).reshape(rows, heads, 2, size)
    keys_act, values_act = kv[:, :, 0], kv[:, :, 1].astype(BF)
    rate_vec = decay_rates(decay_index, rows * 8)
    local_pos = jnp.arange(rows, dtype=F32)
    state_weight = jnp.exp(-rate_vec[None, :] * (rows - 1.0 - local_pos)[:, None])
    local_state = jnp.einsum(
        "shd,she->hde",
        (keys_act * state_weight[:, :, None]).astype(BF),
        values_act,
        preferred_element_type=F32,
    ).astype(BF)
    keys_act = keys_act.astype(BF)
    carried = jnp.zeros(local_state.shape, F32)
    for step in range(1, 8):
        earlier = send(local_state, later_row(step)).astype(F32)
        carried += jnp.exp(-rate_vec * (rows * (step - 1.0)))[:, None, None] * earlier

    qg = qg.reshape(rows, heads, 2, size)
    queries, gate_part = jax.nn.silu(qg[:, :, 0]).astype(BF), qg[:, :, 1]
    distance = local_pos[:, None] - local_pos[None, :]
    weight = jnp.where(
        distance[None] >= 0,
        jnp.exp(-rate_vec[:, None, None] * jnp.maximum(distance, 0.0)[None]),
        0.0,
    )
    scores = jnp.einsum("thd,shd->hts", queries, keys_act, preferred_element_type=F32) * weight
    inner_part = jnp.einsum(
        "hts,shd->thd", scores.astype(BF), values_act, preferred_element_type=F32
    )
    entry_decay = jnp.exp(-rate_vec[None, :] * (local_pos[:, None] + 1.0))
    carried_part = entry_decay[:, :, None] * jnp.einsum(
        "thd,hde->the", queries, carried.astype(BF), preferred_element_type=F32
    )
    attended = inner_part + carried_part
    mean_square = jnp.mean(attended * attended, axis=-1, keepdims=True)
    normed = attended * lax.rsqrt(mean_square + 1e-06) * norm_gain[None]
    hidden = (normed * jax.nn.sigmoid(gate_part)).astype(BF).reshape(rows, heads * size)

    hidden_all = jnp.zeros((rows, 4 * heads * size), BF)
    hidden_all = lax.dynamic_update_slice(hidden_all, hidden, (0, y * heads * size))
    for step in (2, 1, 3):
        piece = send(hidden, along_y(step))
        hidden_all = lax.dynamic_update_slice(hidden_all, piece, (0, (y + 4 - step) % 4 * heads * size))

    depth = 4 * heads * size
    wide = [
        half_dot(hidden_all, w_out_all[part * depth : (part + 1) * depth]).reshape(rows, 2, 2, -1)
        for part in range(2)
    ]
    blocks = jnp.stack([wide[part][:, turn] for part in range(2) for turn in range(2)])
    kept = jnp.where(core == 0, blocks[:, :, 0], blocks[:, :, 1])
    given = jnp.where(core == 0, blocks[:, :, 1], blocks[:, :, 0]).astype(BF)
    summed = kept + send(given, other_core).astype(F32)
    total = lax.dynamic_index_in_dim(summed, zh, 0, False)
    outgoing = summed.astype(BF)
    for step in (2, 1, 3):
        piece = lax.dynamic_index_in_dim(outgoing, (zh + step) % 4, 0, False)
        total += send(piece, along_zh(step)).astype(F32)
    return total.astype(BF)


def solution(mesh):
    fine = Mesh(mesh.devices.reshape(SIZES), AXES)
    row, col = ("zl", "x"), ("y", "zh", "core")
    in_specs = (P(row, col), P(row, col, None), P(col, None, row), P(col, None), P(col))
    return jax.shard_map(
        local, mesh=fine, in_specs=in_specs, out_specs=P(row, col), check_vma=False
    )
```

time: 389 us -> 231 us (0.59)
  waiting for transfers between devices: 285 us -> 89.5 us
  starting transfers between devices: 0.12 us -> 70.9 us
  blocking collectives: 45.5 us -> 0 us
  other arithmetic: 2.26 us -> 9.55 us
  local copies, waits for them, and re-layouts: 17.5 us -> 24.5 us
  matrix products: 23.9 us -> 19.8 us
    all_gather x3 -> x2, waiting for transfers between devices: 173 us -> 0.02 us  [the longest x1 0.02 us: local(): w_out_all = lax.all_gather(w_out_moved, ('zl', 'x'), axis=0, tiled=True)]
    reduce_scatter x1 -> x0, waiting for transfers between devices: 110 us -> none  [local(): lax.psum_scatter(partial_terms.astype(jnp.bfloat16), 'col', scatter_dimen...]
    ppermute x0 -> x24, waiting for transfers between devices: none -> 89.5 us  [send(): return lax.ppermute(array, AXES, moves(target))]
    ppermute x0 -> x24, starting transfers between devices: none -> 70.8 us  [send(): return lax.ppermute(array, AXES, moves(target))]
    all_gather x1 -> x0, blocking collectives: 28.4 us -> none  [carried_in(): lax.all_gather(a.astype(kind), axis)]
    unnamed x1 -> x0, blocking collectives: 17.1 us -> none
    dynamic_update_slice x0 -> x11, local copies, waits for them, and re-layouts: none -> 10.7 us  [the longest x7 10.6 us: gather_x(): whole = lax.dynamic_update_slice(whole, piece, (start, 0))]
    unnamed x14 -> x22, local copies, waits for them, and re-layouts: 16.1 us -> 5.85 us
  transfers between devices with their start and end apart: 4 -> 26, of which waited for: 3 -> 12; matrix products, arithmetic and copies ran while one was open for 10% -> 17% of each run, Pallas kernels for 0% -> 0%
where the time goes in v1:
time: 231 us; the launch traced here: 228 us
  waiting for transfers between devices  89.5 us (39%)
  starting transfers between devices  70.9 us (31%)
  local copies, waits for them, and re-layouts  24.5 us (11%)
  matrix products  19.8 us (9%)
  between operations  13.9 us (6%)
  other arithmetic  9.55 us (4%)
    ppermute x24, waiting for transfers between devices, send(): return lax.ppermute(array, AXES, moves(target))  89.5 us
    ppermute x24, starting transfers between devices, send(): return lax.ppermute(array, AXES, moves(target))  70.8 us
    dot_general x6, matrix products, half_dot(): return jnp.dot(a, b, preferred_element_type=F32)  14 us
    dynamic_update_slice x7, local copies, waits for them, and re-layouts, gather_x(): whole = lax.dynamic_update_slice(whole, piece, (start, 0))  10.6 us
    unnamed x22, local copies, waits for them, and re-layouts  5.85 us
  transfers between devices with their start and end apart: 26, of which 12 were waited for; matrix products, arithmetic and copies ran while one was open for 17% of the time, Pallas kernels for 0%

profile of v1, /device:TPU:4, one launch (start us, length us, event | category | flops | bytes accessed | tf_op | source)
XLA Modules:
  0.0 228.1 jit_solution(18207035463642586828)
XLA Ops:
  8.9 2.8 %reshape.146 = bf16[768,2,4,128]{3,2,1,0:T(4,128)(2,1)S(1)} reshape(bf16[768,2,512]{2,1,0:T(2,128)(2,1)} %param.6) | data formatting | bytes 3145728 | tf_op jit(solution)/shard_map/reshape | solution.py:117
  21.6 5.8 %collective-permute-start.19 = (bf16[256,768]{1,0:T(8,128)(2,1)}, bf16[256,768]{1,0:T(8,128)(2,1)}, u32[]{:S(2)}, u32[]{:S(2)}) collective-permute-start(bf16[256,768]{1,0:T(8,128)(2,1)} %bitcast.14), channel_id=1, source_target_pairs={{0,0},{1,1},{2,2},{3,3},{4,4},{5,5},{6,6},{7,7},{8,32},{9,33},{10,... | collective-permute-start | bytes 1179656 | tf_op jit(solution)/shard_map/ppermute | solution.py:28
  27.6 10.5 %collective-permute-done = bf16[384,1024]{1,0:T(8,128)(2,1)S(1)} collective-permute-done((bf16[384,1024]{1,0:T(8,128)(2,1)}, bf16[384,1024]{1,0:T(8,128)(2,1)S(1)}, u32[]{:S(2)}, u32[]{:S(2)}) %collective-permute-start) | collective-permute-done | bytes 786464 | tf_op jit(solution)/shard_map/ppermute | solution.py:28
  40.4 2.7 %copy-done = bf16[3072,1024]{1,0:T(8,128)(2,1)} copy-done((bf16[3072,1024]{1,0:T(8,128)(2,1)}, bf16[3072,1024]{1,0:T(8,128)(2,1)S(1)}, u32[]{:S(2)}) %copy-start) | copy-done | bytes 6291480
  43.1 11.8 %collective-permute-done.3 = bf16[384,1024]{1,0:T(8,128)(2,1)} collective-permute-done((bf16[384,1024]{1,0:T(8,128)(2,1)}, bf16[384,1024]{1,0:T(8,128)(2,1)}, u32[]{:S(2)}, u32[]{:S(2)}) %collective-permute-start.3) | collective-permute-done | bytes 786464 | tf_op jit(solution)/shard_map/ppermute | solution.py:28
  55.9 28.3 %collective-permute-done.19 = bf16[256,768]{1,0:T(8,128)(2,1)} collective-permute-done((bf16[256,768]{1,0:T(8,128)(2,1)}, bf16[256,768]{1,0:T(8,128)(2,1)}, u32[]{:S(2)}, u32[]{:S(2)}) %collective-permute-start.19) | collective-permute-done | bytes 393248 | tf_op jit(solution)/shard_map/ppermute | solution.py:28
  94.7 4.8 %fusion.62 = bf16[512,512]{0,1:T(8,128)(2,1)S(1)} fusion(bf16[512,6144]{0,1:T(8,128)(2,1)} %all-gather.3.cloned.1.call-done, bf16[3072,1024]{1,0:T(8,128)(2,1)} %constant_dynamic-update-slice_fusion.6), kind=kOutput, calls=%fused_computation.32 | convolution fusion | flops 1610874880 | bytes 6815744 | tf_op jit(solution)/shard_map/dot_general | solution.py:127
  103.6 10.9 %collective-permute-done.7 = bf16[512,512]{0,1:T(8,128)(2,1)S(1)} collective-permute-done((bf16[512,512]{0,1:T(8,128)(2,1)S(1)}, bf16[512,512]{0,1:T(8,128)(2,1)S(1)}, u32[]{:S(2)}, u32[]{:S(2)}) %collective-permute-start.7) | collective-permute-done | bytes 524320 | tf_op jit(solution)/shard_map/ppermute | solution.py:28
  116.7 17.9 %collective-permute-start.10 = (bf16[2,128,128]{2,1,0:T(8,128)(2,1)S(1)}, bf16[2,128,128]{2,1,0:T(8,128)(2,1)S(1)}, u32[]{:S(2)}, u32[]{:S(2)}) collective-permute-start(bf16[2,128,128]{2,1,0:T(8,128)(2,1)S(1)} %convolution_convert_fusion), channel_id=1, source_target_pairs={{0,64},{1,65},{2,66},{3,67},{4,68},{5,69},{6,70},{7,71},{8,72},{9,... | collective-permute-start | bytes 196616 | tf_op jit(solution)/shard_map/ppermute | solution.py:28
  134.6 2.8 %collective-permute-start.11 = (bf16[2,128,128]{2,1,0:T(8,128)(2,1)S(1)}, bf16[2,128,128]{2,1,0:T(8,128)(2,1)S(1)}, u32[]{:S(2)}, u32[]{:S(2)}) collective-permute-start(bf16[2,128,128]{2,1,0:T(8,128)(2,1)S(1)} %convolution_convert_fusion), channel_id=1, source_target_pairs={{0,96},{1,97},{2,98},{3,99},{4,100},{5,101},{6,102},{7,103},{8,104... | collective-permute-start | bytes 196616 | tf_op jit(solution)/shard_map/ppermute | solution.py:28
  144.7 12.9 %collective-permute-start.9 = (bf16[2,128,128]{2,1,0:T(8,128)(2,1)S(1)}, bf16[2,128,128]{2,1,0:T(8,128)(2,1)}, u32[]{:S(2)}, u32[]{:S(2)}) collective-permute-start(bf16[2,128,128]{2,1,0:T(8,128)(2,1)S(1)} %convolution_convert_fusion), channel_id=1, source_target_pairs={{0,32},{1,33},{2,34},{3,35},{4,36},{5,37},{6,38},{7,39},{8,40},{9,... | collective-permute-start | bytes 196616 | tf_op jit(solution)/shard_map/ppermute | solution.py:28
  159.9 2.6 %collective-permute-done.9 = bf16[2,128,128]{2,1,0:T(8,128)(2,1)} collective-permute-done((bf16[2,128,128]{2,1,0:T(8,128)(2,1)S(1)}, bf16[2,128,128]{2,1,0:T(8,128)(2,1)}, u32[]{:S(2)}, u32[]{:S(2)}) %collective-permute-start.9) | collective-permute-done | bytes 65568 | tf_op jit(solution)/shard_map/ppermute | solution.py:28
  164.8 3.2 %multiply_reduce_fusion = (f32[512,2]{0,1:T(2,128)S(1)}, f32[512,2,128]{0,2,1:T(8,128)}) fusion(f32[512,2,128]{0,2,1:T(8,128)} %fusion.69, f32[512,512]{1,0:T(8,128)S(1)} %fusion.76, f32[2]{0:T(128)S(1)} %get-tuple-element.8, pred[512,512]{1,0:T(8,128)(4,1)S(1)} %fusion.77, f32[512,2,1,128]{3,0,1,2:T(8,128)S(1)} %copy.35, f32[512,2,2,128]{0,3,2,1:T(8,128)} %bitcast.124), kind=kOutput, calls=%fused_computation.68 | convolution fusion | flops 271580160 | bytes 3674120 | tf_op jit(solution)/shard_map/hts,shd->thd/dot_general | solution.py:160
  169.3 5.1 %collective-permute-start.17 = (bf16[512,256]{0,1:T(8,128)(2,1)S(1)}, bf16[512,256]{0,1:T(8,128)(2,1)S(1)}, u32[]{:S(2)}, u32[]{:S(2)}) collective-permute-start(bf16[512,256]{0,1:T(8,128)(2,1)S(1)} %bitcast.126), channel_id=1, source_target_pairs={{0,8},{1,9},{2,10},{3,11},{4,12},{5,13},{6,14},{7,15},{8,16},{9,17... | collective-permute-start | bytes 786440 | tf_op jit(solution)/shard_map/ppermute | solution.py:28
  174.5 2.8 %collective-permute-done.16 = bf16[512,256]{0,1:T(8,128)(2,1)S(1)} collective-permute-done((bf16[512,256]{0,1:T(8,128)(2,1)S(1)}, bf16[512,256]{0,1:T(8,128)(2,1)S(1)}, u32[]{:S(2)}, u32[]{:S(2)}) %collective-permute-start.16) | collective-permute-done | bytes 262176 | tf_op jit(solution)/shard_map/ppermute | solution.py:28
  177.3 2.7 %collective-permute-done.17 = bf16[512,256]{0,1:T(8,128)(2,1)S(1)} collective-permute-done((bf16[512,256]{0,1:T(8,128)(2,1)S(1)}, bf16[512,256]{0,1:T(8,128)(2,1)S(1)}, u32[]{:S(2)}, u32[]{:S(2)}) %collective-permute-start.17) | collective-permute-done | bytes 262176 | tf_op jit(solution)/shard_map/ppermute | solution.py:28
  181.7 2.6 %fusion.14 = f32[512,768]{0,1:T(8,128)S(1)} fusion(bf16[512,1024]{0,1:T(8,128)(2,1)S(1)} %constant_dynamic-update-slice_fusion.2, bf16[2048,768]{1,0:T(8,128)(2,1)} %all-gather.5.cloned.1.call-done), kind=kOutput, calls=%fused_computation.16 | convolution fusion | flops 805306368 | bytes 4194304 | tf_op jit(solution)/shard_map/dot_general | solution.py:127
  187.0 2.6 %collective-permute-done.20 = bf16[4,512,192]{1,2,0:T(8,128)(2,1)} collective-permute-done((bf16[4,512,192]{1,2,0:T(8,128)(2,1)}, bf16[4,512,192]{1,2,0:T(8,128)(2,1)}, u32[]{:S(2)}, u32[]{:S(2)}) %collective-permute-start.20) | collective-permute-done | bytes 786464 | tf_op jit(solution)/shard_map/ppermute | solution.py:28
  189.6 2.8 %fusion.116 = (bf16[4,512,192]{1,2,0:T(8,128)(2,1)S(1)}, f32[4,512,192]{1,2,0:T(8,128)}) fusion(bf16[4,512,192]{1,2,0:T(8,128)(2,1)} %collective-permute-done.20, f32[4,512,2,192]{1,3,2,0:T(8,128)S(1)} %pad_maximum_fusion, pred[]{:T(512)S(6)} %eq.14), kind=kLoop, calls=%fused_computation.117 | loop fusion | flops 1572864 | bytes 6291457 | tf_op jit(solution)/shard_map/convert_element_type | solution.py:188
  192.4 7.5 %collective-permute-start.21 = (bf16[512,192]{0,1:T(8,128)(2,1)S(1)}, bf16[512,192]{0,1:T(8,128)(2,1)S(1)}, u32[]{:S(2)}, u32[]{:S(2)}) collective-permute-start(bf16[512,192]{0,1:T(8,128)(2,1)S(1)} %get-tuple-element.17), channel_id=1, source_target_pairs={{0,4},{1,5},{2,6},{3,7},{4,0},{5,1},{6,2},{7,3},{8,12},{9,13},{10,... | collective-permute-start | bytes 589832 | tf_op jit(solution)/shard_map/ppermute | solution.py:28
  201.4 2.6 %collective-permute-start.23 = (bf16[512,192]{0,1:T(8,128)(2,1)S(1)}, bf16[512,192]{0,1:T(8,128)(2,1)S(1)}, u32[]{:S(2)}, u32[]{:S(2)}) collective-permute-start(bf16[512,192]{0,1:T(8,128)(2,1)S(1)} %get-tuple-element.18), channel_id=1, source_target_pairs={{0,6},{1,7},{2,0},{3,1},{4,2},{5,3},{6,4},{7,5},{8,14},{9,15},{10,... | collective-permute-start | bytes 589832 | tf_op jit(solution)/shard_map/ppermute | solution.py:28
  204.0 4.5 %collective-permute-done.21 = bf16[512,192]{0,1:T(8,128)(2,1)S(1)} collective-permute-done((bf16[512,192]{0,1:T(8,128)(2,1)S(1)}, bf16[512,192]{0,1:T(8,128)(2,1)S(1)}, u32[]{:S(2)}, u32[]{:S(2)}) %collective-permute-start.21) | collective-permute-done | bytes 196640 | tf_op jit(solution)/shard_map/ppermute | solution.py:28
  208.5 4.5 %collective-permute-done.22 = bf16[512,192]{0,1:T(8,128)(2,1)S(1)} collective-permute-done((bf16[512,192]{0,1:T(8,128)(2,1)S(1)}, bf16[512,192]{0,1:T(8,128)(2,1)S(1)}, u32[]{:S(2)}, u32[]{:S(2)}) %collective-permute-start.22) | collective-permute-done | bytes 196640 | tf_op jit(solution)/shard_map/ppermute | solution.py:28
  213.0 6.5 %collective-permute-done.23 = bf16[512,192]{0,1:T(8,128)(2,1)S(1)} collective-permute-done((bf16[512,192]{0,1:T(8,128)(2,1)S(1)}, bf16[512,192]{0,1:T(8,128)(2,1)S(1)}, u32[]{:S(2)}, u32[]{:S(2)}) %collective-permute-start.23) | collective-permute-done | bytes 196640 | tf_op jit(solution)/shard_map/ppermute | solution.py:28
  (99 shorter events, 53.0 us)
Async XLA Ops:
  6.5 88.2 %all-gather.3.cloned.1.call-start = ((), (), s32[]{:S(2)}) async-start(), calls=%async_computation | async-start | bytes 6488064 | tf_op jit(solution)/shard_map/all_gather | solution.py:113
  8.8 172.8 %all-gather.5.cloned.1.call-start = ((), (), s32[]{:S(2)}) async-start(), calls=%async_computation.1 | async-start | bytes 3538944 | tf_op jit(solution)/shard_map/all_gather | solution.py:124
  17.5 20.6 %collective-permute-start = (bf16[384,1024]{1,0:T(8,128)(2,1)}, bf16[384,1024]{1,0:T(8,128)(2,1)S(1)}, u32[]{:S(2)}, u32[]{:S(2)}) collective-permute-start(bf16[384,1024]{1,0:T(8,128)(2,1)} %get-tuple-element.14), channel_id=1, source_target_pairs={{0,32},{1,33},{2,34},{3,35},{4,36},{5,37},{6,38},{7,39},{8,40},{9,... | collective-permute-start | bytes 2359304 | tf_op jit(solution)/shard_map/ppermute | solution.py:28
  18.7 68.7 %collective-permute-start.2 = (bf16[384,1024]{1,0:T(8,128)(2,1)}, bf16[384,1024]{1,0:T(8,128)(2,1)}, u32[]{:S(2)}, u32[]{:S(2)}) collective-permute-start(bf16[384,1024]{1,0:T(8,128)(2,1)} %get-tuple-element.14), channel_id=1, source_target_pairs={{0,96},{1,97},{2,98},{3,99},{4,100},{5,101},{6,102},{7,103},{8,104... | collective-permute-start | bytes 2359304 | tf_op jit(solution)/shard_map/ppermute | solution.py:28
  19.6 65.7 %collective-permute-start.1 = (bf16[384,1024]{1,0:T(8,128)(2,1)}, bf16[384,1024]{1,0:T(8,128)(2,1)}, u32[]{:S(2)}, u32[]{:S(2)}) collective-permute-start(bf16[384,1024]{1,0:T(8,128)(2,1)} %get-tuple-element.13), channel_id=1, source_target_pairs={{0,32},{1,33},{2,34},{3,35},{4,36},{5,37},{6,38},{7,39},{8,40},{9,... | collective-permute-start | bytes 2359304 | tf_op jit(solution)/shard_map/ppermute | solution.py:28
  21.0 34.0 %collective-permute-start.3 = (bf16[384,1024]{1,0:T(8,128)(2,1)}, bf16[384,1024]{1,0:T(8,128)(2,1)}, u32[]{:S(2)}, u32[]{:S(2)}) collective-permute-start(bf16[384,1024]{1,0:T(8,128)(2,1)} %get-tuple-element.13), channel_id=1, source_target_pairs={{0,96},{1,97},{2,98},{3,99},{4,100},{5,101},{6,102},{7,103},{8,104... | collective-permute-start | bytes 2359304 | tf_op jit(solution)/shard_map/ppermute | solution.py:28
  21.6 62.7 %collective-permute-start.19 = (bf16[256,768]{1,0:T(8,128)(2,1)}, bf16[256,768]{1,0:T(8,128)(2,1)}, u32[]{:S(2)}, u32[]{:S(2)}) collective-permute-start(bf16[256,768]{1,0:T(8,128)(2,1)} %bitcast.14), channel_id=1, source_target_pairs={{0,0},{1,1},{2,2},{3,3},{4,4},{5,5},{6,6},{7,7},{8,32},{9,33},{10,... | collective-permute-start | bytes 1179656 | tf_op jit(solution)/shard_map/ppermute | solution.py:28
  38.2 53.5 %collective-permute-start.4 = (bf16[384,1024]{1,0:T(8,128)(2,1)S(1)}, bf16[384,1024]{1,0:T(8,128)(2,1)}, u32[]{:S(2)}, u32[]{:S(2)}) collective-permute-start(bf16[384,1024]{1,0:T(8,128)(2,1)S(1)} %collective-permute-done), channel_id=1, source_target_pairs={{0,32},{1,33},{2,34},{3,35},{4,36},{5,37},{6,38},{7,39},{8,40},{9,... | collective-permute-start | bytes 2359304 | tf_op jit(solution)/shard_map/ppermute | solution.py:28
  54.9 38.8 %collective-permute-start.5 = (bf16[384,1024]{1,0:T(8,128)(2,1)}, bf16[384,1024]{1,0:T(8,128)(2,1)S(1)}, u32[]{:S(2)}, u32[]{:S(2)}) collective-permute-start(bf16[384,1024]{1,0:T(8,128)(2,1)} %collective-permute-done.3), channel_id=1, source_target_pairs={{0,96},{1,97},{2,98},{3,99},{4,100},{5,101},{6,102},{7,103},{8,104... | collective-permute-start | bytes 2359304 | tf_op jit(solution)/shard_map/ppermute | solution.py:28
  99.5 15.0 %collective-permute-start.7 = (bf16[512,512]{0,1:T(8,128)(2,1)S(1)}, bf16[512,512]{0,1:T(8,128)(2,1)S(1)}, u32[]{:S(2)}, u32[]{:S(2)}) collective-permute-start(bf16[512,512]{0,1:T(8,128)(2,1)S(1)} %fusion.62), channel_id=1, source_target_pairs={{0,128},{1,129},{2,130},{3,131},{4,132},{5,133},{6,134},{7,135},{8... | collective-permute-start | bytes 1572872 | tf_op jit(solution)/shard_map/ppermute | solution.py:28
  103.0 38.5 %collective-permute-start.8 = (bf16[512,512]{0,1:T(8,128)(2,1)S(1)}, bf16[512,512]{0,1:T(8,128)(2,1)S(1)}, u32[]{:S(2)}, u32[]{:S(2)}) collective-permute-start(bf16[512,512]{0,1:T(8,128)(2,1)S(1)} %fusion.57), channel_id=1, source_target_pairs={{0,128},{1,129},{2,130},{3,131},{4,132},{5,133},{6,134},{7,135},{8... | collective-permute-start | bytes 1572872 | tf_op jit(solution)/shard_map/ppermute | solution.py:28
  116.7 26.1 %collective-permute-start.10 = (bf16[2,128,128]{2,1,0:T(8,128)(2,1)S(1)}, bf16[2,128,128]{2,1,0:T(8,128)(2,1)S(1)}, u32[]{:S(2)}, u32[]{:S(2)}) collective-permute-start(bf16[2,128,128]{2,1,0:T(8,128)(2,1)S(1)} %convolution_convert_fusion), channel_id=1, source_target_pairs={{0,64},{1,65},{2,66},{3,67},{4,68},{5,69},{6,70},{7,71},{8,72},{9,... | collective-permute-start | bytes 196616 | tf_op jit(solution)/shard_map/ppermute | solution.py:28
  134.6 9.4 %collective-permute-start.11 = (bf16[2,128,128]{2,1,0:T(8,128)(2,1)S(1)}, bf16[2,128,128]{2,1,0:T(8,128)(2,1)S(1)}, u32[]{:S(2)}, u32[]{:S(2)}) collective-permute-start(bf16[2,128,128]{2,1,0:T(8,128)(2,1)S(1)} %convolution_convert_fusion), channel_id=1, source_target_pairs={{0,96},{1,97},{2,98},{3,99},{4,100},{5,101},{6,102},{7,103},{8,104... | collective-permute-start | bytes 196616 | tf_op jit(solution)/shard_map/ppermute | solution.py:28
  137.6 22.2 %collective-permute-start.12 = (bf16[2,128,128]{2,1,0:T(8,128)(2,1)S(1)}, bf16[2,128,128]{2,1,0:T(8,128)(2,1)}, u32[]{:S(2)}, u32[]{:S(2)}) collective-permute-start(bf16[2,128,128]{2,1,0:T(8,128)(2,1)S(1)} %convolution_convert_fusion), channel_id=1, source_target_pairs={{0,128},{1,129},{2,130},{3,131},{4,132},{5,133},{6,134},{7,135},{8... | collective-permute-start | bytes 196616 | tf_op jit(solution)/shard_map/ppermute | solution.py:28
  139.6 20.3 %collective-permute-start.13 = (bf16[2,128,128]{2,1,0:T(8,128)(2,1)S(1)}, bf16[2,128,128]{2,1,0:T(8,128)(2,1)}, u32[]{:S(2)}, u32[]{:S(2)}) collective-permute-start(bf16[2,128,128]{2,1,0:T(8,128)(2,1)S(1)} %convolution_convert_fusion), channel_id=1, source_target_pairs={{0,160},{1,161},{2,162},{3,163},{4,164},{5,165},{6,166},{7,167},{8... | collective-permute-start | bytes 196616 | tf_op jit(solution)/shard_map/ppermute | solution.py:28
  141.5 18.3 %collective-permute-start.14 = (bf16[2,128,128]{2,1,0:T(8,128)(2,1)S(1)}, bf16[2,128,128]{2,1,0:T(8,128)(2,1)}, u32[]{:S(2)}, u32[]{:S(2)}) collective-permute-start(bf16[2,128,128]{2,1,0:T(8,128)(2,1)S(1)} %convolution_convert_fusion), channel_id=1, source_target_pairs={{0,192},{1,193},{2,194},{3,195},{4,196},{5,197},{6,198},{7,199},{8... | collective-permute-start | bytes 196616 | tf_op jit(solution)/shard_map/ppermute | solution.py:28
  142.8 17.1 %collective-permute-start.15 = (bf16[2,128,128]{2,1,0:T(8,128)(2,1)S(1)}, bf16[2,128,128]{2,1,0:T(8,128)(2,1)}, u32[]{:S(2)}, u32[]{:S(2)}) collective-permute-start(bf16[2,128,128]{2,1,0:T(8,128)(2,1)S(1)} %convolution_convert_fusion), channel_id=1, source_target_pairs={{0,224},{1,225},{2,226},{3,227},{4,228},{5,229},{6,230},{7,231},{8... | collective-permute-start | bytes 196616 | tf_op jit(solution)/shard_map/ppermute | solution.py:28
  144.7 17.8 %collective-permute-start.9 = (bf16[2,128,128]{2,1,0:T(8,128)(2,1)S(1)}, bf16[2,128,128]{2,1,0:T(8,128)(2,1)}, u32[]{:S(2)}, u32[]{:S(2)}) collective-permute-start(bf16[2,128,128]{2,1,0:T(8,128)(2,1)S(1)} %convolution_convert_fusion), channel_id=1, source_target_pairs={{0,32},{1,33},{2,34},{3,35},{4,36},{5,37},{6,38},{7,39},{8,40},{9,... | collective-permute-start | bytes 196616 | tf_op jit(solution)/shard_map/ppermute | solution.py:28
  169.2 8.1 %collective-permute-start.16 = (bf16[512,256]{0,1:T(8,128)(2,1)S(1)}, bf16[512,256]{0,1:T(8,128)(2,1)S(1)}, u32[]{:S(2)}, u32[]{:S(2)}) collective-permute-start(bf16[512,256]{0,1:T(8,128)(2,1)S(1)} %bitcast.125), channel_id=1, source_target_pairs={{0,16},{1,17},{2,18},{3,19},{4,20},{5,21},{6,22},{7,23},{8,24},{9,... | collective-permute-start | bytes 786440 | tf_op jit(solution)/shard_map/ppermute | solution.py:28
  169.3 10.7 %collective-permute-start.17 = (bf16[512,256]{0,1:T(8,128)(2,1)S(1)}, bf16[512,256]{0,1:T(8,128)(2,1)S(1)}, u32[]{:S(2)}, u32[]{:S(2)}) collective-permute-start(bf16[512,256]{0,1:T(8,128)(2,1)S(1)} %bitcast.126), channel_id=1, source_target_pairs={{0,8},{1,9},{2,10},{3,11},{4,12},{5,13},{6,14},{7,15},{8,16},{9,17... | collective-permute-start | bytes 786440 | tf_op jit(solution)/shard_map/ppermute | solution.py:28
  174.4 7.2 %collective-permute-start.18 = (bf16[512,256]{0,1:T(8,128)(2,1)S(1)}, bf16[512,256]{0,1:T(8,128)(2,1)S(1)}, u32[]{:S(2)}, u32[]{:S(2)}) collective-permute-start(bf16[512,256]{0,1:T(8,128)(2,1)S(1)} %bitcast.127), channel_id=1, source_target_pairs={{0,24},{1,25},{2,26},{3,27},{4,28},{5,29},{6,30},{7,31},{8,0},{9,1... | collective-permute-start | bytes 786440 | tf_op jit(solution)/shard_map/ppermute | solution.py:28
  192.4 16.1 %collective-permute-start.21 = (bf16[512,192]{0,1:T(8,128)(2,1)S(1)}, bf16[512,192]{0,1:T(8,128)(2,1)S(1)}, u32[]{:S(2)}, u32[]{:S(2)}) collective-permute-start(bf16[512,192]{0,1:T(8,128)(2,1)S(1)} %get-tuple-element.17), channel_id=1, source_target_pairs={{0,4},{1,5},{2,6},{3,7},{4,0},{5,1},{6,2},{7,3},{8,12},{9,13},{10,... | collective-permute-start | bytes 589832 | tf_op jit(solution)/shard_map/ppermute | solution.py:28
  199.9 13.2 %collective-permute-start.22 = (bf16[512,192]{0,1:T(8,128)(2,1)S(1)}, bf16[512,192]{0,1:T(8,128)(2,1)S(1)}, u32[]{:S(2)}, u32[]{:S(2)}) collective-permute-start(bf16[512,192]{0,1:T(8,128)(2,1)S(1)} %get-tuple-element.19), channel_id=1, source_target_pairs={{0,2},{1,3},{2,4},{3,5},{4,6},{5,7},{6,0},{7,1},{8,10},{9,11},{10,... | collective-permute-start | bytes 589832 | tf_op jit(solution)/shard_map/ppermute | solution.py:28
  201.4 18.2 %collective-permute-start.23 = (bf16[512,192]{0,1:T(8,128)(2,1)S(1)}, bf16[512,192]{0,1:T(8,128)(2,1)S(1)}, u32[]{:S(2)}, u32[]{:S(2)}) collective-permute-start(bf16[512,192]{0,1:T(8,128)(2,1)S(1)} %get-tuple-element.18), channel_id=1, source_target_pairs={{0,6},{1,7},{2,0},{3,1},{4,2},{5,3},{6,4},{7,5},{8,14},{9,15},{10,... | collective-permute-start | bytes 589832 | tf_op jit(solution)/shard_map/ppermute | solution.py:28
  (12 other events, 65.9 us)
Sparse Core Ops, SparseCore 0:
  9.9 81.7 all-gather.2
  93.4 63.1 all-gather.4

commit v2 on v1

--- a/solution.py
+++ b/solution.py
@@ -48,12 +48,8 @@
     return (zl, x, y, zh, 1 - c)
 
 
-def later_row(step):
-    def target(zl, x, y, zh, c):
-        row = zl * 4 + x + step
-        return (row // 4, row % 4, y, zh, c) if row < 8 else None
-
-    return target
+def later_half(zl, x, y, zh, c):
+    return (1, x, y, zh, c) if zl == 0 else None
 
 
 def tokens_to_half(zl, x, y, zh, c):
@@ -62,36 +58,28 @@
 
 
 def w_out_to_columns(zl, x, y, zh, c):
-    row = zl * 4 + x
-    return (row % 2, y, row // 2, zh, c)
-
-
-def gather_x(block):
-    place = lax.axis_index("x")
-    rows, columns = block.shape
-    half = rows // 2
-    low, high = block[:half], block[half:]
-    left_low = send(low, along_x(1))
-    right_high = send(high, along_x(-1))
-    left_high = send(high, along_x(1))
-    right_low = send(low, along_x(-1))
-    far_low = send(left_low, along_x(1))
-    far_high = send(right_high, along_x(-1))
-    whole = jnp.zeros((4 * rows, columns), block.dtype)
-    left = (place + 3) % 4 * rows
-    right = (place + 1) % 4 * rows
-    far = (place + 2) % 4 * rows
-    for piece, start in (
-        (block, place * rows),
-        (left_low, left),
-        (left_high, left + half),
-        (right_low, right),
-        (right_high, right + half),
-        (far_low, far),
-        (far_high, far + half),
-    ):
-        whole = lax.dynamic_update_slice(whole, piece, (start, 0))
-    return whole
+    there = zl * 2 + x // 2
+    apart = y ^ there
+    return (apart // 2, (apart % 2) * 2 + x % 2, there, zh, c)
+
+
+def gather_ring(block, axis, along, half):
+    left = send(block, along(1))
+    right = send(block, along(-1))
+    far_low = send(left[:half], along(1))
+    far_high = send(right[half:], along(-1))
+    place = lax.axis_index(axis)
+    return (
+        (block, 0, place),
+        (left, 0, (place + 3) % 4),
+        (right, 0, (place + 1) % 4),
+        (far_low, 0, (place + 2) % 4),
+        (far_high, half, (place + 2) % 4),
+    )
+
+
+def after(array, other):
+    return array + other[(0,) * other.ndim] * jnp.zeros((), array.dtype)
 
 
 def decay_rates(index_vec, total_rows):
@@ -109,27 +97,49 @@
     zh = lax.axis_index("zh")
     y = lax.axis_index("y")
 
-    moved = send(tokens, tokens_to_half)
-    gathered = lax.all_gather(moved, ("y", "zh", "core"), axis=1, tiled=True)
-    width = gathered.shape[1] // 2
-    mine, theirs = gathered[:, :width], gathered[:, width:]
-
-    parts = w_qkvg.reshape(-1, heads, 4, size)
-    kv_block = parts[:, :, 1:3].reshape(-1, heads * 2 * size)
-    qg_block = jnp.stack([parts[:, :, 0], parts[:, :, 3]], axis=2).reshape(-1, heads * 2 * size)
-    weight_cols = gather_x(jnp.concatenate([kv_block, qg_block], axis=1))
-    w_kv, w_qg = weight_cols[:, : heads * 2 * size], weight_cols[:, heads * 2 * size :]
-
-    w_out_moved = send(w_out.reshape(heads * size, -1), w_out_to_columns)
-    w_out_all = lax.all_gather(w_out_moved, ("zl", "x"), axis=0, tiled=True)
+    w_block = w_qkvg.reshape(w_qkvg.shape[0], -1)
+    weight_cols = lax.all_gather(w_block, "x", axis=0, tiled=True)
+
+    moved = send(tokens.T, tokens_to_half)
+    depth, across = moved.shape
+    stacked = jnp.zeros((4, depth, across), BF)
+    stacked = lax.dynamic_update_slice(stacked, moved[None], (zh, 0, 0))
+    for step in (2, 1, 3):
+        piece = send(moved, along_zh(step))
+        stacked = lax.dynamic_update_slice(stacked, piece[None], ((zh + 4 - step) % 4, 0, 0))
+    gathered = jnp.zeros((4, 4, 2, depth, across), BF)
+    for piece, start, place in gather_ring(stacked, "y", along_y, 2):
+        for part, owner in ((piece, core), (send(piece, other_core), 1 - core)):
+            gathered = lax.dynamic_update_slice(
+                gathered, part[None, :, None], (place, start, owner, 0, 0)
+            )
+    gathered = gathered.reshape(2, 16 * depth, across)
+    mine, theirs = gathered[0], gathered[1]
+
+    w_out_block = after(w_out.reshape(heads * size, -1), piece)
+    w_out_moved = send(w_out_block, w_out_to_columns)
+    w_out_pair = jnp.stack([w_out_moved, send(w_out_moved, other_zl)])
+    w_out_all = lax.all_gather(w_out_pair, "x", axis=0, tiled=True)
 
     def half_dot(a, b):
         return jnp.dot(a, b, preferred_element_type=F32)
 
-    kv_sent = send(half_dot(theirs, w_kv).astype(BF), other_zl)
-    qg_sent = send(half_dot(theirs, w_qg).astype(BF), other_zl)
-    kv = (half_dot(mine, w_kv) + kv_sent.astype(F32)).astype(BF).astype(F32)
-    qg = (half_dot(mine, w_qg) + qg_sent.astype(F32)).astype(BF).astype(F32)
+    def projection(a):
+        return lax.dot_general(
+            a, weight_cols, (((0,), (0,)), ((), ())), preferred_element_type=F32
+        )
+
+    def columns(array, parts):
+        return jnp.concatenate(
+            [array[:, (4 * h + p) * size : (4 * h + p + 1) * size] for h in range(heads) for p in parts],
+            axis=1,
+        )
+
+    own_part, other_part = projection(mine), projection(theirs).astype(BF)
+    kv_sent = send(columns(other_part, (1, 2)), other_zl)
+    qg_sent = send(columns(other_part, (0, 3)), other_zl)
+    kv = (columns(own_part, (1, 2)) + kv_sent.astype(F32)).astype(BF).astype(F32)
+    qg = (columns(own_part, (0, 3)) + qg_sent.astype(F32)).astype(BF).astype(F32)
 
     kv = jax.nn.silu(kv).reshape(rows, heads, 2, size)
     keys_act, values_act = kv[:, :, 0], kv[:, :, 1].astype(BF)
@@ -143,10 +153,18 @@
         preferred_element_type=F32,
     ).astype(BF)
     keys_act = keys_act.astype(BF)
+    place = lax.axis_index("x")
+
+    def power(count):
+        return jnp.exp(-rate_vec * (rows * 1.0) * count)[:, None, None]
+
     carried = jnp.zeros(local_state.shape, F32)
-    for step in range(1, 8):
-        earlier = send(local_state, later_row(step)).astype(F32)
-        carried += jnp.exp(-rate_vec * (rows * (step - 1.0)))[:, None, None] * earlier
+    total = power((3 - place).astype(F32)) * local_state.astype(F32)
+    for step in (2, 1, 3):
+        earlier = send(local_state, along_x(step)).astype(F32)
+        carried += jnp.where(place >= step, power(step - 1.0), 0.0) * earlier
+        total += power((3 - (place + 4 - step) % 4).astype(F32)) * earlier
+    carried += power(place.astype(F32)) * send(total.astype(BF), later_half).astype(F32)
 
     qg = qg.reshape(rows, heads, 2, size)
     queries, gate_part = jax.nn.silu(qg[:, :, 0]).astype(BF), qg[:, :, 1]
@@ -169,17 +187,21 @@
     normed = attended * lax.rsqrt(mean_square + 1e-06) * norm_gain[None]
     hidden = (normed * jax.nn.sigmoid(gate_part)).astype(BF).reshape(rows, heads * size)
 
+    def slot(origin):
+        apart = origin ^ y
+        return (apart % 2 * 2 + (apart // 2 ^ lax.axis_index("zl"))) * heads * size
+
     hidden_all = jnp.zeros((rows, 4 * heads * size), BF)
-    hidden_all = lax.dynamic_update_slice(hidden_all, hidden, (0, y * heads * size))
+    hidden_all = lax.dynamic_update_slice(hidden_all, hidden, (0, slot(y)))
     for step in (2, 1, 3):
         piece = send(hidden, along_y(step))
-        hidden_all = lax.dynamic_update_slice(hidden_all, piece, (0, (y + 4 - step) % 4 * heads * size))
-
-    depth = 4 * heads * size
-    wide = [
-        half_dot(hidden_all, w_out_all[part * depth : (part + 1) * depth]).reshape(rows, 2, 2, -1)
-        for part in range(2)
-    ]
+        hidden_all = lax.dynamic_update_slice(hidden_all, piece, (0, slot((y + 4 - step) % 4)))
+
+    span = 2 * heads * size
+    w_out_all = w_out_all.reshape(4, span, -1)
+    near, far = hidden_all[:, :span], hidden_all[:, span:]
+    wide = [half_dot(near, w_out_all[part]) + half_dot(far, w_out_all[2 + part]) for part in range(2)]
+    wide = [array.reshape(rows, 2, 2, -1) for array in wide]
     blocks = jnp.stack([wide[part][:, turn] for part in range(2) for turn in range(2)])
     kept = jnp.where(core == 0, blocks[:, :, 0], blocks[:, :, 1])
     given = jnp.where(core == 0, blocks[:, :, 1], blocks[:, :, 0]).astype(BF)

time: 231 us -> 213 us (0.922)
  starting transfers between devices: 70.9 us -> 58.1 us
  local copies, waits for them, and re-layouts: 24.5 us -> 21.4 us
  other arithmetic: 9.55 us -> 6.91 us
  waiting for transfers between devices: 89.5 us -> 92.1 us
    ppermute x24 -> x28, starting transfers between devices: 70.8 us -> 58.1 us  [send(): return lax.ppermute(array, AXES, moves(target))]
    dot_general x0 -> x2, matrix products: none -> 10.8 us  [projection(): lax.dot_general(a, weight_cols, (((0,), (0,)), ((), ())), preferred_eleme...]
    dot_general x6 -> x4, matrix products: 14 us -> 3.57 us  [half_dot(): return jnp.dot(a, b, preferred_element_type=F32)]
    dynamic_update_slice x11 -> x18, local copies, waits for them, and re-layouts: 10.7 us -> 0.72 us  [the longest x10 0.55 us: local(): lax.dynamic_update_slice(gathered, part[None, :, None], (place, start, ow...]
    slice x3 -> x11, local copies, waits for them, and re-layouts: 3.23 us -> 7 us  [the longest x1 2.93 us: local(): w_out_all[part]]
    add x0 -> x2, local copies, waits for them, and re-layouts: none -> 3.52 us  [local(): half_dot(near, w_out_all[part]) + half_dot(far, w_out_all[2 + part])]
    ppermute x24 -> x28, waiting for transfers between devices: 89.5 us -> 92.1 us  [send(): return lax.ppermute(array, AXES, moves(target))]
    another operation x2, local copies, waits for them, and re-layouts: 0.3 us -> 2.76 us  [local(): jnp.stack([wide[part][:, turn] for part in range(2) for turn in range(2)])]
  transfers between devices with their start and end apart: 26 -> 30, of which waited for: 12 -> 19; matrix products, arithmetic and copies ran while one was open for 17% -> 15% of each run, Pallas kernels for 0% -> 0%
where the time goes in v2:
time: 213 us; the launch traced here: 212 us
  waiting for transfers between devices  92.1 us (43%)
  starting transfers between devices  58.1 us (27%)
  local copies, waits for them, and re-layouts  21.4 us (10%)
  matrix products  18.4 us (9%)
  between operations  14.9 us (7%)
  other arithmetic  6.91 us (3%)
    ppermute x28, waiting for transfers between devices, send(): return lax.ppermute(array, AXES, moves(target))  92.1 us
    ppermute x28, starting transfers between devices, send(): return lax.ppermute(array, AXES, moves(target))  58.1 us
    dot_general x2, matrix products, projection(): lax.dot_general(a, weight_cols, (((0,), (0,)), ((), ())), preferred_eleme...  10.8 us
    unnamed x25, local copies, waits for them, and re-layouts  4.39 us
  transfers between devices with their start and end apart: 30, of which 19 were waited for; matrix products, arithmetic and copies ran while one was open for 15% of the time, Pallas kernels for 0%

profile of v2, /device:TPU:4, one launch (start us, length us, event | category | flops | bytes accessed | tf_op | source)
XLA Modules:
  0.0 211.8 jit_solution(7815233239016345998)
XLA Ops:
  6.5 3.0 %copy.65 = bf16[96,8,2,512]{3,1,2,0:T(8,128)(2,1)} copy(bf16[96,8,2,512]{3,2,1,0:T(2,128)(2,1)} %bitcast.145) | data formatting | bytes 3145728
  10.5 7.3 %collective-permute-start.1 = (bf16[192,512]{1,0:T(8,128)(2,1)S(1)}, bf16[192,512]{1,0:T(8,128)(2,1)S(1)}, u32[]{:S(2)}, u32[]{:S(2)}) collective-permute-start(bf16[192,512]{1,0:T(8,128)(2,1)S(1)} %collective-permute-done), channel_id=1, source_target_pairs={{0,4},{1,5},{2,6},{3,7},{4,0},{5,1},{6,2},{7,3},{8,12},{9,13},{10,... | collective-permute-start | bytes 589832 | tf_op jit(solution)/shard_map/ppermute | solution.py:28
  22.0 4.4 %collective-permute-done.1 = bf16[192,512]{1,0:T(8,128)(2,1)S(1)} collective-permute-done((bf16[192,512]{1,0:T(8,128)(2,1)S(1)}, bf16[192,512]{1,0:T(8,128)(2,1)S(1)}, u32[]{:S(2)}, u32[]{:S(2)}) %collective-permute-start.1) | collective-permute-done | bytes 196640 | tf_op jit(solution)/shard_map/ppermute | solution.py:28
  26.5 4.0 %collective-permute-done.2 = bf16[192,512]{1,0:T(8,128)(2,1)S(1)} collective-permute-done((bf16[192,512]{1,0:T(8,128)(2,1)S(1)}, bf16[192,512]{1,0:T(8,128)(2,1)S(1)}, u32[]{:S(2)}, u32[]{:S(2)}) %collective-permute-start.2) | collective-permute-done | bytes 196640 | tf_op jit(solution)/shard_map/ppermute | solution.py:28
  30.6 16.5 %collective-permute-start.7 = (bf16[4,192,512]{2,1,0:T(8,128)(2,1)S(1)}, bf16[4,192,512]{2,1,0:T(8,128)(2,1)S(1)}, u32[]{:S(2)}, u32[]{:S(2)}) collective-permute-start(bf16[4,192,512]{2,1,0:T(8,128)(2,1)S(1)} %bitcast_dynamic-update-slice_fusion.10), channel_id=1, source_target_pairs={{0,24},{1,25},{2,26},{3,27},{4,28},{5,29},{6,30},{7,31},{8,0},{9,1... | collective-permute-start | bytes 2359304 | tf_op jit(solution)/shard_map/ppermute | solution.py:28
  47.9 14.8 %collective-permute-done.7 = bf16[4,192,512]{2,1,0:T(8,128)(2,1)S(1)} collective-permute-done((bf16[4,192,512]{2,1,0:T(8,128)(2,1)S(1)}, bf16[4,192,512]{2,1,0:T(8,128)(2,1)S(1)}, u32[]{:S(2)}, u32[]{:S(2)}) %collective-permute-start.7) | collective-permute-done | bytes 786464 | tf_op jit(solution)/shard_map/ppermute | solution.py:28
  62.7 3.8 %collective-permute-start.11 = (bf16[2,192,512]{2,1,0:T(8,128)(2,1)S(1)}, bf16[2,192,512]{2,1,0:T(8,128)(2,1)S(1)}, u32[]{:S(2)}, u32[]{:S(2)}) collective-permute-start(bf16[2,192,512]{2,1,0:T(8,128)(2,1)S(1)} %slice.146), channel_id=1, source_target_pairs={{0,24},{1,25},{2,26},{3,27},{4,28},{5,29},{6,30},{7,31},{8,0},{9,1... | collective-permute-start | bytes 1179656 | tf_op jit(solution)/shard_map/ppermute | solution.py:28
  69.2 3.5 %collective-permute-done.11 = bf16[2,192,512]{2,1,0:T(8,128)(2,1)S(1)} collective-permute-done((bf16[2,192,512]{2,1,0:T(8,128)(2,1)S(1)}, bf16[2,192,512]{2,1,0:T(8,128)(2,1)S(1)}, u32[]{:S(2)}, u32[]{:S(2)}) %collective-permute-start.11) | collective-permute-done | bytes 393248 | tf_op jit(solution)/shard_map/ppermute | solution.py:28
  76.1 5.2 %collective-permute-done.9 = bf16[2,192,512]{2,1,0:T(8,128)(2,1)S(1)} collective-permute-done((bf16[2,192,512]{2,1,0:T(8,128)(2,1)S(1)}, bf16[2,192,512]{2,1,0:T(8,128)(2,1)S(1)}, u32[]{:S(2)}, u32[]{:S(2)}) %collective-permute-start.9) | collective-permute-done | bytes 393248 | tf_op jit(solution)/shard_map/ppermute | solution.py:28
  81.3 6.4 %collective-permute-done.22 = bf16[256,768]{1,0:T(8,128)(2,1)S(1)} collective-permute-done((bf16[256,768]{1,0:T(8,128)(2,1)S(1)}, bf16[256,768]{1,0:T(8,128)(2,1)S(1)}, u32[]{:S(2)}, u32[]{:S(2)}) %collective-permute-start.22) | collective-permute-done | bytes 393248 | tf_op jit(solution)/shard_map/ppermute | solution.py:28
  92.5 7.0 %collective-permute-done.23 = bf16[256,768]{1,0:T(8,128)(2,1)S(1)} collective-permute-done((bf16[256,768]{1,0:T(8,128)(2,1)S(1)}, bf16[256,768]{1,0:T(8,128)(2,1)S(1)}, u32[]{:S(2)}, u32[]{:S(2)}) %collective-permute-start.23) | collective-permute-done | bytes 393248 | tf_op jit(solution)/shard_map/ppermute | solution.py:28
  100.5 7.3 %convolution_convert_fusion = bf16[512,1024]{1,0:T(8,128)(2,1)S(1)} fusion(bf16[3072,512]{1,0:T(8,128)(2,1)} %bitcast.142, bf16[3072,1024]{1,0:T(8,128)(2,1)} %all-gather.3.cloned.1.call-done), kind=kOutput, calls=%fused_computation.6 | convolution fusion | flops 3221749760 | bytes 10485760 | tf_op jit(solution)/shard_map/dot_general | solution.py:128
  110.2 3.5 %fusion.59 = f32[512,1024]{1,0:T(8,128)S(1)} fusion(bf16[3072,512]{1,0:T(8,128)(2,1)S(1)} %bitcast.141, bf16[3072,1024]{1,0:T(8,128)(2,1)S(1)} %copy-done.9), kind=kOutput, calls=%fused_computation.124 | convolution fusion | flops 3221225472 | bytes 11534336 | tf_op jit(solution)/shard_map/dot_general | solution.py:128
  113.9 9.0 %collective-permute-done.14 = bf16[512,512]{1,0:T(8,128)(2,1)S(1)} collective-permute-done((bf16[512,512]{1,0:T(8,128)(2,1)S(1)}, bf16[512,512]{1,0:T(8,128)(2,1)S(1)}, u32[]{:S(2)}, u32[]{:S(2)}) %collective-permute-start.14) | collective-permute-done | bytes 524320 | tf_op jit(solution)/shard_map/ppermute | solution.py:28
  122.9 10.2 %collective-permute-done.13 = bf16[512,512]{1,0:T(8,128)(2,1)S(1)} collective-permute-done((bf16[512,512]{1,0:T(8,128)(2,1)S(1)}, bf16[512,512]{1,0:T(8,128)(2,1)S(1)}, u32[]{:S(2)}, u32[]{:S(2)}) %collective-permute-start.13) | collective-permute-done | bytes 524320 | tf_op jit(solution)/shard_map/ppermute | solution.py:28
  144.6 4.1 %collective-permute-start.18 = (bf16[2,128,128]{2,1,0:T(8,128)(2,1)}, bf16[2,128,128]{2,1,0:T(8,128)(2,1)}, u32[]{:S(2)}, u32[]{:S(2)}) collective-permute-start(bf16[2,128,128]{2,1,0:T(8,128)(2,1)} %fusion.40), channel_id=1, source_target_pairs={{0,128},{1,129},{2,130},{3,131},{4,132},{5,133},{6,134},{7,135},{8... | collective-permute-start | bytes 196616 | tf_op jit(solution)/shard_map/ppermute | solution.py:28
  156.9 2.9 %fusion.51 = (bf16[2,256,768]{2,1,0:T(8,128)(2,1)S(1)}, bf16[2,256,768]{2,1,0:T(8,128)(2,1)S(1)}, bf16[2,256,768]{2,1,0:T(8,128)(2,1)}, bf16[2,256,768]{2,1,0:T(8,128)(2,1)S(1)}) fusion(bf16[8,256,768]{2,1,0:T(8,128)(2,1)} %all-gather.5.cloned.1.call-done), kind=kLoop, calls=%fused_computation.118 | loop fusion | bytes 6291456 | tf_op jit(solution)/shard_map/slice | solution.py:203
  160.6 4.3 %collective-permute-done.19 = bf16[512,256]{0,1:T(8,128)(2,1)S(1)} collective-permute-done((bf16[512,256]{0,1:T(8,128)(2,1)S(1)}, bf16[512,256]{0,1:T(8,128)(2,1)S(1)}, u32[]{:S(2)}, u32[]{:S(2)}) %collective-permute-start.19) | collective-permute-done | bytes 262176 | tf_op jit(solution)/shard_map/ppermute | solution.py:28
  164.9 3.5 %collective-permute-done.20 = bf16[512,256]{0,1:T(8,128)(2,1)S(1)} collective-permute-done((bf16[512,256]{0,1:T(8,128)(2,1)S(1)}, bf16[512,256]{0,1:T(8,128)(2,1)S(1)}, u32[]{:S(2)}, u32[]{:S(2)}) %collective-permute-start.20) | collective-permute-done | bytes 262176 | tf_op jit(solution)/shard_map/ppermute | solution.py:28
  181.8 4.2 %collective-permute-start.25 = (bf16[512,192]{0,1:T(8,128)(2,1)S(1)}, bf16[512,192]{0,1:T(8,128)(2,1)S(1)}, u32[]{:S(2)}, u32[]{:S(2)}) collective-permute-start(bf16[512,192]{0,1:T(8,128)(2,1)S(1)} %get-tuple-element.31), channel_id=1, source_target_pairs={{0,4},{1,5},{2,6},{3,7},{4,0},{5,1},{6,2},{7,3},{8,12},{9,13},{10,... | collective-permute-start | bytes 589832 | tf_op jit(solution)/shard_map/ppermute | solution.py:28
  185.9 4.1 %collective-permute-start.27 = (bf16[512,192]{0,1:T(8,128)(2,1)S(1)}, bf16[512,192]{0,1:T(8,128)(2,1)S(1)}, u32[]{:S(2)}, u32[]{:S(2)}) collective-permute-start(bf16[512,192]{0,1:T(8,128)(2,1)S(1)} %get-tuple-element.32), channel_id=1, source_target_pairs={{0,6},{1,7},{2,0},{3,1},{4,2},{5,3},{6,4},{7,5},{8,14},{9,15},{10,... | collective-permute-start | bytes 589832 | tf_op jit(solution)/shard_map/ppermute | solution.py:28
  190.1 7.1 %collective-permute-done.25 = bf16[512,192]{0,1:T(8,128)(2,1)S(1)} collective-permute-done((bf16[512,192]{0,1:T(8,128)(2,1)S(1)}, bf16[512,192]{0,1:T(8,128)(2,1)S(1)}, u32[]{:S(2)}, u32[]{:S(2)}) %collective-permute-start.25) | collective-permute-done | bytes 196640 | tf_op jit(solution)/shard_map/ppermute | solution.py:28
  197.2 3.2 %collective-permute-done.26 = bf16[512,192]{0,1:T(8,128)(2,1)S(1)} collective-permute-done((bf16[512,192]{0,1:T(8,128)(2,1)S(1)}, bf16[512,192]{0,1:T(8,128)(2,1)S(1)}, u32[]{:S(2)}, u32[]{:S(2)}) %collective-permute-start.26) | collective-permute-done | bytes 196640 | tf_op jit(solution)/shard_map/ppermute | solution.py:28
  200.3 3.8 %collective-permute-done.27 = bf16[512,192]{0,1:T(8,128)(2,1)S(1)} collective-permute-done((bf16[512,192]{0,1:T(8,128)(2,1)S(1)}, bf16[512,192]{0,1:T(8,128)(2,1)S(1)}, u32[]{:S(2)}, u32[]{:S(2)}) %collective-permute-start.27) | collective-permute-done | bytes 196640 | tf_op jit(solution)/shard_map/ppermute | solution.py:28
  (130 shorter events, 54.0 us)
Async XLA Ops:
  6.5 93.9 %all-gather.3.cloned.1.call-start = ((), (), s32[]{:S(2)}) async-start(), calls=%async_computation | async-start | bytes 7864320 | tf_op jit(solution)/shard_map/all_gather | solution.py:101
  9.6 147.3 %all-gather.5.cloned.1.call-start = ((), (), s32[]{:S(2)}) async-start(), calls=%async_computation.1 | async-start | bytes 3932160 | tf_op jit(solution)/shard_map/all_gather | solution.py:122
  10.5 15.9 %collective-permute-start.1 = (bf16[192,512]{1,0:T(8,128)(2,1)S(1)}, bf16[192,512]{1,0:T(8,128)(2,1)S(1)}, u32[]{:S(2)}, u32[]{:S(2)}) collective-permute-start(bf16[192,512]{1,0:T(8,128)(2,1)S(1)} %collective-permute-done), channel_id=1, source_target_pairs={{0,4},{1,5},{2,6},{3,7},{4,0},{5,1},{6,2},{7,3},{8,12},{9,13},{10,... | collective-permute-start | bytes 589832 | tf_op jit(solution)/shard_map/ppermute | solution.py:28
  17.8 12.7 %collective-permute-start.2 = (bf16[192,512]{1,0:T(8,128)(2,1)S(1)}, bf16[192,512]{1,0:T(8,128)(2,1)S(1)}, u32[]{:S(2)}, u32[]{:S(2)}) collective-permute-start(bf16[192,512]{1,0:T(8,128)(2,1)S(1)} %collective-permute-done), channel_id=1, source_target_pairs={{0,2},{1,3},{2,4},{3,5},{4,6},{5,7},{6,0},{7,1},{8,10},{9,11},{10,... | collective-permute-start | bytes 589832 | tf_op jit(solution)/shard_map/ppermute | solution.py:28
  19.3 11.2 %collective-permute-start.3 = (bf16[192,512]{1,0:T(8,128)(2,1)S(1)}, bf16[192,512]{1,0:T(8,128)(2,1)S(1)}, u32[]{:S(2)}, u32[]{:S(2)}) collective-permute-start(bf16[192,512]{1,0:T(8,128)(2,1)S(1)} %collective-permute-done), channel_id=1, source_target_pairs={{0,6},{1,7},{2,0},{3,1},{4,2},{5,3},{6,4},{7,5},{8,14},{9,15},{10,... | collective-permute-start | bytes 589832 | tf_op jit(solution)/shard_map/ppermute | solution.py:28
  30.6 32.1 %collective-permute-start.7 = (bf16[4,192,512]{2,1,0:T(8,128)(2,1)S(1)}, bf16[4,192,512]{2,1,0:T(8,128)(2,1)S(1)}, u32[]{:S(2)}, u32[]{:S(2)}) collective-permute-start(bf16[4,192,512]{2,1,0:T(8,128)(2,1)S(1)} %bitcast_dynamic-update-slice_fusion.10), channel_id=1, source_target_pairs={{0,24},{1,25},{2,26},{3,27},{4,28},{5,29},{6,30},{7,31},{8,0},{9,1... | collective-permute-start | bytes 2359304 | tf_op jit(solution)/shard_map/ppermute | solution.py:28
  47.0 20.6 %collective-permute-start.5 = (bf16[4,192,512]{2,1,0:T(8,128)(2,1)S(1)}, bf16[4,192,512]{2,1,0:T(8,128)(2,1)S(1)}, u32[]{:S(2)}, u32[]{:S(2)}) collective-permute-start(bf16[4,192,512]{2,1,0:T(8,128)(2,1)S(1)} %bitcast_dynamic-update-slice_fusion.10), channel_id=1, source_target_pairs={{0,8},{1,9},{2,10},{3,11},{4,12},{5,13},{6,14},{7,15},{8,16},{9,17... | collective-permute-start | bytes 2359304 | tf_op jit(solution)/shard_map/ppermute | solution.py:28
  47.2 28.7 %collective-permute-start.4 = (bf16[4,192,512]{2,1,0:T(8,128)(2,1)S(1)}, bf16[4,192,512]{2,1,0:T(8,128)(2,1)S(1)}, u32[]{:S(2)}, u32[]{:S(2)}) collective-permute-start(bf16[4,192,512]{2,1,0:T(8,128)(2,1)S(1)} %bitcast_dynamic-update-slice_fusion.10), channel_id=1, source_target_pairs={{0,1},{1,0},{2,3},{3,2},{4,5},{5,4},{6,7},{7,6},{8,9},{9,8},{10,11... | collective-permute-start | bytes 2359304 | tf_op jit(solution)/shard_map/ppermute | solution.py:28
  62.7 10.0 %collective-permute-start.11 = (bf16[2,192,512]{2,1,0:T(8,128)(2,1)S(1)}, bf16[2,192,512]{2,1,0:T(8,128)(2,1)S(1)}, u32[]{:S(2)}, u32[]{:S(2)}) collective-permute-start(bf16[2,192,512]{2,1,0:T(8,128)(2,1)S(1)} %slice.146), channel_id=1, source_target_pairs={{0,24},{1,25},{2,26},{3,27},{4,28},{5,29},{6,30},{7,31},{8,0},{9,1... | collective-permute-start | bytes 1179656 | tf_op jit(solution)/shard_map/ppermute | solution.py:28
  67.6 22.0 %collective-permute-start.6 = (bf16[4,192,512]{2,1,0:T(8,128)(2,1)S(1)}, bf16[4,192,512]{2,1,0:T(8,128)(2,1)S(1)}, u32[]{:S(2)}, u32[]{:S(2)}) collective-permute-start(bf16[4,192,512]{2,1,0:T(8,128)(2,1)S(1)} %collective-permute-done.5), channel_id=1, source_target_pairs={{0,1},{1,0},{2,3},{3,2},{4,5},{5,4},{6,7},{7,6},{8,9},{9,8},{10,11... | collective-permute-start | bytes 2359304 | tf_op jit(solution)/shard_map/ppermute | solution.py:28
  68.5 12.8 %collective-permute-start.9 = (bf16[2,192,512]{2,1,0:T(8,128)(2,1)S(1)}, bf16[2,192,512]{2,1,0:T(8,128)(2,1)S(1)}, u32[]{:S(2)}, u32[]{:S(2)}) collective-permute-start(bf16[2,192,512]{2,1,0:T(8,128)(2,1)S(1)} %slice.145), channel_id=1, source_target_pairs={{0,8},{1,9},{2,10},{3,11},{4,12},{5,13},{6,14},{7,15},{8,16},{9,17... | collective-permute-start | bytes 1179656 | tf_op jit(solution)/shard_map/ppermute | solution.py:28
  68.6 21.3 %collective-permute-start.8 = (bf16[4,192,512]{2,1,0:T(8,128)(2,1)S(1)}, bf16[4,192,512]{2,1,0:T(8,128)(2,1)S(1)}, u32[]{:S(2)}, u32[]{:S(2)}) collective-permute-start(bf16[4,192,512]{2,1,0:T(8,128)(2,1)S(1)} %collective-permute-done.7), channel_id=1, source_target_pairs={{0,1},{1,0},{2,3},{3,2},{4,5},{5,4},{6,7},{7,6},{8,9},{9,8},{10,11... | collective-permute-start | bytes 2359304 | tf_op jit(solution)/shard_map/ppermute | solution.py:28
  73.9 13.8 %collective-permute-start.22 = (bf16[256,768]{1,0:T(8,128)(2,1)S(1)}, bf16[256,768]{1,0:T(8,128)(2,1)S(1)}, u32[]{:S(2)}, u32[]{:S(2)}) collective-permute-start(bf16[256,768]{1,0:T(8,128)(2,1)S(1)} %bitcast.152), channel_id=1, source_target_pairs={{0,0},{1,1},{2,2},{3,3},{4,4},{5,5},{6,6},{7,7},{8,64},{9,65},{10,... | collective-permute-start | bytes 1179656 | tf_op jit(solution)/shard_map/ppermute | solution.py:28
  76.0 14.1 %collective-permute-start.12 = (bf16[2,192,512]{2,1,0:T(8,128)(2,1)S(1)}, bf16[2,192,512]{2,1,0:T(8,128)(2,1)S(1)}, u32[]{:S(2)}, u32[]{:S(2)}) collective-permute-start(bf16[2,192,512]{2,1,0:T(8,128)(2,1)S(1)} %collective-permute-done.11), channel_id=1, source_target_pairs={{0,1},{1,0},{2,3},{3,2},{4,5},{5,4},{6,7},{7,6},{8,9},{9,8},{10,11... | collective-permute-start | bytes 1179656 | tf_op jit(solution)/shard_map/ppermute | solution.py:28
  81.3 8.7 %collective-permute-start.10 = (bf16[2,192,512]{2,1,0:T(8,128)(2,1)S(1)}, bf16[2,192,512]{2,1,0:T(8,128)(2,1)S(1)}, u32[]{:S(2)}, u32[]{:S(2)}) collective-permute-start(bf16[2,192,512]{2,1,0:T(8,128)(2,1)S(1)} %collective-permute-done.9), channel_id=1, source_target_pairs={{0,1},{1,0},{2,3},{3,2},{4,5},{5,4},{6,7},{7,6},{8,9},{9,8},{10,11... | collective-permute-start | bytes 1179656 | tf_op jit(solution)/shard_map/ppermute | solution.py:28
  87.7 11.8 %collective-permute-start.23 = (bf16[256,768]{1,0:T(8,128)(2,1)S(1)}, bf16[256,768]{1,0:T(8,128)(2,1)S(1)}, u32[]{:S(2)}, u32[]{:S(2)}) collective-permute-start(bf16[256,768]{1,0:T(8,128)(2,1)S(1)} %collective-permute-done.22), channel_id=1, source_target_pairs={{0,128},{1,129},{2,130},{3,131},{4,132},{5,133},{6,134},{7,135},{8... | collective-permute-start | bytes 1179656 | tf_op jit(solution)/shard_map/ppermute | solution.py:28
  108.0 14.9 %collective-permute-start.14 = (bf16[512,512]{1,0:T(8,128)(2,1)S(1)}, bf16[512,512]{1,0:T(8,128)(2,1)S(1)}, u32[]{:S(2)}, u32[]{:S(2)}) collective-permute-start(bf16[512,512]{1,0:T(8,128)(2,1)S(1)} %pad_maximum_fusion.3), channel_id=1, source_target_pairs={{0,128},{1,129},{2,130},{3,131},{4,132},{5,133},{6,134},{7,135},{8... | collective-permute-start | bytes 1572872 | tf_op jit(solution)/shard_map/ppermute | solution.py:28
  109.8 23.2 %collective-permute-start.13 = (bf16[512,512]{1,0:T(8,128)(2,1)S(1)}, bf16[512,512]{1,0:T(8,128)(2,1)S(1)}, u32[]{:S(2)}, u32[]{:S(2)}) collective-permute-start(bf16[512,512]{1,0:T(8,128)(2,1)S(1)} %pad_maximum_fusion.2), channel_id=1, source_target_pairs={{0,128},{1,129},{2,130},{3,131},{4,132},{5,133},{6,134},{7,135},{8... | collective-permute-start | bytes 1572872 | tf_op jit(solution)/shard_map/ppermute | solution.py:28
  154.1 10.8 %collective-permute-start.19 = (bf16[512,256]{0,1:T(8,128)(2,1)S(1)}, bf16[512,256]{0,1:T(8,128)(2,1)S(1)}, u32[]{:S(2)}, u32[]{:S(2)}) collective-permute-start(bf16[512,256]{0,1:T(8,128)(2,1)S(1)} %bitcast.146), channel_id=1, source_target_pairs={{0,16},{1,17},{2,18},{3,19},{4,20},{5,21},{6,22},{7,23},{8,24},{9,... | collective-permute-start | bytes 786440 | tf_op jit(solution)/shard_map/ppermute | solution.py:28
  154.4 14.0 %collective-permute-start.20 = (bf16[512,256]{0,1:T(8,128)(2,1)S(1)}, bf16[512,256]{0,1:T(8,128)(2,1)S(1)}, u32[]{:S(2)}, u32[]{:S(2)}) collective-permute-start(bf16[512,256]{0,1:T(8,128)(2,1)S(1)} %bitcast.147), channel_id=1, source_target_pairs={{0,8},{1,9},{2,10},{3,11},{4,12},{5,13},{6,14},{7,15},{8,16},{9,17... | collective-permute-start | bytes 786440 | tf_op jit(solution)/shard_map/ppermute | solution.py:28
  159.8 8.6 %collective-permute-start.21 = (bf16[512,256]{0,1:T(8,128)(2,1)S(1)}, bf16[512,256]{0,1:T(8,128)(2,1)S(1)}, u32[]{:S(2)}, u32[]{:S(2)}) collective-permute-start(bf16[512,256]{0,1:T(8,128)(2,1)S(1)} %bitcast.148), channel_id=1, source_target_pairs={{0,24},{1,25},{2,26},{3,27},{4,28},{5,29},{6,30},{7,31},{8,0},{9,1... | collective-permute-start | bytes 786440 | tf_op jit(solution)/shard_map/ppermute | solution.py:28
  181.8 15.4 %collective-permute-start.25 = (bf16[512,192]{0,1:T(8,128)(2,1)S(1)}, bf16[512,192]{0,1:T(8,128)(2,1)S(1)}, u32[]{:S(2)}, u32[]{:S(2)}) collective-permute-start(bf16[512,192]{0,1:T(8,128)(2,1)S(1)} %get-tuple-element.31), channel_id=1, source_target_pairs={{0,4},{1,5},{2,6},{3,7},{4,0},{5,1},{6,2},{7,3},{8,12},{9,13},{10,... | collective-permute-start | bytes 589832 | tf_op jit(solution)/shard_map/ppermute | solution.py:28
  185.9 14.4 %collective-permute-start.26 = (bf16[512,192]{0,1:T(8,128)(2,1)S(1)}, bf16[512,192]{0,1:T(8,128)(2,1)S(1)}, u32[]{:S(2)}, u32[]{:S(2)}) collective-permute-start(bf16[512,192]{0,1:T(8,128)(2,1)S(1)} %get-tuple-element.33), channel_id=1, source_target_pairs={{0,2},{1,3},{2,4},{3,5},{4,6},{5,7},{6,0},{7,1},{8,10},{9,11},{10,... | collective-permute-start | bytes 589832 | tf_op jit(solution)/shard_map/ppermute | solution.py:28
  185.9 18.2 %collective-permute-start.27 = (bf16[512,192]{0,1:T(8,128)(2,1)S(1)}, bf16[512,192]{0,1:T(8,128)(2,1)S(1)}, u32[]{:S(2)}, u32[]{:S(2)}) collective-permute-start(bf16[512,192]{0,1:T(8,128)(2,1)S(1)} %get-tuple-element.32), channel_id=1, source_target_pairs={{0,6},{1,7},{2,0},{3,1},{4,2},{5,3},{6,4},{7,5},{8,14},{9,15},{10,... | collective-permute-start | bytes 589832 | tf_op jit(solution)/shard_map/ppermute | solution.py:28
  (17 other events, 109.2 us)
Sparse Core Ops, SparseCore 0:
  9.7 70.5 all-gather.2
  100.6 42.9 all-gather.4

commit v3 on v2

--- a/solution.py
+++ b/solution.py
@@ -57,16 +57,21 @@
     return (half, x, (zl ^ half) * 2 + y % 2, zh, c)
 
 
-def w_out_to_columns(zl, x, y, zh, c):
-    there = zl * 2 + x // 2
-    apart = y ^ there
-    return (apart // 2, (apart % 2) * 2 + x % 2, there, zh, c)
-
-
-def gather_ring(block, axis, along, half):
+def w_out_to_columns(high):
+    def target(zl, x, y, zh, c):
+        return (zl, (y % 2) * 2 + x % 2, zl * 2 + x // 2, zh, c) if y // 2 == high else None
+
+    return target
+
+
+def w_out_to_other_zl(zl, x, y, zh, c):
+    return (1 - zl, x, y, zh, c) if y // 2 == zl else None
+
+
+def gather_ring(block, axis, along, half, other):
     left = send(block, along(1))
     right = send(block, along(-1))
-    far_low = send(left[:half], along(1))
+    far_low = send(after(left[:half], other), along(1))
     far_high = send(right[half:], along(-1))
     place = lax.axis_index(axis)
     return (
@@ -97,8 +102,19 @@
     zh = lax.axis_index("zh")
     y = lax.axis_index("y")
 
-    w_block = w_qkvg.reshape(w_qkvg.shape[0], -1)
+    w_block = w_qkvg.reshape(2, 2, tokens.shape[1], -1)
+    kv_cuts = [(4 * h + 1, 4 * h + 3) for h in range(heads)]
+    qg_cuts = [(0, 1)] + [(4 * h + 3, 4 * h + 5) for h in range(heads - 1)] + [(4 * heads - 1, 4 * heads)]
+    w_block = jnp.concatenate(
+        [w_block[..., low * size : high * size] for low, high in kv_cuts + qg_cuts], axis=-1
+    )
+    w_block = jnp.stack(
+        [jnp.where(core == own, w_block[:, 0], w_block[:, 1]) for own in range(2)], axis=1
+    ).reshape(w_qkvg.shape[0], -1)
     weight_cols = lax.all_gather(w_block, "x", axis=0, tiled=True)
+
+    w_out_block = w_out.reshape(heads * size, -1)
+    w_out_moved = jnp.stack([send(w_out_block, w_out_to_columns(high)) for high in range(2)])
 
     moved = send(tokens.T, tokens_to_half)
     depth, across = moved.shape
@@ -108,38 +124,28 @@
         piece = send(moved, along_zh(step))
         stacked = lax.dynamic_update_slice(stacked, piece[None], ((zh + 4 - step) % 4, 0, 0))
     gathered = jnp.zeros((4, 4, 2, depth, across), BF)
-    for piece, start, place in gather_ring(stacked, "y", along_y, 2):
-        for part, owner in ((piece, core), (send(piece, other_core), 1 - core)):
-            gathered = lax.dynamic_update_slice(
-                gathered, part[None, :, None], (place, start, owner, 0, 0)
-            )
+    swapped = []
+    for piece, start, place in gather_ring(stacked, "y", along_y, 2, w_out_moved):
+        swapped.append(send(piece, other_core))
+        both = jnp.stack([piece, swapped[-1]], axis=1)
+        gathered = lax.dynamic_update_slice(gathered, both[None], (place, start, 0, 0, 0))
     gathered = gathered.reshape(2, 16 * depth, across)
     mine, theirs = gathered[0], gathered[1]
 
-    w_out_block = after(w_out.reshape(heads * size, -1), piece)
-    w_out_moved = send(w_out_block, w_out_to_columns)
-    w_out_pair = jnp.stack([w_out_moved, send(w_out_moved, other_zl)])
+    w_out_pair = w_out_moved + send(w_out_moved, w_out_to_other_zl)
     w_out_all = lax.all_gather(w_out_pair, "x", axis=0, tiled=True)
-
-    def half_dot(a, b):
-        return jnp.dot(a, b, preferred_element_type=F32)
-
-    def projection(a):
-        return lax.dot_general(
-            a, weight_cols, (((0,), (0,)), ((), ())), preferred_element_type=F32
-        )
-
-    def columns(array, parts):
-        return jnp.concatenate(
-            [array[:, (4 * h + p) * size : (4 * h + p + 1) * size] for h in range(heads) for p in parts],
-            axis=1,
-        )
-
-    own_part, other_part = projection(mine), projection(theirs).astype(BF)
-    kv_sent = send(columns(other_part, (1, 2)), other_zl)
-    qg_sent = send(columns(other_part, (0, 3)), other_zl)
-    kv = (columns(own_part, (1, 2)) + kv_sent.astype(F32)).astype(BF).astype(F32)
-    qg = (columns(own_part, (0, 3)) + qg_sent.astype(F32)).astype(BF).astype(F32)
+    weight_cols = after(weight_cols, swapped[0])
+
+    def projection(a, b):
+        return lax.dot_general(a, b, (((0,), (0,)), ((), ())), preferred_element_type=F32)
+
+    w_kv, w_qg = jnp.split(weight_cols, 2, axis=1)
+    kv_theirs = projection(theirs, w_kv).astype(BF)
+    kv_sent = send(kv_theirs, other_zl)
+    qg_sent = send(projection(theirs, w_qg).astype(BF), other_zl)
+    kv_own, qg_own = jnp.split(projection(mine, weight_cols), 2, axis=1)
+    kv = (kv_own + kv_sent.astype(F32)).astype(BF).astype(F32)
+    qg = (qg_own + qg_sent.astype(F32)).astype(BF).astype(F32)
 
     kv = jax.nn.silu(kv).reshape(rows, heads, 2, size)
     keys_act, values_act = kv[:, :, 0], kv[:, :, 1].astype(BF)
@@ -166,7 +172,7 @@
         total += power((3 - (place + 4 - step) % 4).astype(F32)) * earlier
     carried += power(place.astype(F32)) * send(total.astype(BF), later_half).astype(F32)
 
-    qg = qg.reshape(rows, heads, 2, size)
+    qg = after(qg, local_state).reshape(rows, heads, 2, size)
     queries, gate_part = jax.nn.silu(qg[:, :, 0]).astype(BF), qg[:, :, 1]
     distance = local_pos[:, None] - local_pos[None, :]
     weight = jnp.where(
@@ -188,8 +194,7 @@
     hidden = (normed * jax.nn.sigmoid(gate_part)).astype(BF).reshape(rows, heads * size)
 
     def slot(origin):
-        apart = origin ^ y
-        return (apart % 2 * 2 + (apart // 2 ^ lax.axis_index("zl"))) * heads * size
+        return (origin % 2 * 2 + origin // 2) * heads * size
 
     hidden_all = jnp.zeros((rows, 4 * heads * size), BF)
     hidden_all = lax.dynamic_update_slice(hidden_all, hidden, (0, slot(y)))
@@ -200,18 +205,24 @@
     span = 2 * heads * size
     w_out_all = w_out_all.reshape(4, span, -1)
     near, far = hidden_all[:, :span], hidden_all[:, span:]
-    wide = [half_dot(near, w_out_all[part]) + half_dot(far, w_out_all[2 + part]) for part in range(2)]
-    wide = [array.reshape(rows, 2, 2, -1) for array in wide]
-    blocks = jnp.stack([wide[part][:, turn] for part in range(2) for turn in range(2)])
-    kept = jnp.where(core == 0, blocks[:, :, 0], blocks[:, :, 1])
-    given = jnp.where(core == 0, blocks[:, :, 1], blocks[:, :, 0]).astype(BF)
+
+    def columns_first(weights, rows_first):
+        return lax.dot_general(
+            weights, rows_first, (((0,), (1,)), ((), ())), preferred_element_type=F32
+        )
+
+    blocks = jnp.stack(
+        [columns_first(w_out_all[p], near) + columns_first(w_out_all[2 + p], far) for p in range(2)]
+    ).reshape(4, 2, -1, rows)
+    kept = jnp.where(core == 0, blocks[:, 0], blocks[:, 1])
+    given = jnp.where(core == 0, blocks[:, 1], blocks[:, 0]).astype(BF)
     summed = kept + send(given, other_core).astype(F32)
     total = lax.dynamic_index_in_dim(summed, zh, 0, False)
     outgoing = summed.astype(BF)
     for step in (2, 1, 3):
         piece = lax.dynamic_index_in_dim(outgoing, (zh + step) % 4, 0, False)
         total += send(piece, along_zh(step)).astype(F32)
-    return total.astype(BF)
+    return total.astype(BF).T
 
 
 def solution(mesh):

time: 213 us -> 195 us (0.915)
  waiting for transfers between devices: 92.1 us -> 62.1 us
  other arithmetic: 6.91 us -> 18.5 us
  starting transfers between devices: 58.1 us -> 67.3 us
  local copies, waits for them, and re-layouts: 21.4 us -> 14.8 us
  matrix products: 18.4 us -> 14.4 us
    ppermute x28 -> x29, waiting for transfers between devices: 92.1 us -> 62 us  [send(): return lax.ppermute(array, AXES, moves(target))]
    ppermute x28 -> x29, starting transfers between devices: 58.1 us -> 67.2 us  [send(): return lax.ppermute(array, AXES, moves(target))]
    add x1 -> x3, other arithmetic: 0.03 us -> 5.35 us  [after(): return array + other[(0,) * other.ndim] * jnp.zeros((), array.dtype)]
    dynamic_update_slice x0 -> x5, other arithmetic: none -> 5.02 us  [local(): lax.dynamic_update_slice(gathered, both[None], (place, start, 0, 0, 0))]
    dot_general x6 -> x7, matrix products: 14.4 us -> 10.2 us  [the longest x3 7.85 us: projection(): lax.dot_general(a, b, (((0,), (0,)), ((), ())), preferred_element_type=F32)]
    add x2 -> x0, local copies, waits for them, and re-layouts: 3.52 us -> none  [local(): half_dot(near, w_out_all[part]) + half_dot(far, w_out_all[2 + part])]
    reshape x1 -> x2, local copies, waits for them, and re-layouts: 0.67 us -> 3.5 us  [the longest x1 2.82 us: local(): w_block = w_qkvg.reshape(2, 2, tokens.shape[1], -1)]
    another operation x2 -> x0, local copies, waits for them, and re-layouts: 2.76 us -> none  [local(): jnp.stack([wide[part][:, turn] for part in range(2) for turn in range(2)])]
  transfers between devices with their start and end apart: 30 -> 31, of which waited for: 19 -> 14; matrix products, arithmetic and copies ran while one was open for 15% -> 20% of each run, Pallas kernels for 0% -> 0%
where the time goes in v3:
time: 195 us; the launch traced here: 193 us
  starting transfers between devices  67.3 us (35%)
  waiting for transfers between devices  62.1 us (32%)
  other arithmetic  18.5 us (9%)
  between operations  16.3 us (8%)
  local copies, waits for them, and re-layouts  14.8 us (8%)
  matrix products  14.4 us (7%)
    ppermute x29, starting transfers between devices, send(): return lax.ppermute(array, AXES, moves(target))  67.2 us
    ppermute x29, waiting for transfers between devices, send(): return lax.ppermute(array, AXES, moves(target))  62 us
    dot_general x3, matrix products, projection(): lax.dot_general(a, b, (((0,), (0,)), ((), ())), preferred_element_type=F32)  7.85 us
    add x3, other arithmetic, after(): return array + other[(0,) * other.ndim] * jnp.zeros((), array.dtype)  5.35 us
    dynamic_update_slice x5, other arithmetic, local(): lax.dynamic_update_slice(gathered, both[None], (place, start, 0, 0, 0))  5.02 us
  transfers between devices with their start and end apart: 31, of which 14 were waited for; matrix products, arithmetic and copies ran while one was open for 20% of the time, Pallas kernels for 0%

profile of v3, /device:TPU:4, one launch (start us, length us, event | category | flops | bytes accessed | tf_op | source)
XLA Modules:
  0.0 193.3 jit_solution(5162004596871690722)
XLA Ops:
  6.5 2.8 %reshape.163 = bf16[2,2,192,1024]{3,2,1,0:T(8,128)(2,1)S(1)} reshape(bf16[768,2,512]{2,1,0:T(2,128)(2,1)} %param.6) | data formatting | bytes 3145728 | tf_op jit(solution)/shard_map/reshape | solution.py:105
  11.2 3.4 %collective-permute-start = (bf16[256,768]{1,0:T(8,128)(2,1)S(1)}, bf16[256,768]{1,0:T(8,128)(2,1)S(1)}, u32[]{:S(2)}, u32[]{:S(2)}) collective-permute-start(bf16[256,768]{1,0:T(8,128)(2,1)S(1)} %bitcast.168), channel_id=1, source_target_pairs={{0,0},{1,1},{2,2},{3,3},{4,4},{5,5},{6,6},{7,7},{8,64},{9,65},{10,... | collective-permute-start | bytes 1179656 | tf_op jit(solution)/shard_map/ppermute | solution.py:28
  17.9 7.2 %collective-permute-start.4 = (bf16[192,512]{1,0:T(8,128)(2,1)S(1)}, bf16[192,512]{1,0:T(8,128)(2,1)S(1)}, u32[]{:S(2)}, u32[]{:S(2)}) collective-permute-start(bf16[192,512]{1,0:T(8,128)(2,1)S(1)} %collective-permute-done.3), channel_id=1, source_target_pairs={{0,4},{1,5},{2,6},{3,7},{4,0},{5,1},{6,2},{7,3},{8,12},{9,13},{10,... | collective-permute-start | bytes 589832 | tf_op jit(solution)/shard_map/ppermute | solution.py:28
  26.6 2.7 %collective-permute-start.6 = (bf16[192,512]{1,0:T(8,128)(2,1)S(1)}, bf16[192,512]{1,0:T(8,128)(2,1)S(1)}, u32[]{:S(2)}, u32[]{:S(2)}) collective-permute-start(bf16[192,512]{1,0:T(8,128)(2,1)S(1)} %collective-permute-done.3), channel_id=1, source_target_pairs={{0,6},{1,7},{2,0},{3,1},{4,2},{5,3},{6,4},{7,5},{8,14},{9,15},{10,... | collective-permute-start | bytes 589832 | tf_op jit(solution)/shard_map/ppermute | solution.py:28
  29.3 4.6 %collective-permute-done.4 = bf16[192,512]{1,0:T(8,128)(2,1)S(1)} collective-permute-done((bf16[192,512]{1,0:T(8,128)(2,1)S(1)}, bf16[192,512]{1,0:T(8,128)(2,1)S(1)}, u32[]{:S(2)}, u32[]{:S(2)}) %collective-permute-start.4) | collective-permute-done | bytes 196640 | tf_op jit(solution)/shard_map/ppermute | solution.py:28
  33.9 3.6 %collective-permute-done.5 = bf16[192,512]{1,0:T(8,128)(2,1)S(1)} collective-permute-done((bf16[192,512]{1,0:T(8,128)(2,1)S(1)}, bf16[192,512]{1,0:T(8,128)(2,1)S(1)}, u32[]{:S(2)}, u32[]{:S(2)}) %collective-permute-start.5) | collective-permute-done | bytes 196640 | tf_op jit(solution)/shard_map/ppermute | solution.py:28
  37.7 21.2 %collective-permute-start.10 = (bf16[4,192,512]{2,1,0:T(8,128)(2,1)S(1)}, bf16[4,192,512]{2,1,0:T(8,128)(2,1)S(1)}, u32[]{:S(2)}, u32[]{:S(2)}) collective-permute-start(bf16[4,192,512]{2,1,0:T(8,128)(2,1)S(1)} %bitcast_dynamic-update-slice_fusion), channel_id=1, source_target_pairs={{0,24},{1,25},{2,26},{3,27},{4,28},{5,29},{6,30},{7,31},{8,0},{9,1... | collective-permute-start | bytes 2359304 | tf_op jit(solution)/shard_map/ppermute | solution.py:28
  63.6 12.9 %collective-permute-done.8 = bf16[4,192,512]{2,1,0:T(8,128)(2,1)S(1)} collective-permute-done((bf16[4,192,512]{2,1,0:T(8,128)(2,1)S(1)}, bf16[4,192,512]{2,1,0:T(8,128)(2,1)S(1)}, u32[]{:S(2)}, u32[]{:S(2)}) %collective-permute-start.8) | collective-permute-done | bytes 786464 | tf_op jit(solution)/shard_map/ppermute | solution.py:28
  79.6 2.7 %collective-permute-start.14 = (bf16[2,192,512]{2,1,0:T(8,128)(2,1)S(1)}, bf16[2,192,512]{2,1,0:T(8,128)(2,1)}, u32[]{:S(2)}, u32[]{:S(2)}) collective-permute-start(bf16[2,192,512]{2,1,0:T(8,128)(2,1)S(1)} %slice.118), channel_id=1, source_target_pairs={{0,24},{1,25},{2,26},{3,27},{4,28},{5,29},{6,30},{7,31},{8,0},{9,1... | collective-permute-start | bytes 1179656 | tf_op jit(solution)/shard_map/ppermute | solution.py:28
  84.5 5.9 %collective-permute-done.12 = bf16[2,192,512]{2,1,0:T(8,128)(2,1)} collective-permute-done((bf16[2,192,512]{2,1,0:T(8,128)(2,1)}, bf16[2,192,512]{2,1,0:T(8,128)(2,1)}, u32[]{:S(2)}, u32[]{:S(2)}) %collective-permute-start.12) | collective-permute-done | bytes 393248 | tf_op jit(solution)/shard_map/ppermute | solution.py:28
  99.8 3.3 %broadcast_add_fusion = bf16[3072,1024]{1,0:T(8,128)(2,1)S(1)} fusion(bf16[3072,1024]{1,0:T(8,128)(2,1)} %all-gather.5.cloned.1.call-done, bf16[]{:T(256)} %bitcast.28), kind=kLoop, calls=%fused_computation.5 | loop fusion | flops 3145728 | bytes 12582914 | tf_op jit(solution)/shard_map/add | solution.py:87
  105.6 2.6 %fusion.10 = bf16[512,512]{1,0:T(8,128)(2,1)} fusion(bf16[3072,512]{1,0:T(8,128)(2,1)S(1)} %bitcast.150, bf16[3072,1024]{1,0:T(8,128)(2,1)S(1)} %broadcast_add_fusion), kind=kOutput, calls=%fused_computation.24 | convolution fusion | flops 1610874880 | bytes 6815744 | tf_op jit(solution)/shard_map/dot_general | solution.py:140
  110.0 3.4 %fusion.69 = f32[512,1024]{1,0:T(8,128)S(1)} fusion(bf16[3072,512]{1,0:T(8,128)(2,1)S(1)} %bitcast.148, bf16[3072,1024]{1,0:T(8,128)(2,1)S(1)} %broadcast_add_fusion), kind=kOutput, calls=%fused_computation.130 | convolution fusion | flops 3221225472 | bytes 11534336 | tf_op jit(solution)/shard_map/dot_general | solution.py:140
  113.5 6.7 %collective-permute-done.16 = bf16[512,512]{1,0:T(8,128)(2,1)S(1)} collective-permute-done((bf16[512,512]{1,0:T(8,128)(2,1)S(1)}, bf16[512,512]{1,0:T(8,128)(2,1)S(1)}, u32[]{:S(2)}, u32[]{:S(2)}) %collective-permute-start.16) | collective-permute-done | bytes 524320 | tf_op jit(solution)/shard_map/ppermute | solution.py:28
  126.8 3.8 %collective-permute-done.17 = bf16[512,512]{1,0:T(8,128)(2,1)} collective-permute-done((bf16[512,512]{1,0:T(8,128)(2,1)}, bf16[512,512]{1,0:T(8,128)(2,1)}, u32[]{:S(2)}, u32[]{:S(2)}) %collective-permute-start.17) | collective-permute-done | bytes 524320 | tf_op jit(solution)/shard_map/ppermute | solution.py:28
  140.7 2.5 %collective-permute-start.22 = (bf16[512,256]{0,1:T(8,128)(2,1)S(1)}, bf16[512,256]{0,1:T(8,128)(2,1)S(1)}, u32[]{:S(2)}, u32[]{:S(2)}) collective-permute-start(bf16[512,256]{0,1:T(8,128)(2,1)S(1)} %bitcast.161), channel_id=1, source_target_pairs={{0,16},{1,17},{2,18},{3,19},{4,20},{5,21},{6,22},{7,23},{8,24},{9,... | collective-permute-start | bytes 786440 | tf_op jit(solution)/shard_map/ppermute | solution.py:28
  146.1 2.5 %collective-permute-start.24 = (bf16[512,256]{0,1:T(8,128)(2,1)S(1)}, bf16[512,256]{0,1:T(8,128)(2,1)S(1)}, u32[]{:S(2)}, u32[]{:S(2)}) collective-permute-start(bf16[512,256]{0,1:T(8,128)(2,1)S(1)} %bitcast.163), channel_id=1, source_target_pairs={{0,24},{1,25},{2,26},{3,27},{4,28},{5,29},{6,30},{7,31},{8,0},{9,1... | collective-permute-start | bytes 786440 | tf_op jit(solution)/shard_map/ppermute | solution.py:28
  148.7 2.8 %collective-permute-done.22 = bf16[512,256]{0,1:T(8,128)(2,1)S(1)} collective-permute-done((bf16[512,256]{0,1:T(8,128)(2,1)S(1)}, bf16[512,256]{0,1:T(8,128)(2,1)S(1)}, u32[]{:S(2)}, u32[]{:S(2)}) %collective-permute-start.22) | collective-permute-done | bytes 262176 | tf_op jit(solution)/shard_map/ppermute | solution.py:28
  151.6 3.2 %collective-permute-done.23 = bf16[512,256]{0,1:T(8,128)(2,1)S(1)} collective-permute-done((bf16[512,256]{0,1:T(8,128)(2,1)S(1)}, bf16[512,256]{0,1:T(8,128)(2,1)S(1)}, u32[]{:S(2)}, u32[]{:S(2)}) %collective-permute-start.23) | collective-permute-done | bytes 262176 | tf_op jit(solution)/shard_map/ppermute | solution.py:28
  160.8 5.0 %collective-permute-start.26 = (bf16[192,512]{1,0:T(8,128)(2,1)S(1)}, bf16[192,512]{1,0:T(8,128)(2,1)S(1)}, u32[]{:S(2)}, u32[]{:S(2)}) collective-permute-start(bf16[192,512]{1,0:T(8,128)(2,1)S(1)} %get-tuple-element.19), channel_id=1, source_target_pairs={{0,4},{1,5},{2,6},{3,7},{4,0},{5,1},{6,2},{7,3},{8,12},{9,13},{10,... | collective-permute-start | bytes 589832 | tf_op jit(solution)/shard_map/ppermute | solution.py:28
  167.1 2.8 %collective-permute-start.28 = (bf16[192,512]{1,0:T(8,128)(2,1)S(1)}, bf16[192,512]{1,0:T(8,128)(2,1)S(1)}, u32[]{:S(2)}, u32[]{:S(2)}) collective-permute-start(bf16[192,512]{1,0:T(8,128)(2,1)S(1)} %get-tuple-element.20), channel_id=1, source_target_pairs={{0,6},{1,7},{2,0},{3,1},{4,2},{5,3},{6,4},{7,5},{8,14},{9,15},{10,... | collective-permute-start | bytes 589832 | tf_op jit(solution)/shard_map/ppermute | solution.py:28
  169.9 3.9 %collective-permute-done.26 = bf16[192,512]{1,0:T(8,128)(2,1)S(1)} collective-permute-done((bf16[192,512]{1,0:T(8,128)(2,1)S(1)}, bf16[192,512]{1,0:T(8,128)(2,1)S(1)}, u32[]{:S(2)}, u32[]{:S(2)}) %collective-permute-start.26) | collective-permute-done | bytes 196640 | tf_op jit(solution)/shard_map/ppermute | solution.py:28
  173.8 6.5 %collective-permute-done.27 = bf16[192,512]{1,0:T(8,128)(2,1)S(1)} collective-permute-done((bf16[192,512]{1,0:T(8,128)(2,1)S(1)}, bf16[192,512]{1,0:T(8,128)(2,1)S(1)}, u32[]{:S(2)}, u32[]{:S(2)}) %collective-permute-start.27) | collective-permute-done | bytes 196640 | tf_op jit(solution)/shard_map/ppermute | solution.py:28
  180.3 5.4 %collective-permute-done.28 = bf16[192,512]{1,0:T(8,128)(2,1)S(1)} collective-permute-done((bf16[192,512]{1,0:T(8,128)(2,1)S(1)}, bf16[192,512]{1,0:T(8,128)(2,1)S(1)}, u32[]{:S(2)}, u32[]{:S(2)}) %collective-permute-start.28) | collective-permute-done | bytes 196640 | tf_op jit(solution)/shard_map/ppermute | solution.py:28
  (140 shorter events, 55.6 us)
Async XLA Ops:
  6.5 93.2 %all-gather.5.cloned.1.call-start = ((), (), s32[]{:S(2)}) async-start(), calls=%async_computation.1 | async-start | bytes 7864320 | tf_op jit(solution)/shard_map/all_gather | solution.py:114
  11.2 132.9 %all-gather.3.cloned.1.call-start = ((), (), s32[]{:S(2)}) async-start(), calls=%async_computation | async-start | bytes 3932160 | tf_op jit(solution)/shard_map/all_gather | solution.py:136
  11.2 48.2 %collective-permute-start = (bf16[256,768]{1,0:T(8,128)(2,1)S(1)}, bf16[256,768]{1,0:T(8,128)(2,1)S(1)}, u32[]{:S(2)}, u32[]{:S(2)}) collective-permute-start(bf16[256,768]{1,0:T(8,128)(2,1)S(1)} %bitcast.168), channel_id=1, source_target_pairs={{0,0},{1,1},{2,2},{3,3},{4,4},{5,5},{6,6},{7,7},{8,64},{9,65},{10,... | collective-permute-start | bytes 1179656 | tf_op jit(solution)/shard_map/ppermute | solution.py:28
  14.7 44.8 %collective-permute-start.1 = (bf16[256,768]{1,0:T(8,128)(2,1)S(1)}, bf16[256,768]{1,0:T(8,128)(2,1)S(1)}, u32[]{:S(2)}, u32[]{:S(2)}) collective-permute-start(bf16[256,768]{1,0:T(8,128)(2,1)S(1)} %bitcast.169), channel_id=1, source_target_pairs={{16,0},{17,1},{18,2},{19,3},{20,4},{21,5},{22,6},{23,7},{24,64},{2... | collective-permute-start | bytes 1179656 | tf_op jit(solution)/shard_map/ppermute | solution.py:28
  17.9 16.0 %collective-permute-start.4 = (bf16[192,512]{1,0:T(8,128)(2,1)S(1)}, bf16[192,512]{1,0:T(8,128)(2,1)S(1)}, u32[]{:S(2)}, u32[]{:S(2)}) collective-permute-start(bf16[192,512]{1,0:T(8,128)(2,1)S(1)} %collective-permute-done.3), channel_id=1, source_target_pairs={{0,4},{1,5},{2,6},{3,7},{4,0},{5,1},{6,2},{7,3},{8,12},{9,13},{10,... | collective-permute-start | bytes 589832 | tf_op jit(solution)/shard_map/ppermute | solution.py:28
  25.1 12.4 %collective-permute-start.5 = (bf16[192,512]{1,0:T(8,128)(2,1)S(1)}, bf16[192,512]{1,0:T(8,128)(2,1)S(1)}, u32[]{:S(2)}, u32[]{:S(2)}) collective-permute-start(bf16[192,512]{1,0:T(8,128)(2,1)S(1)} %collective-permute-done.3), channel_id=1, source_target_pairs={{0,2},{1,3},{2,4},{3,5},{4,6},{5,7},{6,0},{7,1},{8,10},{9,11},{10,... | collective-permute-start | bytes 589832 | tf_op jit(solution)/shard_map/ppermute | solution.py:28
  26.6 11.0 %collective-permute-start.6 = (bf16[192,512]{1,0:T(8,128)(2,1)S(1)}, bf16[192,512]{1,0:T(8,128)(2,1)S(1)}, u32[]{:S(2)}, u32[]{:S(2)}) collective-permute-start(bf16[192,512]{1,0:T(8,128)(2,1)S(1)} %collective-permute-done.3), channel_id=1, source_target_pairs={{0,6},{1,7},{2,0},{3,1},{4,2},{5,3},{6,4},{7,5},{8,14},{9,15},{10,... | collective-permute-start | bytes 589832 | tf_op jit(solution)/shard_map/ppermute | solution.py:28
  37.6 38.9 %collective-permute-start.8 = (bf16[4,192,512]{2,1,0:T(8,128)(2,1)S(1)}, bf16[4,192,512]{2,1,0:T(8,128)(2,1)S(1)}, u32[]{:S(2)}, u32[]{:S(2)}) collective-permute-start(bf16[4,192,512]{2,1,0:T(8,128)(2,1)S(1)} %bitcast_dynamic-update-slice_fusion), channel_id=1, source_target_pairs={{0,8},{1,9},{2,10},{3,11},{4,12},{5,13},{6,14},{7,15},{8,16},{9,17... | collective-permute-start | bytes 2359304 | tf_op jit(solution)/shard_map/ppermute | solution.py:28
  37.7 38.8 %collective-permute-start.10 = (bf16[4,192,512]{2,1,0:T(8,128)(2,1)S(1)}, bf16[4,192,512]{2,1,0:T(8,128)(2,1)S(1)}, u32[]{:S(2)}, u32[]{:S(2)}) collective-permute-start(bf16[4,192,512]{2,1,0:T(8,128)(2,1)S(1)} %bitcast_dynamic-update-slice_fusion), channel_id=1, source_target_pairs={{0,24},{1,25},{2,26},{3,27},{4,28},{5,29},{6,30},{7,31},{8,0},{9,1... | collective-permute-start | bytes 2359304 | tf_op jit(solution)/shard_map/ppermute | solution.py:28
  59.4 20.2 %collective-permute-start.7 = (bf16[4,192,512]{2,1,0:T(8,128)(2,1)S(1)}, bf16[4,192,512]{2,1,0:T(8,128)(2,1)S(1)}, u32[]{:S(2)}, u32[]{:S(2)}) collective-permute-start(bf16[4,192,512]{2,1,0:T(8,128)(2,1)S(1)} %bitcast_dynamic-update-slice_fusion), channel_id=1, source_target_pairs={{0,1},{1,0},{2,3},{3,2},{4,5},{5,4},{6,7},{7,6},{8,9},{9,8},{10,11... | collective-permute-start | bytes 2359304 | tf_op jit(solution)/shard_map/ppermute | solution.py:28
  59.5 24.0 %collective-permute-start.2 = (bf16[2,256,768]{2,1,0:T(8,128)(2,1)S(1)}, bf16[2,256,768]{2,1,0:T(8,128)(2,1)S(1)}, u32[]{:S(2)}, u32[]{:S(2)}) collective-permute-start(bf16[2,256,768]{2,1,0:T(8,128)(2,1)S(1)} %pad_maximum_fusion.2), channel_id=1, source_target_pairs={{0,128},{1,129},{2,130},{3,131},{4,132},{5,133},{6,134},{7,135},{8... | collective-permute-start | bytes 2359304 | tf_op jit(solution)/shard_map/ppermute | solution.py:28
  76.5 16.1 %collective-permute-start.9 = (bf16[4,192,512]{2,1,0:T(8,128)(2,1)S(1)}, bf16[4,192,512]{2,1,0:T(8,128)(2,1)}, u32[]{:S(2)}, u32[]{:S(2)}) collective-permute-start(bf16[4,192,512]{2,1,0:T(8,128)(2,1)S(1)} %collective-permute-done.8), channel_id=1, source_target_pairs={{0,1},{1,0},{2,3},{3,2},{4,5},{5,4},{6,7},{7,6},{8,9},{9,8},{10,11... | collective-permute-start | bytes 2359304 | tf_op jit(solution)/shard_map/ppermute | solution.py:28
  76.5 17.4 %collective-permute-start.11 = (bf16[4,192,512]{2,1,0:T(8,128)(2,1)S(1)}, bf16[4,192,512]{2,1,0:T(8,128)(2,1)}, u32[]{:S(2)}, u32[]{:S(2)}) collective-permute-start(bf16[4,192,512]{2,1,0:T(8,128)(2,1)S(1)} %collective-permute-done.10), channel_id=1, source_target_pairs={{0,1},{1,0},{2,3},{3,2},{4,5},{5,4},{6,7},{7,6},{8,9},{9,8},{10,11... | collective-permute-start | bytes 2359304 | tf_op jit(solution)/shard_map/ppermute | solution.py:28
  77.8 12.6 %collective-permute-start.12 = (bf16[2,192,512]{2,1,0:T(8,128)(2,1)}, bf16[2,192,512]{2,1,0:T(8,128)(2,1)}, u32[]{:S(2)}, u32[]{:S(2)}) collective-permute-start(bf16[2,192,512]{2,1,0:T(8,128)(2,1)} %slice_add_fusion.2), channel_id=1, source_target_pairs={{0,8},{1,9},{2,10},{3,11},{4,12},{5,13},{6,14},{7,15},{8,16},{9,17... | collective-permute-start | bytes 1179656 | tf_op jit(solution)/shard_map/ppermute | solution.py:28
  79.6 12.1 %collective-permute-start.14 = (bf16[2,192,512]{2,1,0:T(8,128)(2,1)S(1)}, bf16[2,192,512]{2,1,0:T(8,128)(2,1)}, u32[]{:S(2)}, u32[]{:S(2)}) collective-permute-start(bf16[2,192,512]{2,1,0:T(8,128)(2,1)S(1)} %slice.118), channel_id=1, source_target_pairs={{0,24},{1,25},{2,26},{3,27},{4,28},{5,29},{6,30},{7,31},{8,0},{9,1... | collective-permute-start | bytes 1179656 | tf_op jit(solution)/shard_map/ppermute | solution.py:28
  105.3 14.9 %collective-permute-start.16 = (bf16[512,512]{1,0:T(8,128)(2,1)S(1)}, bf16[512,512]{1,0:T(8,128)(2,1)S(1)}, u32[]{:S(2)}, u32[]{:S(2)}) collective-permute-start(bf16[512,512]{1,0:T(8,128)(2,1)S(1)} %fusion.7), channel_id=1, source_target_pairs={{0,128},{1,129},{2,130},{3,131},{4,132},{5,133},{6,134},{7,135},{8... | collective-permute-start | bytes 1572872 | tf_op jit(solution)/shard_map/ppermute | solution.py:28
  108.2 22.4 %collective-permute-start.17 = (bf16[512,512]{1,0:T(8,128)(2,1)}, bf16[512,512]{1,0:T(8,128)(2,1)}, u32[]{:S(2)}, u32[]{:S(2)}) collective-permute-start(bf16[512,512]{1,0:T(8,128)(2,1)} %fusion.10), channel_id=1, source_target_pairs={{0,128},{1,129},{2,130},{3,131},{4,132},{5,133},{6,134},{7,135},{8... | collective-permute-start | bytes 1572872 | tf_op jit(solution)/shard_map/ppermute | solution.py:28
  122.6 10.0 %collective-permute-start.18 = (bf16[2,128,128]{2,1,0:T(8,128)(2,1)S(1)}, bf16[2,128,128]{2,1,0:T(8,128)(2,1)S(1)}, u32[]{:S(2)}, u32[]{:S(2)}) collective-permute-start(bf16[2,128,128]{2,1,0:T(8,128)(2,1)S(1)} %convolution_convert_fusion), channel_id=1, source_target_pairs={{0,64},{1,65},{2,66},{3,67},{4,68},{5,69},{6,70},{7,71},{8,72},{9,... | collective-permute-start | bytes 196616 | tf_op jit(solution)/shard_map/ppermute | solution.py:28
  123.6 9.0 %collective-permute-start.19 = (bf16[2,128,128]{2,1,0:T(8,128)(2,1)S(1)}, bf16[2,128,128]{2,1,0:T(8,128)(2,1)S(1)}, u32[]{:S(2)}, u32[]{:S(2)}) collective-permute-start(bf16[2,128,128]{2,1,0:T(8,128)(2,1)S(1)} %convolution_convert_fusion), channel_id=1, source_target_pairs={{0,32},{1,33},{2,34},{3,35},{4,36},{5,37},{6,38},{7,39},{8,40},{9,... | collective-permute-start | bytes 196616 | tf_op jit(solution)/shard_map/ppermute | solution.py:28
  140.7 10.8 %collective-permute-start.22 = (bf16[512,256]{0,1:T(8,128)(2,1)S(1)}, bf16[512,256]{0,1:T(8,128)(2,1)S(1)}, u32[]{:S(2)}, u32[]{:S(2)}) collective-permute-start(bf16[512,256]{0,1:T(8,128)(2,1)S(1)} %bitcast.161), channel_id=1, source_target_pairs={{0,16},{1,17},{2,18},{3,19},{4,20},{5,21},{6,22},{7,23},{8,24},{9,... | collective-permute-start | bytes 786440 | tf_op jit(solution)/shard_map/ppermute | solution.py:28
  143.2 11.5 %collective-permute-start.23 = (bf16[512,256]{0,1:T(8,128)(2,1)S(1)}, bf16[512,256]{0,1:T(8,128)(2,1)S(1)}, u32[]{:S(2)}, u32[]{:S(2)}) collective-permute-start(bf16[512,256]{0,1:T(8,128)(2,1)S(1)} %bitcast.162), channel_id=1, source_target_pairs={{0,8},{1,9},{2,10},{3,11},{4,12},{5,13},{6,14},{7,15},{8,16},{9,17... | collective-permute-start | bytes 786440 | tf_op jit(solution)/shard_map/ppermute | solution.py:28
  160.8 13.1 %collective-permute-start.26 = (bf16[192,512]{1,0:T(8,128)(2,1)S(1)}, bf16[192,512]{1,0:T(8,128)(2,1)S(1)}, u32[]{:S(2)}, u32[]{:S(2)}) collective-permute-start(bf16[192,512]{1,0:T(8,128)(2,1)S(1)} %get-tuple-element.19), channel_id=1, source_target_pairs={{0,4},{1,5},{2,6},{3,7},{4,0},{5,1},{6,2},{7,3},{8,12},{9,13},{10,... | collective-permute-start | bytes 589832 | tf_op jit(solution)/shard_map/ppermute | solution.py:28
  165.8 14.5 %collective-permute-start.27 = (bf16[192,512]{1,0:T(8,128)(2,1)S(1)}, bf16[192,512]{1,0:T(8,128)(2,1)S(1)}, u32[]{:S(2)}, u32[]{:S(2)}) collective-permute-start(bf16[192,512]{1,0:T(8,128)(2,1)S(1)} %get-tuple-element.21), channel_id=1, source_target_pairs={{0,2},{1,3},{2,4},{3,5},{4,6},{5,7},{6,0},{7,1},{8,10},{9,11},{10,... | collective-permute-start | bytes 589832 | tf_op jit(solution)/shard_map/ppermute | solution.py:28
  167.1 18.6 %collective-permute-start.28 = (bf16[192,512]{1,0:T(8,128)(2,1)S(1)}, bf16[192,512]{1,0:T(8,128)(2,1)S(1)}, u32[]{:S(2)}, u32[]{:S(2)}) collective-permute-start(bf16[192,512]{1,0:T(8,128)(2,1)S(1)} %get-tuple-element.20), channel_id=1, source_target_pairs={{0,6},{1,7},{2,0},{3,1},{4,2},{5,3},{6,4},{7,5},{8,14},{9,15},{10,... | collective-permute-start | bytes 589832 | tf_op jit(solution)/shard_map/ppermute | solution.py:28
  (24 other events, 140.9 us)
Sparse Core Ops, SparseCore 0:
  11.3 70.5 all-gather.4
  84.6 42.0 all-gather.2

commit v4 on v3

--- a/solution.py
+++ b/solution.py
@@ -102,6 +102,10 @@
     zh = lax.axis_index("zh")
     y = lax.axis_index("y")
 
+    w_out_block = w_out.reshape(heads * size, -1)
+    w_out_moved = jnp.stack([send(w_out_block, w_out_to_columns(high)) for high in range(2)])
+
+    moved = send(tokens.T, tokens_to_half)
     w_block = w_qkvg.reshape(2, 2, tokens.shape[1], -1)
     kv_cuts = [(4 * h + 1, 4 * h + 3) for h in range(heads)]
     qg_cuts = [(0, 1)] + [(4 * h + 3, 4 * h + 5) for h in range(heads - 1)] + [(4 * heads - 1, 4 * heads)]
@@ -111,12 +115,8 @@
     w_block = jnp.stack(
         [jnp.where(core == own, w_block[:, 0], w_block[:, 1]) for own in range(2)], axis=1
     ).reshape(w_qkvg.shape[0], -1)
-    weight_cols = lax.all_gather(w_block, "x", axis=0, tiled=True)
-
-    w_out_block = w_out.reshape(heads * size, -1)
-    w_out_moved = jnp.stack([send(w_out_block, w_out_to_columns(high)) for high in range(2)])
-
-    moved = send(tokens.T, tokens_to_half)
+    weight_cols = lax.all_gather(after(w_block, moved), "x", axis=0, tiled=True)
+
     depth, across = moved.shape
     stacked = jnp.zeros((4, depth, across), BF)
     stacked = lax.dynamic_update_slice(stacked, moved[None], (zh, 0, 0))

time: 195 us -> 191 us (0.979)
  the two profiles are of different devices: /device:TPU:4 before, /device:TPU:1 now
where the time goes in v4:
time: 191 us; the launch traced here: 190 us
  waiting for transfers between devices  64.6 us (34%)
  starting transfers between devices  59.2 us (31%)
  other arithmetic  19.1 us (10%)
  between operations  16.9 us (9%)
  local copies, waits for them, and re-layouts  15.3 us (8%)
  matrix products  15.2 us (8%)
    ppermute x29, waiting for transfers between devices, send(): return lax.ppermute(array, AXES, moves(target))  64.6 us
    ppermute x29, starting transfers between devices, send(): return lax.ppermute(array, AXES, moves(target))  59.2 us
    dot_general x3, matrix products, projection(): lax.dot_general(a, b, (((0,), (0,)), ((), ())), preferred_element_type=F32)  7.84 us
    add x4, other arithmetic, after(): return array + other[(0,) * other.ndim] * jnp.zeros((), array.dtype)  6.63 us
    dynamic_update_slice x5, other arithmetic, local(): lax.dynamic_update_slice(gathered, both[None], (place, start, 0, 0, 0))  4.98 us
  transfers between devices with their start and end apart: 31, of which 12 were waited for; matrix products, arithmetic and copies ran while one was open for 22% of the time, Pallas kernels for 0%

profile of v4, /device:TPU:1, one launch (start us, length us, event | category | flops | bytes accessed | tf_op | source)
XLA Modules:
  0.0 190.4 jit_solution(18323943223889188790)
XLA Ops:
  8.1 2.8 %reshape.165 = bf16[2,2,192,1024]{3,2,1,0:T(8,128)(2,1)S(1)} reshape(bf16[768,2,512]{2,1,0:T(2,128)(2,1)} %param.6) | data formatting | bytes 3145728 | tf_op jit(solution)/shard_map/reshape | solution.py:109
  18.1 7.7 %collective-permute-start.4 = (bf16[192,512]{1,0:T(8,128)(2,1)S(1)}, bf16[192,512]{1,0:T(8,128)(2,1)S(1)}, u32[]{:S(2)}, u32[]{:S(2)}) collective-permute-start(bf16[192,512]{1,0:T(8,128)(2,1)S(1)} %collective-permute-done.3), channel_id=1, source_target_pairs={{0,4},{1,5},{2,6},{3,7},{4,0},{5,1},{6,2},{7,3},{8,12},{9,13},{10,... | collective-permute-start | bytes 589832 | tf_op jit(solution)/shard_map/ppermute | solution.py:28
  27.1 2.4 %collective-permute-start.6 = (bf16[192,512]{1,0:T(8,128)(2,1)S(1)}, bf16[192,512]{1,0:T(8,128)(2,1)S(1)}, u32[]{:S(2)}, u32[]{:S(2)}) collective-permute-start(bf16[192,512]{1,0:T(8,128)(2,1)S(1)} %collective-permute-done.3), channel_id=1, source_target_pairs={{0,6},{1,7},{2,0},{3,1},{4,2},{5,3},{6,4},{7,5},{8,14},{9,15},{10,... | collective-permute-start | bytes 589832 | tf_op jit(solution)/shard_map/ppermute | solution.py:28
  30.0 8.5 %collective-permute-done.5 = bf16[192,512]{1,0:T(8,128)(2,1)S(1)} collective-permute-done((bf16[192,512]{1,0:T(8,128)(2,1)S(1)}, bf16[192,512]{1,0:T(8,128)(2,1)S(1)}, u32[]{:S(2)}, u32[]{:S(2)}) %collective-permute-start.5) | collective-permute-done | bytes 196640 | tf_op jit(solution)/shard_map/ppermute | solution.py:28
  38.6 11.9 %collective-permute-start.8 = (bf16[4,192,512]{2,1,0:T(8,128)(2,1)S(1)}, bf16[4,192,512]{2,1,0:T(8,128)(2,1)S(1)}, u32[]{:S(2)}, u32[]{:S(2)}) collective-permute-start(bf16[4,192,512]{2,1,0:T(8,128)(2,1)S(1)} %bitcast_dynamic-update-slice_fusion), channel_id=1, source_target_pairs={{0,8},{1,9},{2,10},{3,11},{4,12},{5,13},{6,14},{7,15},{8,16},{9,17... | collective-permute-start | bytes 2359304 | tf_op jit(solution)/shard_map/ppermute | solution.py:28
  50.5 3.1 %collective-permute-start.10 = (bf16[4,192,512]{2,1,0:T(8,128)(2,1)S(1)}, bf16[4,192,512]{2,1,0:T(8,128)(2,1)S(1)}, u32[]{:S(2)}, u32[]{:S(2)}) collective-permute-start(bf16[4,192,512]{2,1,0:T(8,128)(2,1)S(1)} %bitcast_dynamic-update-slice_fusion), channel_id=1, source_target_pairs={{0,24},{1,25},{2,26},{3,27},{4,28},{5,29},{6,30},{7,31},{8,0},{9,1... | collective-permute-start | bytes 2359304 | tf_op jit(solution)/shard_map/ppermute | solution.py:28
  58.2 12.9 %collective-permute-done.8 = bf16[4,192,512]{2,1,0:T(8,128)(2,1)S(1)} collective-permute-done((bf16[4,192,512]{2,1,0:T(8,128)(2,1)S(1)}, bf16[4,192,512]{2,1,0:T(8,128)(2,1)S(1)}, u32[]{:S(2)}, u32[]{:S(2)}) %collective-permute-start.8) | collective-permute-done | bytes 786464 | tf_op jit(solution)/shard_map/ppermute | solution.py:28
  79.1 5.6 %collective-permute-done.12 = bf16[2,192,512]{2,1,0:T(8,128)(2,1)} collective-permute-done((bf16[2,192,512]{2,1,0:T(8,128)(2,1)}, bf16[2,192,512]{2,1,0:T(8,128)(2,1)}, u32[]{:S(2)}, u32[]{:S(2)}) %collective-permute-start.12) | collective-permute-done | bytes 393248 | tf_op jit(solution)/shard_map/ppermute | solution.py:28
  92.4 2.3 %fusion.64 = (bf16[2,4,2,192,512]{4,3,2,1,0:T(8,128)(2,1)S(1)}, bf16[2,4,2,192,512]{4,3,2,1,0:T(8,128)(2,1)}) fusion(bf16[4,4,2,192,512]{4,3,2,1,0:T(8,128)(2,1)S(1)} %fusion.28), kind=kLoop, calls=%fused_computation.127 | loop fusion | bytes 12582912 | tf_op jit(solution)/shard_map/slice | solution.py:133
  94.8 3.3 %broadcast_add_fusion = bf16[3072,1024]{1,0:T(8,128)(2,1)S(1)} fusion(bf16[3072,1024]{1,0:T(8,128)(2,1)} %all-gather.5.cloned.1.call-done, bf16[]{:T(256)} %bitcast.29), kind=kLoop, calls=%fused_computation.5 | loop fusion | flops 3145728 | bytes 12582914 | tf_op jit(solution)/shard_map/add | solution.py:87
  100.4 2.6 %fusion.10 = bf16[512,512]{1,0:T(8,128)(2,1)} fusion(bf16[3072,512]{1,0:T(8,128)(2,1)S(1)} %bitcast.151, bf16[3072,1024]{1,0:T(8,128)(2,1)S(1)} %broadcast_add_fusion), kind=kOutput, calls=%fused_computation.24 | convolution fusion | flops 1610874880 | bytes 6815744 | tf_op jit(solution)/shard_map/dot_general | solution.py:140
  104.4 3.4 %fusion.69 = f32[512,1024]{1,0:T(8,128)S(1)} fusion(bf16[3072,512]{1,0:T(8,128)(2,1)S(1)} %bitcast.149, bf16[3072,1024]{1,0:T(8,128)(2,1)S(1)} %broadcast_add_fusion), kind=kOutput, calls=%fused_computation.130 | convolution fusion | flops 3221225472 | bytes 11534336 | tf_op jit(solution)/shard_map/dot_general | solution.py:140
  107.9 5.6 %collective-permute-done.16 = bf16[512,512]{1,0:T(8,128)(2,1)S(1)} collective-permute-done((bf16[512,512]{1,0:T(8,128)(2,1)S(1)}, bf16[512,512]{1,0:T(8,128)(2,1)S(1)}, u32[]{:S(2)}, u32[]{:S(2)}) %collective-permute-start.16) | collective-permute-done | bytes 524320 | tf_op jit(solution)/shard_map/ppermute | solution.py:28
  120.3 4.5 %collective-permute-done.17 = bf16[512,512]{1,0:T(8,128)(2,1)} collective-permute-done((bf16[512,512]{1,0:T(8,128)(2,1)}, bf16[512,512]{1,0:T(8,128)(2,1)}, u32[]{:S(2)}, u32[]{:S(2)}) %collective-permute-start.17) | collective-permute-done | bytes 524320 | tf_op jit(solution)/shard_map/ppermute | solution.py:28
  127.5 3.0 %collective-permute-start.21 = (bf16[2,128,128]{2,1,0:T(8,128)(2,1)}, bf16[2,128,128]{2,1,0:T(8,128)(2,1)}, u32[]{:S(2)}, u32[]{:S(2)}) collective-permute-start(bf16[2,128,128]{2,1,0:T(8,128)(2,1)} %fusion.52), channel_id=1, source_target_pairs={{0,128},{1,129},{2,130},{3,131},{4,132},{5,133},{6,134},{7,135},{8... | collective-permute-start | bytes 196616 | tf_op jit(solution)/shard_map/ppermute | solution.py:28
  132.1 2.2 %fusion.15 = f32[512,2,128]{0,2,1:T(8,128)} fusion(f32[512,2]{0,1:T(2,128)S(1)} %get-tuple-element.29, bf16[2,128,128]{2,1,0:T(8,128)(2,1)S(1)} %collective-permute-done.18, bf16[2,128,128]{2,1,0:T(8,128)(2,1)S(1)} %collective-permute-done.19, bf16[2,128,128]{2,1,0:T(8,128)(2,1)} %copy-done.8, bf16[2,128,128]{2,1,0:T(8,128)(2,1)} %collective-permute-done.21, ...), kind=kOutput, calls=%fused_computation.28 | convolution fusion | flops 34734080 | bytes 1314848 | tf_op jit(solution)/shard_map/thd,hde->the/dot_general | solution.py:188
  134.3 2.3 %multiply_reduce_fusion = (f32[512,2]{0,1:T(2,128)S(1)}, f32[512,2,128]{0,2,1:T(8,128)S(1)}) fusion(f32[512,2,128]{0,2,1:T(8,128)} %fusion.15, f32[512,512]{1,0:T(8,128)S(1)} %copy-done.3, f32[2]{0:T(128)S(1)} %get-tuple-element.8, pred[512,512]{1,0:T(8,128)(4,1)S(1)} %copy-done.7, f32[512,2,1,128]{3,2,1,0:T(1,128)S(1)} %slice.135, ...), kind=kOutput, calls=%fused_computation.58 | convolution fusion | flops 271580160 | bytes 3674120 | tf_op jit(solution)/shard_map/hts,shd->thd/dot_general | solution.py:184
  136.7 2.3 %collective-permute-start.22 = (bf16[512,256]{0,1:T(8,128)(2,1)S(1)}, bf16[512,256]{0,1:T(8,128)(2,1)S(1)}, u32[]{:S(2)}, u32[]{:S(2)}) collective-permute-start(bf16[512,256]{0,1:T(8,128)(2,1)S(1)} %bitcast.162), channel_id=1, source_target_pairs={{0,16},{1,17},{2,18},{3,19},{4,20},{5,21},{6,22},{7,23},{8,24},{9,... | collective-permute-start | bytes 786440 | tf_op jit(solution)/shard_map/ppermute | solution.py:28
  141.9 2.4 %collective-permute-start.24 = (bf16[512,256]{0,1:T(8,128)(2,1)S(1)}, bf16[512,256]{0,1:T(8,128)(2,1)S(1)}, u32[]{:S(2)}, u32[]{:S(2)}) collective-permute-start(bf16[512,256]{0,1:T(8,128)(2,1)S(1)} %bitcast.164), channel_id=1, source_target_pairs={{0,24},{1,25},{2,26},{3,27},{4,28},{5,29},{6,30},{7,31},{8,0},{9,1... | collective-permute-start | bytes 786440 | tf_op jit(solution)/shard_map/ppermute | solution.py:28
  144.9 7.3 %collective-permute-done.23 = bf16[512,256]{0,1:T(8,128)(2,1)S(1)} collective-permute-done((bf16[512,256]{0,1:T(8,128)(2,1)S(1)}, bf16[512,256]{0,1:T(8,128)(2,1)S(1)}, u32[]{:S(2)}, u32[]{:S(2)}) %collective-permute-start.23) | collective-permute-done | bytes 262176 | tf_op jit(solution)/shard_map/ppermute | solution.py:28
  158.2 3.6 %collective-permute-start.26 = (bf16[192,512]{1,0:T(8,128)(2,1)S(1)}, bf16[192,512]{1,0:T(8,128)(2,1)S(1)}, u32[]{:S(2)}, u32[]{:S(2)}) collective-permute-start(bf16[192,512]{1,0:T(8,128)(2,1)S(1)} %get-tuple-element.19), channel_id=1, source_target_pairs={{0,4},{1,5},{2,6},{3,7},{4,0},{5,1},{6,2},{7,3},{8,12},{9,13},{10,... | collective-permute-start | bytes 589832 | tf_op jit(solution)/shard_map/ppermute | solution.py:28
  165.4 5.0 %collective-permute-done.26 = bf16[192,512]{1,0:T(8,128)(2,1)S(1)} collective-permute-done((bf16[192,512]{1,0:T(8,128)(2,1)S(1)}, bf16[192,512]{1,0:T(8,128)(2,1)S(1)}, u32[]{:S(2)}, u32[]{:S(2)}) %collective-permute-start.26) | collective-permute-done | bytes 196640 | tf_op jit(solution)/shard_map/ppermute | solution.py:28
  170.4 5.0 %collective-permute-done.27 = bf16[192,512]{1,0:T(8,128)(2,1)S(1)} collective-permute-done((bf16[192,512]{1,0:T(8,128)(2,1)S(1)}, bf16[192,512]{1,0:T(8,128)(2,1)S(1)}, u32[]{:S(2)}, u32[]{:S(2)}) %collective-permute-start.27) | collective-permute-done | bytes 196640 | tf_op jit(solution)/shard_map/ppermute | solution.py:28
  175.4 7.4 %collective-permute-done.28 = bf16[192,512]{1,0:T(8,128)(2,1)S(1)} collective-permute-done((bf16[192,512]{1,0:T(8,128)(2,1)S(1)}, bf16[192,512]{1,0:T(8,128)(2,1)S(1)}, u32[]{:S(2)}, u32[]{:S(2)}) %collective-permute-start.28) | collective-permute-done | bytes 196640 | tf_op jit(solution)/shard_map/ppermute | solution.py:28
  (139 shorter events, 56.3 us)
Async XLA Ops:
  6.5 88.2 %all-gather.5.cloned.1.call-start = ((), (), s32[]{:S(2)}) async-start(), calls=%async_computation.1 | async-start | bytes 7864320 | tf_op jit(solution)/shard_map/all_gather | solution.py:118
  13.9 126.0 %all-gather.3.cloned.1.call-start = ((), (), s32[]{:S(2)}) async-start(), calls=%async_computation | async-start | bytes 3932160 | tf_op jit(solution)/shard_map/all_gather | solution.py:136
  14.0 40.9 %collective-permute-start = (bf16[256,768]{1,0:T(8,128)(2,1)}, bf16[256,768]{1,0:T(8,128)(2,1)S(1)}, u32[]{:S(2)}, u32[]{:S(2)}) collective-permute-start(bf16[256,768]{1,0:T(8,128)(2,1)} %bitcast), channel_id=1, source_target_pairs={{0,0},{1,1},{2,2},{3,3},{4,4},{5,5},{6,6},{7,7},{8,64},{9,65},{10,... | collective-permute-start | bytes 1179656 | tf_op jit(solution)/shard_map/ppermute | solution.py:28
  15.6 39.3 %collective-permute-start.1 = (bf16[256,768]{1,0:T(8,128)(2,1)}, bf16[256,768]{1,0:T(8,128)(2,1)S(1)}, u32[]{:S(2)}, u32[]{:S(2)}) collective-permute-start(bf16[256,768]{1,0:T(8,128)(2,1)} %bitcast), channel_id=1, source_target_pairs={{16,0},{17,1},{18,2},{19,3},{20,4},{21,5},{22,6},{23,7},{24,64},{2... | collective-permute-start | bytes 1179656 | tf_op jit(solution)/shard_map/ppermute | solution.py:28
  18.1 11.8 %collective-permute-start.4 = (bf16[192,512]{1,0:T(8,128)(2,1)S(1)}, bf16[192,512]{1,0:T(8,128)(2,1)S(1)}, u32[]{:S(2)}, u32[]{:S(2)}) collective-permute-start(bf16[192,512]{1,0:T(8,128)(2,1)S(1)} %collective-permute-done.3), channel_id=1, source_target_pairs={{0,4},{1,5},{2,6},{3,7},{4,0},{5,1},{6,2},{7,3},{8,12},{9,13},{10,... | collective-permute-start | bytes 589832 | tf_op jit(solution)/shard_map/ppermute | solution.py:28
  25.9 12.7 %collective-permute-start.5 = (bf16[192,512]{1,0:T(8,128)(2,1)S(1)}, bf16[192,512]{1,0:T(8,128)(2,1)S(1)}, u32[]{:S(2)}, u32[]{:S(2)}) collective-permute-start(bf16[192,512]{1,0:T(8,128)(2,1)S(1)} %collective-permute-done.3), channel_id=1, source_target_pairs={{0,2},{1,3},{2,4},{3,5},{4,6},{5,7},{6,0},{7,1},{8,10},{9,11},{10,... | collective-permute-start | bytes 589832 | tf_op jit(solution)/shard_map/ppermute | solution.py:28
  27.1 11.5 %collective-permute-start.6 = (bf16[192,512]{1,0:T(8,128)(2,1)S(1)}, bf16[192,512]{1,0:T(8,128)(2,1)S(1)}, u32[]{:S(2)}, u32[]{:S(2)}) collective-permute-start(bf16[192,512]{1,0:T(8,128)(2,1)S(1)} %collective-permute-done.3), channel_id=1, source_target_pairs={{0,6},{1,7},{2,0},{3,1},{4,2},{5,3},{6,4},{7,5},{8,14},{9,15},{10,... | collective-permute-start | bytes 589832 | tf_op jit(solution)/shard_map/ppermute | solution.py:28
  38.6 32.5 %collective-permute-start.8 = (bf16[4,192,512]{2,1,0:T(8,128)(2,1)S(1)}, bf16[4,192,512]{2,1,0:T(8,128)(2,1)S(1)}, u32[]{:S(2)}, u32[]{:S(2)}) collective-permute-start(bf16[4,192,512]{2,1,0:T(8,128)(2,1)S(1)} %bitcast_dynamic-update-slice_fusion), channel_id=1, source_target_pairs={{0,8},{1,9},{2,10},{3,11},{4,12},{5,13},{6,14},{7,15},{8,16},{9,17... | collective-permute-start | bytes 2359304 | tf_op jit(solution)/shard_map/ppermute | solution.py:28
  50.5 21.5 %collective-permute-start.10 = (bf16[4,192,512]{2,1,0:T(8,128)(2,1)S(1)}, bf16[4,192,512]{2,1,0:T(8,128)(2,1)S(1)}, u32[]{:S(2)}, u32[]{:S(2)}) collective-permute-start(bf16[4,192,512]{2,1,0:T(8,128)(2,1)S(1)} %bitcast_dynamic-update-slice_fusion), channel_id=1, source_target_pairs={{0,24},{1,25},{2,26},{3,27},{4,28},{5,29},{6,30},{7,31},{8,0},{9,1... | collective-permute-start | bytes 2359304 | tf_op jit(solution)/shard_map/ppermute | solution.py:28
  54.2 20.7 %collective-permute-start.7 = (bf16[4,192,512]{2,1,0:T(8,128)(2,1)S(1)}, bf16[4,192,512]{2,1,0:T(8,128)(2,1)S(1)}, u32[]{:S(2)}, u32[]{:S(2)}) collective-permute-start(bf16[4,192,512]{2,1,0:T(8,128)(2,1)S(1)} %bitcast_dynamic-update-slice_fusion), channel_id=1, source_target_pairs={{0,1},{1,0},{2,3},{3,2},{4,5},{5,4},{6,7},{7,6},{8,9},{9,8},{10,11... | collective-permute-start | bytes 2359304 | tf_op jit(solution)/shard_map/ppermute | solution.py:28
  55.0 23.0 %collective-permute-start.2 = (bf16[2,256,768]{2,1,0:T(8,128)(2,1)S(1)}, bf16[2,256,768]{2,1,0:T(8,128)(2,1)S(1)}, u32[]{:S(2)}, u32[]{:S(2)}) collective-permute-start(bf16[2,256,768]{2,1,0:T(8,128)(2,1)S(1)} %pad_maximum_fusion.1), channel_id=1, source_target_pairs={{0,128},{1,129},{2,130},{3,131},{4,132},{5,133},{6,134},{7,135},{8... | collective-permute-start | bytes 2359304 | tf_op jit(solution)/shard_map/ppermute | solution.py:28
  71.1 16.4 %collective-permute-start.9 = (bf16[4,192,512]{2,1,0:T(8,128)(2,1)S(1)}, bf16[4,192,512]{2,1,0:T(8,128)(2,1)}, u32[]{:S(2)}, u32[]{:S(2)}) collective-permute-start(bf16[4,192,512]{2,1,0:T(8,128)(2,1)S(1)} %collective-permute-done.8), channel_id=1, source_target_pairs={{0,1},{1,0},{2,3},{3,2},{4,5},{5,4},{6,7},{7,6},{8,9},{9,8},{10,11... | collective-permute-start | bytes 2359304 | tf_op jit(solution)/shard_map/ppermute | solution.py:28
  72.0 16.9 %collective-permute-start.11 = (bf16[4,192,512]{2,1,0:T(8,128)(2,1)S(1)}, bf16[4,192,512]{2,1,0:T(8,128)(2,1)}, u32[]{:S(2)}, u32[]{:S(2)}) collective-permute-start(bf16[4,192,512]{2,1,0:T(8,128)(2,1)S(1)} %collective-permute-done.10), channel_id=1, source_target_pairs={{0,1},{1,0},{2,3},{3,2},{4,5},{5,4},{6,7},{7,6},{8,9},{9,8},{10,11... | collective-permute-start | bytes 2359304 | tf_op jit(solution)/shard_map/ppermute | solution.py:28
  72.8 11.9 %collective-permute-start.12 = (bf16[2,192,512]{2,1,0:T(8,128)(2,1)}, bf16[2,192,512]{2,1,0:T(8,128)(2,1)}, u32[]{:S(2)}, u32[]{:S(2)}) collective-permute-start(bf16[2,192,512]{2,1,0:T(8,128)(2,1)} %slice_add_fusion.2), channel_id=1, source_target_pairs={{0,8},{1,9},{2,10},{3,11},{4,12},{5,13},{6,14},{7,15},{8,16},{9,17... | collective-permute-start | bytes 1179656 | tf_op jit(solution)/shard_map/ppermute | solution.py:28
  74.9 12.4 %collective-permute-start.14 = (bf16[2,192,512]{2,1,0:T(8,128)(2,1)S(1)}, bf16[2,192,512]{2,1,0:T(8,128)(2,1)}, u32[]{:S(2)}, u32[]{:S(2)}) collective-permute-start(bf16[2,192,512]{2,1,0:T(8,128)(2,1)S(1)} %slice.122), channel_id=1, source_target_pairs={{0,24},{1,25},{2,26},{3,27},{4,28},{5,29},{6,30},{7,31},{8,0},{9,1... | collective-permute-start | bytes 1179656 | tf_op jit(solution)/shard_map/ppermute | solution.py:28
  100.3 13.2 %collective-permute-start.16 = (bf16[512,512]{1,0:T(8,128)(2,1)S(1)}, bf16[512,512]{1,0:T(8,128)(2,1)S(1)}, u32[]{:S(2)}, u32[]{:S(2)}) collective-permute-start(bf16[512,512]{1,0:T(8,128)(2,1)S(1)} %fusion.7), channel_id=1, source_target_pairs={{0,128},{1,129},{2,130},{3,131},{4,132},{5,133},{6,134},{7,135},{8... | collective-permute-start | bytes 1572872 | tf_op jit(solution)/shard_map/ppermute | solution.py:28
  103.0 21.7 %collective-permute-start.17 = (bf16[512,512]{1,0:T(8,128)(2,1)}, bf16[512,512]{1,0:T(8,128)(2,1)}, u32[]{:S(2)}, u32[]{:S(2)}) collective-permute-start(bf16[512,512]{1,0:T(8,128)(2,1)} %fusion.10), channel_id=1, source_target_pairs={{0,128},{1,129},{2,130},{3,131},{4,132},{5,133},{6,134},{7,135},{8... | collective-permute-start | bytes 1572872 | tf_op jit(solution)/shard_map/ppermute | solution.py:28
  115.9 10.8 %collective-permute-start.18 = (bf16[2,128,128]{2,1,0:T(8,128)(2,1)S(1)}, bf16[2,128,128]{2,1,0:T(8,128)(2,1)S(1)}, u32[]{:S(2)}, u32[]{:S(2)}) collective-permute-start(bf16[2,128,128]{2,1,0:T(8,128)(2,1)S(1)} %convolution_convert_fusion), channel_id=1, source_target_pairs={{0,64},{1,65},{2,66},{3,67},{4,68},{5,69},{6,70},{7,71},{8,72},{9,... | collective-permute-start | bytes 196616 | tf_op jit(solution)/shard_map/ppermute | solution.py:28
  116.4 10.3 %collective-permute-start.19 = (bf16[2,128,128]{2,1,0:T(8,128)(2,1)S(1)}, bf16[2,128,128]{2,1,0:T(8,128)(2,1)S(1)}, u32[]{:S(2)}, u32[]{:S(2)}) collective-permute-start(bf16[2,128,128]{2,1,0:T(8,128)(2,1)S(1)} %convolution_convert_fusion), channel_id=1, source_target_pairs={{0,32},{1,33},{2,34},{3,35},{4,36},{5,37},{6,38},{7,39},{8,40},{9,... | collective-permute-start | bytes 196616 | tf_op jit(solution)/shard_map/ppermute | solution.py:28
  139.0 13.1 %collective-permute-start.23 = (bf16[512,256]{0,1:T(8,128)(2,1)S(1)}, bf16[512,256]{0,1:T(8,128)(2,1)S(1)}, u32[]{:S(2)}, u32[]{:S(2)}) collective-permute-start(bf16[512,256]{0,1:T(8,128)(2,1)S(1)} %bitcast.163), channel_id=1, source_target_pairs={{0,8},{1,9},{2,10},{3,11},{4,12},{5,13},{6,14},{7,15},{8,16},{9,17... | collective-permute-start | bytes 786440 | tf_op jit(solution)/shard_map/ppermute | solution.py:28
  141.9 10.3 %collective-permute-start.24 = (bf16[512,256]{0,1:T(8,128)(2,1)S(1)}, bf16[512,256]{0,1:T(8,128)(2,1)S(1)}, u32[]{:S(2)}, u32[]{:S(2)}) collective-permute-start(bf16[512,256]{0,1:T(8,128)(2,1)S(1)} %bitcast.164), channel_id=1, source_target_pairs={{0,24},{1,25},{2,26},{3,27},{4,28},{5,29},{6,30},{7,31},{8,0},{9,1... | collective-permute-start | bytes 786440 | tf_op jit(solution)/shard_map/ppermute | solution.py:28
  158.2 12.2 %collective-permute-start.26 = (bf16[192,512]{1,0:T(8,128)(2,1)S(1)}, bf16[192,512]{1,0:T(8,128)(2,1)S(1)}, u32[]{:S(2)}, u32[]{:S(2)}) collective-permute-start(bf16[192,512]{1,0:T(8,128)(2,1)S(1)} %get-tuple-element.19), channel_id=1, source_target_pairs={{0,4},{1,5},{2,6},{3,7},{4,0},{5,1},{6,2},{7,3},{8,12},{9,13},{10,... | collective-permute-start | bytes 589832 | tf_op jit(solution)/shard_map/ppermute | solution.py:28
  161.8 13.6 %collective-permute-start.27 = (bf16[192,512]{1,0:T(8,128)(2,1)S(1)}, bf16[192,512]{1,0:T(8,128)(2,1)S(1)}, u32[]{:S(2)}, u32[]{:S(2)}) collective-permute-start(bf16[192,512]{1,0:T(8,128)(2,1)S(1)} %get-tuple-element.21), channel_id=1, source_target_pairs={{0,2},{1,3},{2,4},{3,5},{4,6},{5,7},{6,0},{7,1},{8,10},{9,11},{10,... | collective-permute-start | bytes 589832 | tf_op jit(solution)/shard_map/ppermute | solution.py:28
  163.7 19.1 %collective-permute-start.28 = (bf16[192,512]{1,0:T(8,128)(2,1)S(1)}, bf16[192,512]{1,0:T(8,128)(2,1)S(1)}, u32[]{:S(2)}, u32[]{:S(2)}) collective-permute-start(bf16[192,512]{1,0:T(8,128)(2,1)S(1)} %get-tuple-element.20), channel_id=1, source_target_pairs={{0,6},{1,7},{2,0},{3,1},{4,2},{5,3},{6,4},{7,5},{8,14},{9,15},{10,... | collective-permute-start | bytes 589832 | tf_op jit(solution)/shard_map/ppermute | solution.py:28
  (23 other events, 125.4 us)
Sparse Core Ops, SparseCore 0:
  14.0 78.1 all-gather.4
  94.1 45.6 all-gather.2

commit v5 on v4

--- a/solution.py
+++ b/solution.py
@@ -108,7 +108,7 @@
     moved = send(tokens.T, tokens_to_half)
     w_block = w_qkvg.reshape(2, 2, tokens.shape[1], -1)
     kv_cuts = [(4 * h + 1, 4 * h + 3) for h in range(heads)]
-    qg_cuts = [(0, 1)] + [(4 * h + 3, 4 * h + 5) for h in range(heads - 1)] + [(4 * heads - 1, 4 * heads)]
+    qg_cuts = [(4 * h, 4 * h + 1) for h in range(heads)] + [(4 * h + 3, 4 * h + 4) for h in range(heads)]
     w_block = jnp.concatenate(
         [w_block[..., low * size : high * size] for low, high in kv_cuts + qg_cuts], axis=-1
     )
@@ -136,25 +136,30 @@
     w_out_all = lax.all_gather(w_out_pair, "x", axis=0, tiled=True)
     weight_cols = after(weight_cols, swapped[0])
 
-    def projection(a, b):
-        return lax.dot_general(a, b, (((0,), (0,)), ((), ())), preferred_element_type=F32)
+    def columns_first(weights, rows_last):
+        return lax.dot_general(
+            weights, rows_last, (((0,), (0,)), ((), ())), preferred_element_type=F32
+        )
 
     w_kv, w_qg = jnp.split(weight_cols, 2, axis=1)
-    kv_theirs = projection(theirs, w_kv).astype(BF)
+    kv_theirs = columns_first(w_kv, theirs).astype(BF)
     kv_sent = send(kv_theirs, other_zl)
-    qg_sent = send(projection(theirs, w_qg).astype(BF), other_zl)
-    kv_own, qg_own = jnp.split(projection(mine, weight_cols), 2, axis=1)
-    kv = (kv_own + kv_sent.astype(F32)).astype(BF).astype(F32)
-    qg = (qg_own + qg_sent.astype(F32)).astype(BF).astype(F32)
-
-    kv = jax.nn.silu(kv).reshape(rows, heads, 2, size)
-    keys_act, values_act = kv[:, :, 0], kv[:, :, 1].astype(BF)
+    q_theirs, g_theirs = jnp.split(columns_first(w_qg, theirs).astype(BF), 2, axis=0)
+    q_sent, g_sent = send(q_theirs, other_zl), send(g_theirs, other_zl)
+    span = heads * size
+    own_part = columns_first(weight_cols, mine)
+    kv = (own_part[: 2 * span] + kv_sent.astype(F32)).astype(BF).astype(F32)
+    q_part = (own_part[2 * span : 3 * span] + q_sent.astype(F32)).astype(BF).astype(F32)
+    g_part = (own_part[3 * span :] + g_sent.astype(F32)).astype(BF).astype(F32)
+
+    kv = jax.nn.silu(kv).reshape(heads, 2, size, rows)
+    keys_act, values_act = kv[:, 0], kv[:, 1].astype(BF)
     rate_vec = decay_rates(decay_index, rows * 8)
     local_pos = jnp.arange(rows, dtype=F32)
-    state_weight = jnp.exp(-rate_vec[None, :] * (rows - 1.0 - local_pos)[:, None])
+    state_weight = jnp.exp(-rate_vec[:, None] * (rows - 1.0 - local_pos)[None, :])
     local_state = jnp.einsum(
-        "shd,she->hde",
-        (keys_act * state_weight[:, :, None]).astype(BF),
+        "hds,hes->hde",
+        (keys_act * state_weight[:, None]).astype(BF),
         values_act,
         preferred_element_type=F32,
     ).astype(BF)
@@ -172,44 +177,40 @@
         total += power((3 - (place + 4 - step) % 4).astype(F32)) * earlier
     carried += power(place.astype(F32)) * send(total.astype(BF), later_half).astype(F32)
 
-    qg = after(qg, local_state).reshape(rows, heads, 2, size)
-    queries, gate_part = jax.nn.silu(qg[:, :, 0]).astype(BF), qg[:, :, 1]
+    queries = jax.nn.silu(after(q_part, local_state)).astype(BF).reshape(heads, size, rows)
     distance = local_pos[:, None] - local_pos[None, :]
     weight = jnp.where(
         distance[None] >= 0,
         jnp.exp(-rate_vec[:, None, None] * jnp.maximum(distance, 0.0)[None]),
         0.0,
     )
-    scores = jnp.einsum("thd,shd->hts", queries, keys_act, preferred_element_type=F32) * weight
+    scores = jnp.einsum("hdt,hds->hts", queries, keys_act, preferred_element_type=F32) * weight
     inner_part = jnp.einsum(
-        "hts,shd->thd", scores.astype(BF), values_act, preferred_element_type=F32
-    )
-    entry_decay = jnp.exp(-rate_vec[None, :] * (local_pos[:, None] + 1.0))
-    carried_part = entry_decay[:, :, None] * jnp.einsum(
-        "thd,hde->the", queries, carried.astype(BF), preferred_element_type=F32
+        "hts,hes->het", scores.astype(BF), values_act, preferred_element_type=F32
+    )
+    entry_decay = jnp.exp(-rate_vec[:, None] * (local_pos[None, :] + 1.0))
+    carried_part = entry_decay[:, None] * jnp.einsum(
+        "hdt,hde->het", queries, carried.astype(BF), preferred_element_type=F32
     )
     attended = inner_part + carried_part
-    mean_square = jnp.mean(attended * attended, axis=-1, keepdims=True)
-    normed = attended * lax.rsqrt(mean_square + 1e-06) * norm_gain[None]
-    hidden = (normed * jax.nn.sigmoid(gate_part)).astype(BF).reshape(rows, heads * size)
+    mean_square = jnp.mean(attended * attended, axis=1, keepdims=True)
+    normed = attended * lax.rsqrt(mean_square + 1e-06) * norm_gain[:, :, None]
+    gate = jax.nn.sigmoid(g_part.reshape(heads, size, rows))
+    hidden = (normed * gate).astype(BF).reshape(span, rows)
 
     def slot(origin):
         return (origin % 2 * 2 + origin // 2) * heads * size
 
-    hidden_all = jnp.zeros((rows, 4 * heads * size), BF)
-    hidden_all = lax.dynamic_update_slice(hidden_all, hidden, (0, slot(y)))
+    hidden_all = jnp.zeros((4 * span, rows), BF)
+    hidden_all = lax.dynamic_update_slice(hidden_all, hidden, (slot(y), 0))
     for step in (2, 1, 3):
         piece = send(hidden, along_y(step))
-        hidden_all = lax.dynamic_update_slice(hidden_all, piece, (0, slot((y + 4 - step) % 4)))
-
-    span = 2 * heads * size
-    w_out_all = w_out_all.reshape(4, span, -1)
-    near, far = hidden_all[:, :span], hidden_all[:, span:]
-
-    def columns_first(weights, rows_first):
-        return lax.dot_general(
-            weights, rows_first, (((0,), (1,)), ((), ())), preferred_element_type=F32
-        )
+        if step == 2:
+            w_out_all = after(w_out_all, piece)
+        hidden_all = lax.dynamic_update_slice(hidden_all, piece, (slot((y + 4 - step) % 4), 0))
+
+    w_out_all = w_out_all.reshape(4, 2 * span, -1)
+    near, far = hidden_all[: 2 * span], hidden_all[2 * span :]
 
     blocks = jnp.stack(
         [columns_first(w_out_all[p], near) + columns_first(w_out_all[2 + p], far) for p in range(2)]

time: 191 us -> 185 us (0.969)
  the two profiles are of different devices: /device:TPU:1 before, /device:TPU:4 now
where the time goes in v5:
time: 185 us; the launch traced here: 182 us
  waiting for transfers between devices  62.4 us (34%)
  starting transfers between devices  59 us (32%)
  other arithmetic  20.1 us (11%)
  between operations  17.5 us (9%)
  matrix products  12.9 us (7%)
  local copies, waits for them, and re-layouts  10.3 us (6%)
    ppermute x30, waiting for transfers between devices, send(): return lax.ppermute(array, AXES, moves(target))  62 us
    ppermute x30, starting transfers between devices, send(): return lax.ppermute(array, AXES, moves(target))  58.9 us
    dot_general x7, matrix products, columns_first(): lax.dot_general(weights, rows_last, (((0,), (0,)), ((), ())), preferred_e...  9.46 us
    add x4, other arithmetic, after(): return array + other[(0,) * other.ndim] * jnp.zeros((), array.dtype)  7.5 us
    dynamic_update_slice x5, other arithmetic, local(): lax.dynamic_update_slice(gathered, both[None], (place, start, 0, 0, 0))  4.97 us
  transfers between devices with their start and end apart: 32, of which 17 were waited for; matrix products, arithmetic and copies ran while one was open for 20% of the time, Pallas kernels for 0%

profile of v5, /device:TPU:4, one launch (start us, length us, event | category | flops | bytes accessed | tf_op | source)
XLA Modules:
  0.0 182.2 jit_solution(4932366428876719336)
XLA Ops:
  8.1 2.8 %reshape.162 = bf16[2,2,192,1024]{3,2,1,0:T(8,128)(2,1)S(1)} reshape(bf16[768,2,512]{2,1,0:T(2,128)(2,1)} %param.6) | data formatting | bytes 3145728 | tf_op jit(solution)/shard_map/reshape | solution.py:109
  14.1 3.4 %collective-permute-start = (bf16[256,768]{1,0:T(8,128)(2,1)}, bf16[256,768]{1,0:T(8,128)(2,1)S(1)}, u32[]{:S(2)}, u32[]{:S(2)}) collective-permute-start(bf16[256,768]{1,0:T(8,128)(2,1)} %bitcast), channel_id=1, source_target_pairs={{0,0},{1,1},{2,2},{3,3},{4,4},{5,5},{6,6},{7,7},{8,64},{9,65},{10,... | collective-permute-start | bytes 1179656 | tf_op jit(solution)/shard_map/ppermute | solution.py:28
  19.0 7.3 %collective-permute-start.4 = (bf16[192,512]{1,0:T(8,128)(2,1)S(1)}, bf16[192,512]{1,0:T(8,128)(2,1)S(1)}, u32[]{:S(2)}, u32[]{:S(2)}) collective-permute-start(bf16[192,512]{1,0:T(8,128)(2,1)S(1)} %collective-permute-done.3), channel_id=1, source_target_pairs={{0,4},{1,5},{2,6},{3,7},{4,0},{5,1},{6,2},{7,3},{8,12},{9,13},{10,... | collective-permute-start | bytes 589832 | tf_op jit(solution)/shard_map/ppermute | solution.py:28
  27.8 2.7 %collective-permute-start.6 = (bf16[192,512]{1,0:T(8,128)(2,1)S(1)}, bf16[192,512]{1,0:T(8,128)(2,1)S(1)}, u32[]{:S(2)}, u32[]{:S(2)}) collective-permute-start(bf16[192,512]{1,0:T(8,128)(2,1)S(1)} %collective-permute-done.3), channel_id=1, source_target_pairs={{0,6},{1,7},{2,0},{3,1},{4,2},{5,3},{6,4},{7,5},{8,14},{9,15},{10,... | collective-permute-start | bytes 589832 | tf_op jit(solution)/shard_map/ppermute | solution.py:28
  30.5 4.8 %collective-permute-done.4 = bf16[192,512]{1,0:T(8,128)(2,1)S(1)} collective-permute-done((bf16[192,512]{1,0:T(8,128)(2,1)S(1)}, bf16[192,512]{1,0:T(8,128)(2,1)S(1)}, u32[]{:S(2)}, u32[]{:S(2)}) %collective-permute-start.4) | collective-permute-done | bytes 196640 | tf_op jit(solution)/shard_map/ppermute | solution.py:28
  35.3 3.6 %collective-permute-done.5 = bf16[192,512]{1,0:T(8,128)(2,1)S(1)} collective-permute-done((bf16[192,512]{1,0:T(8,128)(2,1)S(1)}, bf16[192,512]{1,0:T(8,128)(2,1)S(1)}, u32[]{:S(2)}, u32[]{:S(2)}) %collective-permute-start.5) | collective-permute-done | bytes 196640 | tf_op jit(solution)/shard_map/ppermute | solution.py:28
  38.9 4.2 %collective-permute-done.6 = bf16[192,512]{1,0:T(8,128)(2,1)S(1)} collective-permute-done((bf16[192,512]{1,0:T(8,128)(2,1)S(1)}, bf16[192,512]{1,0:T(8,128)(2,1)S(1)}, u32[]{:S(2)}, u32[]{:S(2)}) %collective-permute-start.6) | collective-permute-done | bytes 196640 | tf_op jit(solution)/shard_map/ppermute | solution.py:28
  43.3 5.8 %collective-permute-start.10 = (bf16[4,192,512]{2,1,0:T(8,128)(2,1)S(1)}, bf16[4,192,512]{2,1,0:T(8,128)(2,1)S(1)}, u32[]{:S(2)}, u32[]{:S(2)}) collective-permute-start(bf16[4,192,512]{2,1,0:T(8,128)(2,1)S(1)} %bitcast_dynamic-update-slice_fusion), channel_id=1, source_target_pairs={{0,24},{1,25},{2,26},{3,27},{4,28},{5,29},{6,30},{7,31},{8,0},{9,1... | collective-permute-start | bytes 2359304 | tf_op jit(solution)/shard_map/ppermute | solution.py:28
  49.3 4.4 %collective-permute-start.2 = (bf16[2,256,768]{2,1,0:T(8,128)(2,1)S(1)}, bf16[2,256,768]{2,1,0:T(8,128)(2,1)S(1)}, u32[]{:S(2)}, u32[]{:S(2)}) collective-permute-start(bf16[2,256,768]{2,1,0:T(8,128)(2,1)S(1)} %pad_maximum_fusion.1), channel_id=1, source_target_pairs={{0,128},{1,129},{2,130},{3,131},{4,132},{5,133},{6,134},{7,135},{8... | collective-permute-start | bytes 2359304 | tf_op jit(solution)/shard_map/ppermute | solution.py:28
  55.6 10.4 %collective-permute-done.8 = bf16[4,192,512]{2,1,0:T(8,128)(2,1)S(1)} collective-permute-done((bf16[4,192,512]{2,1,0:T(8,128)(2,1)S(1)}, bf16[4,192,512]{2,1,0:T(8,128)(2,1)S(1)}, u32[]{:S(2)}, u32[]{:S(2)}) %collective-permute-start.8) | collective-permute-done | bytes 786464 | tf_op jit(solution)/shard_map/ppermute | solution.py:28
  74.8 6.3 %collective-permute-done.12 = bf16[2,192,512]{2,1,0:T(8,128)(2,1)} collective-permute-done((bf16[2,192,512]{2,1,0:T(8,128)(2,1)}, bf16[2,192,512]{2,1,0:T(8,128)(2,1)}, u32[]{:S(2)}, u32[]{:S(2)}) %collective-permute-start.12) | collective-permute-done | bytes 393248 | tf_op jit(solution)/shard_map/ppermute | solution.py:28
  90.9 3.3 %broadcast_add_fusion = bf16[3072,1024]{1,0:T(8,128)(2,1)S(1)} fusion(bf16[3072,1024]{1,0:T(8,128)(2,1)} %all-gather.5.cloned.1.call-done, bf16[]{:T(256)} %bitcast.10), kind=kLoop, calls=%fused_computation.5 | loop fusion | flops 3145728 | bytes 12582914 | tf_op jit(solution)/shard_map/add | solution.py:87
  102.0 3.4 %fusion.67 = f32[1024,512]{1,0:T(8,128)S(1)} fusion(bf16[3072,1024]{1,0:T(8,128)(2,1)S(1)} %broadcast_add_fusion, bf16[3072,512]{1,0:T(8,128)(2,1)S(1)} %bitcast.136), kind=kOutput, calls=%fused_computation.130 | convolution fusion | flops 3221225472 | bytes 11534336 | tf_op jit(solution)/shard_map/dot_general | solution.py:140
  105.5 5.8 %collective-permute-done.16 = bf16[512,512]{1,0:T(8,128)(2,1)S(1)} collective-permute-done((bf16[512,512]{1,0:T(8,128)(2,1)S(1)}, bf16[512,512]{1,0:T(8,128)(2,1)S(1)}, u32[]{:S(2)}, u32[]{:S(2)}) %collective-permute-start.16) | collective-permute-done | bytes 524320 | tf_op jit(solution)/shard_map/ppermute | solution.py:28
  121.8 3.0 %collective-permute-start.21 = (bf16[2,128,128]{2,1,0:T(8,128)(2,1)S(1)}, bf16[2,128,128]{2,1,0:T(8,128)(2,1)S(1)}, u32[]{:S(2)}, u32[]{:S(2)}) collective-permute-start(bf16[2,128,128]{2,1,0:T(8,128)(2,1)S(1)} %fusion.50), channel_id=1, source_target_pairs={{0,128},{1,129},{2,130},{3,131},{4,132},{5,133},{6,134},{7,135},{8... | collective-permute-start | bytes 196616 | tf_op jit(solution)/shard_map/ppermute | solution.py:28
  126.9 2.8 %multiply_reduce_fusion = (f32[2,512]{1,0:T(2,128)S(1)}, f32[2,128,512]{2,1,0:T(8,128)}) fusion(f32[2,128,512]{2,1,0:T(8,128)S(1)} %convolution_multiply_fusion, bf16[2,128,512]{2,1,0:T(8,128)(2,1)S(1)} %bitcast.151, f32[512,512]{1,0:T(8,128)S(1)} %copy-done.1, f32[2]{0:T(128)S(1)} %get-tuple-element.8, pred[512,512]{1,0:T(8,128)(4,1)} %fusion.22, ...), kind=kOutput, calls=%fused_computation.57 | convolution fusion | flops 270924800 | bytes 3412480 | tf_op jit(solution)/shard_map/hts,hes->het/dot_general | solution.py:188
  130.9 3.1 %collective-permute-start.23 = (bf16[256,512]{1,0:T(8,128)(2,1)S(1)}, bf16[256,512]{1,0:T(8,128)(2,1)S(1)}, u32[]{:S(2)}, u32[]{:S(2)}) collective-permute-start(bf16[256,512]{1,0:T(8,128)(2,1)S(1)} %bitcast.152), channel_id=1, source_target_pairs={{0,16},{1,17},{2,18},{3,19},{4,20},{5,21},{6,22},{7,23},{8,24},{9,... | collective-permute-start | bytes 786440 | tf_op jit(solution)/shard_map/ppermute | solution.py:28
  134.5 2.7 %collective-permute-start.25 = (bf16[256,512]{1,0:T(8,128)(2,1)S(1)}, bf16[256,512]{1,0:T(8,128)(2,1)S(1)}, u32[]{:S(2)}, u32[]{:S(2)}) collective-permute-start(bf16[256,512]{1,0:T(8,128)(2,1)S(1)} %bitcast.154), channel_id=1, source_target_pairs={{0,24},{1,25},{2,26},{3,27},{4,28},{5,29},{6,30},{7,31},{8,0},{9,1... | collective-permute-start | bytes 786440 | tf_op jit(solution)/shard_map/ppermute | solution.py:28
  137.3 2.6 %collective-permute-done.23 = bf16[256,512]{1,0:T(8,128)(2,1)S(1)} collective-permute-done((bf16[256,512]{1,0:T(8,128)(2,1)S(1)}, bf16[256,512]{1,0:T(8,128)(2,1)S(1)}, u32[]{:S(2)}, u32[]{:S(2)}) %collective-permute-start.23) | collective-permute-done | bytes 262176 | tf_op jit(solution)/shard_map/ppermute | solution.py:28
  149.3 4.9 %collective-permute-start.27 = (bf16[192,512]{1,0:T(8,128)(2,1)S(1)}, bf16[192,512]{1,0:T(8,128)(2,1)S(1)}, u32[]{:S(2)}, u32[]{:S(2)}) collective-permute-start(bf16[192,512]{1,0:T(8,128)(2,1)S(1)} %get-tuple-element.19), channel_id=1, source_target_pairs={{0,4},{1,5},{2,6},{3,7},{4,0},{5,1},{6,2},{7,3},{8,12},{9,13},{10,... | collective-permute-start | bytes 589832 | tf_op jit(solution)/shard_map/ppermute | solution.py:28
  155.0 3.4 %collective-permute-start.29 = (bf16[192,512]{1,0:T(8,128)(2,1)S(1)}, bf16[192,512]{1,0:T(8,128)(2,1)S(1)}, u32[]{:S(2)}, u32[]{:S(2)}) collective-permute-start(bf16[192,512]{1,0:T(8,128)(2,1)S(1)} %get-tuple-element.20), channel_id=1, source_target_pairs={{0,6},{1,7},{2,0},{3,1},{4,2},{5,3},{6,4},{7,5},{8,14},{9,15},{10,... | collective-permute-start | bytes 589832 | tf_op jit(solution)/shard_map/ppermute | solution.py:28
  158.4 4.6 %collective-permute-done.27 = bf16[192,512]{1,0:T(8,128)(2,1)S(1)} collective-permute-done((bf16[192,512]{1,0:T(8,128)(2,1)S(1)}, bf16[192,512]{1,0:T(8,128)(2,1)S(1)}, u32[]{:S(2)}, u32[]{:S(2)}) %collective-permute-start.27) | collective-permute-done | bytes 196640 | tf_op jit(solution)/shard_map/ppermute | solution.py:28
  163.0 5.8 %collective-permute-done.28 = bf16[192,512]{1,0:T(8,128)(2,1)S(1)} collective-permute-done((bf16[192,512]{1,0:T(8,128)(2,1)S(1)}, bf16[192,512]{1,0:T(8,128)(2,1)S(1)}, u32[]{:S(2)}, u32[]{:S(2)}) %collective-permute-start.28) | collective-permute-done | bytes 196640 | tf_op jit(solution)/shard_map/ppermute | solution.py:28
  168.8 5.7 %collective-permute-done.29 = bf16[192,512]{1,0:T(8,128)(2,1)S(1)} collective-permute-done((bf16[192,512]{1,0:T(8,128)(2,1)S(1)}, bf16[192,512]{1,0:T(8,128)(2,1)S(1)}, u32[]{:S(2)}, u32[]{:S(2)}) %collective-permute-start.29) | collective-permute-done | bytes 196640 | tf_op jit(solution)/shard_map/ppermute | solution.py:28
  (133 shorter events, 57.8 us)
Async XLA Ops:
  6.5 84.3 %all-gather.5.cloned.1.call-start = ((), (), s32[]{:S(2)}) async-start(), calls=%async_computation.1 | async-start | bytes 7864320 | tf_op jit(solution)/shard_map/all_gather | solution.py:118
  14.1 127.1 %all-gather.3.cloned.1.call-start = ((), (), s32[]{:S(2)}) async-start(), calls=%async_computation | async-start | bytes 3932160 | tf_op jit(solution)/shard_map/all_gather | solution.py:136
  14.1 35.1 %collective-permute-start = (bf16[256,768]{1,0:T(8,128)(2,1)}, bf16[256,768]{1,0:T(8,128)(2,1)S(1)}, u32[]{:S(2)}, u32[]{:S(2)}) collective-permute-start(bf16[256,768]{1,0:T(8,128)(2,1)} %bitcast), channel_id=1, source_target_pairs={{0,0},{1,1},{2,2},{3,3},{4,4},{5,5},{6,6},{7,7},{8,64},{9,65},{10,... | collective-permute-start | bytes 1179656 | tf_op jit(solution)/shard_map/ppermute | solution.py:28
  17.6 31.6 %collective-permute-start.1 = (bf16[256,768]{1,0:T(8,128)(2,1)}, bf16[256,768]{1,0:T(8,128)(2,1)S(1)}, u32[]{:S(2)}, u32[]{:S(2)}) collective-permute-start(bf16[256,768]{1,0:T(8,128)(2,1)} %bitcast), channel_id=1, source_target_pairs={{16,0},{17,1},{18,2},{19,3},{20,4},{21,5},{22,6},{23,7},{24,64},{2... | collective-permute-start | bytes 1179656 | tf_op jit(solution)/shard_map/ppermute | solution.py:28
  19.0 16.3 %collective-permute-start.4 = (bf16[192,512]{1,0:T(8,128)(2,1)S(1)}, bf16[192,512]{1,0:T(8,128)(2,1)S(1)}, u32[]{:S(2)}, u32[]{:S(2)}) collective-permute-start(bf16[192,512]{1,0:T(8,128)(2,1)S(1)} %collective-permute-done.3), channel_id=1, source_target_pairs={{0,4},{1,5},{2,6},{3,7},{4,0},{5,1},{6,2},{7,3},{8,12},{9,13},{10,... | collective-permute-start | bytes 589832 | tf_op jit(solution)/shard_map/ppermute | solution.py:28
  26.3 12.6 %collective-permute-start.5 = (bf16[192,512]{1,0:T(8,128)(2,1)S(1)}, bf16[192,512]{1,0:T(8,128)(2,1)S(1)}, u32[]{:S(2)}, u32[]{:S(2)}) collective-permute-start(bf16[192,512]{1,0:T(8,128)(2,1)S(1)} %collective-permute-done.3), channel_id=1, source_target_pairs={{0,2},{1,3},{2,4},{3,5},{4,6},{5,7},{6,0},{7,1},{8,10},{9,11},{10,... | collective-permute-start | bytes 589832 | tf_op jit(solution)/shard_map/ppermute | solution.py:28
  27.8 15.4 %collective-permute-start.6 = (bf16[192,512]{1,0:T(8,128)(2,1)S(1)}, bf16[192,512]{1,0:T(8,128)(2,1)S(1)}, u32[]{:S(2)}, u32[]{:S(2)}) collective-permute-start(bf16[192,512]{1,0:T(8,128)(2,1)S(1)} %collective-permute-done.3), channel_id=1, source_target_pairs={{0,6},{1,7},{2,0},{3,1},{4,2},{5,3},{6,4},{7,5},{8,14},{9,15},{10,... | collective-permute-start | bytes 589832 | tf_op jit(solution)/shard_map/ppermute | solution.py:28
  43.2 22.8 %collective-permute-start.8 = (bf16[4,192,512]{2,1,0:T(8,128)(2,1)S(1)}, bf16[4,192,512]{2,1,0:T(8,128)(2,1)S(1)}, u32[]{:S(2)}, u32[]{:S(2)}) collective-permute-start(bf16[4,192,512]{2,1,0:T(8,128)(2,1)S(1)} %bitcast_dynamic-update-slice_fusion), channel_id=1, source_target_pairs={{0,8},{1,9},{2,10},{3,11},{4,12},{5,13},{6,14},{7,15},{8,16},{9,17... | collective-permute-start | bytes 2359304 | tf_op jit(solution)/shard_map/ppermute | solution.py:28
  43.3 24.0 %collective-permute-start.10 = (bf16[4,192,512]{2,1,0:T(8,128)(2,1)S(1)}, bf16[4,192,512]{2,1,0:T(8,128)(2,1)S(1)}, u32[]{:S(2)}, u32[]{:S(2)}) collective-permute-start(bf16[4,192,512]{2,1,0:T(8,128)(2,1)S(1)} %bitcast_dynamic-update-slice_fusion), channel_id=1, source_target_pairs={{0,24},{1,25},{2,26},{3,27},{4,28},{5,29},{6,30},{7,31},{8,0},{9,1... | collective-permute-start | bytes 2359304 | tf_op jit(solution)/shard_map/ppermute | solution.py:28
  49.1 22.0 %collective-permute-start.7 = (bf16[4,192,512]{2,1,0:T(8,128)(2,1)S(1)}, bf16[4,192,512]{2,1,0:T(8,128)(2,1)S(1)}, u32[]{:S(2)}, u32[]{:S(2)}) collective-permute-start(bf16[4,192,512]{2,1,0:T(8,128)(2,1)S(1)} %bitcast_dynamic-update-slice_fusion), channel_id=1, source_target_pairs={{0,1},{1,0},{2,3},{3,2},{4,5},{5,4},{6,7},{7,6},{8,9},{9,8},{10,11... | collective-permute-start | bytes 2359304 | tf_op jit(solution)/shard_map/ppermute | solution.py:28
  49.3 24.5 %collective-permute-start.2 = (bf16[2,256,768]{2,1,0:T(8,128)(2,1)S(1)}, bf16[2,256,768]{2,1,0:T(8,128)(2,1)S(1)}, u32[]{:S(2)}, u32[]{:S(2)}) collective-permute-start(bf16[2,256,768]{2,1,0:T(8,128)(2,1)S(1)} %pad_maximum_fusion.1), channel_id=1, source_target_pairs={{0,128},{1,129},{2,130},{3,131},{4,132},{5,133},{6,134},{7,135},{8... | collective-permute-start | bytes 2359304 | tf_op jit(solution)/shard_map/ppermute | solution.py:28
  66.0 17.3 %collective-permute-start.9 = (bf16[4,192,512]{2,1,0:T(8,128)(2,1)S(1)}, bf16[4,192,512]{2,1,0:T(8,128)(2,1)}, u32[]{:S(2)}, u32[]{:S(2)}) collective-permute-start(bf16[4,192,512]{2,1,0:T(8,128)(2,1)S(1)} %collective-permute-done.8), channel_id=1, source_target_pairs={{0,1},{1,0},{2,3},{3,2},{4,5},{5,4},{6,7},{7,6},{8,9},{9,8},{10,11... | collective-permute-start | bytes 2359304 | tf_op jit(solution)/shard_map/ppermute | solution.py:28
  67.3 17.3 %collective-permute-start.11 = (bf16[4,192,512]{2,1,0:T(8,128)(2,1)S(1)}, bf16[4,192,512]{2,1,0:T(8,128)(2,1)}, u32[]{:S(2)}, u32[]{:S(2)}) collective-permute-start(bf16[4,192,512]{2,1,0:T(8,128)(2,1)S(1)} %collective-permute-done.10), channel_id=1, source_target_pairs={{0,1},{1,0},{2,3},{3,2},{4,5},{5,4},{6,7},{7,6},{8,9},{9,8},{10,11... | collective-permute-start | bytes 2359304 | tf_op jit(solution)/shard_map/ppermute | solution.py:28
  68.1 13.1 %collective-permute-start.12 = (bf16[2,192,512]{2,1,0:T(8,128)(2,1)}, bf16[2,192,512]{2,1,0:T(8,128)(2,1)}, u32[]{:S(2)}, u32[]{:S(2)}) collective-permute-start(bf16[2,192,512]{2,1,0:T(8,128)(2,1)} %slice_add_fusion.3), channel_id=1, source_target_pairs={{0,8},{1,9},{2,10},{3,11},{4,12},{5,13},{6,14},{7,15},{8,16},{9,17... | collective-permute-start | bytes 1179656 | tf_op jit(solution)/shard_map/ppermute | solution.py:28
  71.1 11.4 %collective-permute-start.14 = (bf16[2,192,512]{2,1,0:T(8,128)(2,1)S(1)}, bf16[2,192,512]{2,1,0:T(8,128)(2,1)}, u32[]{:S(2)}, u32[]{:S(2)}) collective-permute-start(bf16[2,192,512]{2,1,0:T(8,128)(2,1)S(1)} %slice.143), channel_id=1, source_target_pairs={{0,24},{1,25},{2,26},{3,27},{4,28},{5,29},{6,30},{7,31},{8,0},{9,1... | collective-permute-start | bytes 1179656 | tf_op jit(solution)/shard_map/ppermute | solution.py:28
  96.4 14.9 %collective-permute-start.16 = (bf16[512,512]{1,0:T(8,128)(2,1)S(1)}, bf16[512,512]{1,0:T(8,128)(2,1)S(1)}, u32[]{:S(2)}, u32[]{:S(2)}) collective-permute-start(bf16[512,512]{1,0:T(8,128)(2,1)S(1)} %fusion.7), channel_id=1, source_target_pairs={{0,128},{1,129},{2,130},{3,131},{4,132},{5,133},{6,134},{7,135},{8... | collective-permute-start | bytes 1572872 | tf_op jit(solution)/shard_map/ppermute | solution.py:28
  99.9 24.9 %collective-permute-start.17 = (bf16[256,512]{1,0:T(8,128)(2,1)S(1)}, bf16[256,512]{1,0:T(8,128)(2,1)S(1)}, u32[]{:S(2)}, u32[]{:S(2)}) collective-permute-start(bf16[256,512]{1,0:T(8,128)(2,1)S(1)} %get-tuple-element.22), channel_id=1, source_target_pairs={{0,128},{1,129},{2,130},{3,131},{4,132},{5,133},{6,134},{7,135},{8... | collective-permute-start | bytes 786440 | tf_op jit(solution)/shard_map/ppermute | solution.py:28
  100.5 24.4 %collective-permute-start.22 = (bf16[256,512]{1,0:T(8,128)(2,1)S(1)}, bf16[256,512]{1,0:T(8,128)(2,1)S(1)}, u32[]{:S(2)}, u32[]{:S(2)}) collective-permute-start(bf16[256,512]{1,0:T(8,128)(2,1)S(1)} %get-tuple-element.23), channel_id=1, source_target_pairs={{0,128},{1,129},{2,130},{3,131},{4,132},{5,133},{6,134},{7,135},{8... | collective-permute-start | bytes 786440 | tf_op jit(solution)/shard_map/ppermute | solution.py:28
  130.9 9.0 %collective-permute-start.23 = (bf16[256,512]{1,0:T(8,128)(2,1)S(1)}, bf16[256,512]{1,0:T(8,128)(2,1)S(1)}, u32[]{:S(2)}, u32[]{:S(2)}) collective-permute-start(bf16[256,512]{1,0:T(8,128)(2,1)S(1)} %bitcast.152), channel_id=1, source_target_pairs={{0,16},{1,17},{2,18},{3,19},{4,20},{5,21},{6,22},{7,23},{8,24},{9,... | collective-permute-start | bytes 786440 | tf_op jit(solution)/shard_map/ppermute | solution.py:28
  134.0 9.3 %collective-permute-start.24 = (bf16[256,512]{1,0:T(8,128)(2,1)S(1)}, bf16[256,512]{1,0:T(8,128)(2,1)S(1)}, u32[]{:S(2)}, u32[]{:S(2)}) collective-permute-start(bf16[256,512]{1,0:T(8,128)(2,1)S(1)} %bitcast.153), channel_id=1, source_target_pairs={{0,8},{1,9},{2,10},{3,11},{4,12},{5,13},{6,14},{7,15},{8,16},{9,17... | collective-permute-start | bytes 786440 | tf_op jit(solution)/shard_map/ppermute | solution.py:28
  134.5 9.0 %collective-permute-start.25 = (bf16[256,512]{1,0:T(8,128)(2,1)S(1)}, bf16[256,512]{1,0:T(8,128)(2,1)S(1)}, u32[]{:S(2)}, u32[]{:S(2)}) collective-permute-start(bf16[256,512]{1,0:T(8,128)(2,1)S(1)} %bitcast.154), channel_id=1, source_target_pairs={{0,24},{1,25},{2,26},{3,27},{4,28},{5,29},{6,30},{7,31},{8,0},{9,1... | collective-permute-start | bytes 786440 | tf_op jit(solution)/shard_map/ppermute | solution.py:28
  149.3 13.7 %collective-permute-start.27 = (bf16[192,512]{1,0:T(8,128)(2,1)S(1)}, bf16[192,512]{1,0:T(8,128)(2,1)S(1)}, u32[]{:S(2)}, u32[]{:S(2)}) collective-permute-start(bf16[192,512]{1,0:T(8,128)(2,1)S(1)} %get-tuple-element.19), channel_id=1, source_target_pairs={{0,4},{1,5},{2,6},{3,7},{4,0},{5,1},{6,2},{7,3},{8,12},{9,13},{10,... | collective-permute-start | bytes 589832 | tf_op jit(solution)/shard_map/ppermute | solution.py:28
  154.2 14.6 %collective-permute-start.28 = (bf16[192,512]{1,0:T(8,128)(2,1)S(1)}, bf16[192,512]{1,0:T(8,128)(2,1)S(1)}, u32[]{:S(2)}, u32[]{:S(2)}) collective-permute-start(bf16[192,512]{1,0:T(8,128)(2,1)S(1)} %get-tuple-element.21), channel_id=1, source_target_pairs={{0,2},{1,3},{2,4},{3,5},{4,6},{5,7},{6,0},{7,1},{8,10},{9,11},{10,... | collective-permute-start | bytes 589832 | tf_op jit(solution)/shard_map/ppermute | solution.py:28
  155.0 19.5 %collective-permute-start.29 = (bf16[192,512]{1,0:T(8,128)(2,1)S(1)}, bf16[192,512]{1,0:T(8,128)(2,1)S(1)}, u32[]{:S(2)}, u32[]{:S(2)}) collective-permute-start(bf16[192,512]{1,0:T(8,128)(2,1)S(1)} %get-tuple-element.20), channel_id=1, source_target_pairs={{0,6},{1,7},{2,0},{3,1},{4,2},{5,3},{6,4},{7,5},{8,14},{9,15},{10,... | collective-permute-start | bytes 589832 | tf_op jit(solution)/shard_map/ppermute | solution.py:28
  (21 other events, 197.0 us)
Sparse Core Ops, SparseCore 0:
  14.2 76.6 all-gather.4
  92.7 45.0 all-gather.2

commit v6 on v5

--- a/solution.py
+++ b/solution.py
@@ -120,7 +120,7 @@
     depth, across = moved.shape
     stacked = jnp.zeros((4, depth, across), BF)
     stacked = lax.dynamic_update_slice(stacked, moved[None], (zh, 0, 0))
-    for step in (2, 1, 3):
+    for step in (1, 3, 2):
         piece = send(moved, along_zh(step))
         stacked = lax.dynamic_update_slice(stacked, piece[None], ((zh + 4 - step) % 4, 0, 0))
     gathered = jnp.zeros((4, 4, 2, depth, across), BF)
@@ -203,9 +203,9 @@
 
     hidden_all = jnp.zeros((4 * span, rows), BF)
     hidden_all = lax.dynamic_update_slice(hidden_all, hidden, (slot(y), 0))
-    for step in (2, 1, 3):
+    for step in (1, 3, 2):
         piece = send(hidden, along_y(step))
-        if step == 2:
+        if step == 1:
             w_out_all = after(w_out_all, piece)
         hidden_all = lax.dynamic_update_slice(hidden_all, piece, (slot((y + 4 - step) % 4), 0))
 
@@ -220,7 +220,7 @@
     summed = kept + send(given, other_core).astype(F32)
     total = lax.dynamic_index_in_dim(summed, zh, 0, False)
     outgoing = summed.astype(BF)
-    for step in (2, 1, 3):
+    for step in (1, 3, 2):
         piece = lax.dynamic_index_in_dim(outgoing, (zh + step) % 4, 0, False)
         total += send(piece, along_zh(step)).astype(F32)
     return total.astype(BF).T

time: 185 us -> 183 us (0.989)
  waiting for transfers between devices: 62.4 us -> 60.3 us
    ppermute x30, waiting for transfers between devices: 62 us -> 59.1 us  [send(): return lax.ppermute(array, AXES, moves(target))]
  transfers between devices with their start and end apart: 32 -> 32, of which waited for: 17 -> 13; matrix products, arithmetic and copies ran while one was open for 20% -> 20% of each run, Pallas kernels for 0% -> 0%
where the time goes in v6:
time: 183 us; the launch traced here: 180 us
  waiting for transfers between devices  60.3 us (33%)
  starting transfers between devices  58.7 us (32%)
  other arithmetic  20.1 us (11%)
  between operations  17.5 us (10%)
  matrix products  12.9 us (7%)
  local copies, waits for them, and re-layouts  10.4 us (6%)
    ppermute x30, waiting for transfers between devices, send(): return lax.ppermute(array, AXES, moves(target))  59.1 us
    ppermute x30, starting transfers between devices, send(): return lax.ppermute(array, AXES, moves(target))  58.6 us
    dot_general x7, matrix products, columns_first(): lax.dot_general(weights, rows_last, (((0,), (0,)), ((), ())), preferred_e...  9.46 us
    add x4, other arithmetic, after(): return array + other[(0,) * other.ndim] * jnp.zeros((), array.dtype)  7.49 us
    dynamic_update_slice x5, other arithmetic, local(): lax.dynamic_update_slice(gathered, both[None], (place, start, 0, 0, 0))  4.97 us
  transfers between devices with their start and end apart: 32, of which 13 were waited for; matrix products, arithmetic and copies ran while one was open for 20% of the time, Pallas kernels for 0%

profile of v6, /device:TPU:4, one launch (start us, length us, event | category | flops | bytes accessed | tf_op | source)
XLA Modules:
  0.0 179.8 jit_solution(13873201226014119129)
XLA Ops:
  8.1 2.8 %reshape.162 = bf16[2,2,192,1024]{3,2,1,0:T(8,128)(2,1)S(1)} reshape(bf16[768,2,512]{2,1,0:T(2,128)(2,1)} %param.6) | data formatting | bytes 3145728 | tf_op jit(solution)/shard_map/reshape | solution.py:109
  14.1 3.4 %collective-permute-start = (bf16[256,768]{1,0:T(8,128)(2,1)}, bf16[256,768]{1,0:T(8,128)(2,1)S(1)}, u32[]{:S(2)}, u32[]{:S(2)}) collective-permute-start(bf16[256,768]{1,0:T(8,128)(2,1)} %bitcast), channel_id=1, source_target_pairs={{0,0},{1,1},{2,2},{3,3},{4,4},{5,5},{6,6},{7,7},{8,64},{9,65},{10,... | collective-permute-start | bytes 1179656 | tf_op jit(solution)/shard_map/ppermute | solution.py:28
  19.0 3.3 %collective-permute-start.4 = (bf16[192,512]{1,0:T(8,128)(2,1)S(1)}, bf16[192,512]{1,0:T(8,128)(2,1)S(1)}, u32[]{:S(2)}, u32[]{:S(2)}) collective-permute-start(bf16[192,512]{1,0:T(8,128)(2,1)S(1)} %collective-permute-done.3), channel_id=1, source_target_pairs={{0,2},{1,3},{2,4},{3,5},{4,6},{5,7},{6,0},{7,1},{8,10},{9,11},{10,... | collective-permute-start | bytes 589832 | tf_op jit(solution)/shard_map/ppermute | solution.py:28
  22.4 3.1 %collective-permute-start.5 = (bf16[192,512]{1,0:T(8,128)(2,1)S(1)}, bf16[192,512]{1,0:T(8,128)(2,1)S(1)}, u32[]{:S(2)}, u32[]{:S(2)}) collective-permute-start(bf16[192,512]{1,0:T(8,128)(2,1)S(1)} %collective-permute-done.3), channel_id=1, source_target_pairs={{0,6},{1,7},{2,0},{3,1},{4,2},{5,3},{6,4},{7,5},{8,14},{9,15},{10,... | collective-permute-start | bytes 589832 | tf_op jit(solution)/shard_map/ppermute | solution.py:28
  25.5 4.9 %collective-permute-start.6 = (bf16[192,512]{1,0:T(8,128)(2,1)S(1)}, bf16[192,512]{1,0:T(8,128)(2,1)S(1)}, u32[]{:S(2)}, u32[]{:S(2)}) collective-permute-start(bf16[192,512]{1,0:T(8,128)(2,1)S(1)} %collective-permute-done.3), channel_id=1, source_target_pairs={{0,4},{1,5},{2,6},{3,7},{4,0},{5,1},{6,2},{7,3},{8,12},{9,13},{10,... | collective-permute-start | bytes 589832 | tf_op jit(solution)/shard_map/ppermute | solution.py:28
  31.3 9.5 %collective-permute-done.6 = bf16[192,512]{1,0:T(8,128)(2,1)S(1)} collective-permute-done((bf16[192,512]{1,0:T(8,128)(2,1)S(1)}, bf16[192,512]{1,0:T(8,128)(2,1)S(1)}, u32[]{:S(2)}, u32[]{:S(2)}) %collective-permute-start.6) | collective-permute-done | bytes 196640 | tf_op jit(solution)/shard_map/ppermute | solution.py:28
  40.9 7.9 %collective-permute-start.10 = (bf16[4,192,512]{2,1,0:T(8,128)(2,1)S(1)}, bf16[4,192,512]{2,1,0:T(8,128)(2,1)S(1)}, u32[]{:S(2)}, u32[]{:S(2)}) collective-permute-start(bf16[4,192,512]{2,1,0:T(8,128)(2,1)S(1)} %bitcast_dynamic-update-slice_fusion), channel_id=1, source_target_pairs={{0,24},{1,25},{2,26},{3,27},{4,28},{5,29},{6,30},{7,31},{8,0},{9,1... | collective-permute-start | bytes 2359304 | tf_op jit(solution)/shard_map/ppermute | solution.py:28
  49.1 5.5 %collective-permute-start.2 = (bf16[2,256,768]{2,1,0:T(8,128)(2,1)S(1)}, bf16[2,256,768]{2,1,0:T(8,128)(2,1)S(1)}, u32[]{:S(2)}, u32[]{:S(2)}) collective-permute-start(bf16[2,256,768]{2,1,0:T(8,128)(2,1)S(1)} %pad_maximum_fusion.1), channel_id=1, source_target_pairs={{0,128},{1,129},{2,130},{3,131},{4,132},{5,133},{6,134},{7,135},{8... | collective-permute-start | bytes 2359304 | tf_op jit(solution)/shard_map/ppermute | solution.py:28
  56.5 10.0 %collective-permute-done.8 = bf16[4,192,512]{2,1,0:T(8,128)(2,1)S(1)} collective-permute-done((bf16[4,192,512]{2,1,0:T(8,128)(2,1)S(1)}, bf16[4,192,512]{2,1,0:T(8,128)(2,1)S(1)}, u32[]{:S(2)}, u32[]{:S(2)}) %collective-permute-start.8) | collective-permute-done | bytes 786464 | tf_op jit(solution)/shard_map/ppermute | solution.py:28
  69.7 2.7 %collective-permute-start.14 = (bf16[2,192,512]{2,1,0:T(8,128)(2,1)S(1)}, bf16[2,192,512]{2,1,0:T(8,128)(2,1)}, u32[]{:S(2)}, u32[]{:S(2)}) collective-permute-start(bf16[2,192,512]{2,1,0:T(8,128)(2,1)S(1)} %slice.143), channel_id=1, source_target_pairs={{0,24},{1,25},{2,26},{3,27},{4,28},{5,29},{6,30},{7,31},{8,0},{9,1... | collective-permute-start | bytes 1179656 | tf_op jit(solution)/shard_map/ppermute | solution.py:28
  74.5 5.9 %collective-permute-done.12 = bf16[2,192,512]{2,1,0:T(8,128)(2,1)} collective-permute-done((bf16[2,192,512]{2,1,0:T(8,128)(2,1)}, bf16[2,192,512]{2,1,0:T(8,128)(2,1)}, u32[]{:S(2)}, u32[]{:S(2)}) %collective-permute-start.12) | collective-permute-done | bytes 393248 | tf_op jit(solution)/shard_map/ppermute | solution.py:28
  90.9 3.3 %broadcast_add_fusion = bf16[3072,1024]{1,0:T(8,128)(2,1)S(1)} fusion(bf16[3072,1024]{1,0:T(8,128)(2,1)} %all-gather.5.cloned.1.call-done, bf16[]{:T(256)} %bitcast.10), kind=kLoop, calls=%fused_computation.5 | loop fusion | flops 3145728 | bytes 12582914 | tf_op jit(solution)/shard_map/add | solution.py:87
  102.0 3.4 %fusion.67 = f32[1024,512]{1,0:T(8,128)S(1)} fusion(bf16[3072,1024]{1,0:T(8,128)(2,1)S(1)} %broadcast_add_fusion, bf16[3072,512]{1,0:T(8,128)(2,1)S(1)} %bitcast.136), kind=kOutput, calls=%fused_computation.130 | convolution fusion | flops 3221225472 | bytes 11534336 | tf_op jit(solution)/shard_map/dot_general | solution.py:140
  105.5 5.8 %collective-permute-done.16 = bf16[512,512]{1,0:T(8,128)(2,1)S(1)} collective-permute-done((bf16[512,512]{1,0:T(8,128)(2,1)S(1)}, bf16[512,512]{1,0:T(8,128)(2,1)S(1)}, u32[]{:S(2)}, u32[]{:S(2)}) %collective-permute-start.16) | collective-permute-done | bytes 524320 | tf_op jit(solution)/shard_map/ppermute | solution.py:28
  113.1 2.4 %collective-permute-start.19 = (bf16[2,128,128]{2,1,0:T(8,128)(2,1)S(1)}, bf16[2,128,128]{2,1,0:T(8,128)(2,1)S(1)}, u32[]{:S(2)}, u32[]{:S(2)}) collective-permute-start(bf16[2,128,128]{2,1,0:T(8,128)(2,1)S(1)} %convolution_convert_fusion), channel_id=1, source_target_pairs={{0,32},{1,33},{2,34},{3,35},{4,36},{5,37},{6,38},{7,39},{8,40},{9,... | collective-permute-start | bytes 196616 | tf_op jit(solution)/shard_map/ppermute | solution.py:28
  119.5 2.5 %collective-permute-done.20 = bf16[2,128,128]{2,1,0:T(8,128)(2,1)S(1)} collective-permute-done((bf16[2,128,128]{2,1,0:T(8,128)(2,1)S(1)}, bf16[2,128,128]{2,1,0:T(8,128)(2,1)S(1)}, u32[]{:S(2)}, u32[]{:S(2)}) %collective-permute-start.20) | collective-permute-done | bytes 65568 | tf_op jit(solution)/shard_map/ppermute | solution.py:28
  122.2 4.0 %collective-permute-start.21 = (bf16[2,128,128]{2,1,0:T(8,128)(2,1)S(1)}, bf16[2,128,128]{2,1,0:T(8,128)(2,1)S(1)}, u32[]{:S(2)}, u32[]{:S(2)}) collective-permute-start(bf16[2,128,128]{2,1,0:T(8,128)(2,1)S(1)} %fusion.50), channel_id=1, source_target_pairs={{0,128},{1,129},{2,130},{3,131},{4,132},{5,133},{6,134},{7,135},{8... | collective-permute-start | bytes 196616 | tf_op jit(solution)/shard_map/ppermute | solution.py:28
  128.2 2.8 %multiply_reduce_fusion = (f32[2,512]{1,0:T(2,128)S(1)}, f32[2,128,512]{2,1,0:T(8,128)}) fusion(f32[2,128,512]{2,1,0:T(8,128)S(1)} %convolution_multiply_fusion, bf16[2,128,512]{2,1,0:T(8,128)(2,1)S(1)} %bitcast.151, f32[512,512]{1,0:T(8,128)S(1)} %copy-done.1, f32[2]{0:T(128)S(1)} %get-tuple-element.8, pred[512,512]{1,0:T(8,128)(4,1)} %fusion.22, ...), kind=kOutput, calls=%fused_computation.57 | convolution fusion | flops 270924800 | bytes 3412480 | tf_op jit(solution)/shard_map/hts,hes->het/dot_general | solution.py:188
  132.9 2.6 %collective-permute-start.24 = (bf16[256,512]{1,0:T(8,128)(2,1)S(1)}, bf16[256,512]{1,0:T(8,128)(2,1)S(1)}, u32[]{:S(2)}, u32[]{:S(2)}) collective-permute-start(bf16[256,512]{1,0:T(8,128)(2,1)S(1)} %bitcast.153), channel_id=1, source_target_pairs={{0,24},{1,25},{2,26},{3,27},{4,28},{5,29},{6,30},{7,31},{8,0},{9,1... | collective-permute-start | bytes 786440 | tf_op jit(solution)/shard_map/ppermute | solution.py:28
  136.6 6.0 %collective-permute-done.23 = bf16[256,512]{1,0:T(8,128)(2,1)S(1)} collective-permute-done((bf16[256,512]{1,0:T(8,128)(2,1)S(1)}, bf16[256,512]{1,0:T(8,128)(2,1)S(1)}, u32[]{:S(2)}, u32[]{:S(2)}) %collective-permute-start.23) | collective-permute-done | bytes 262176 | tf_op jit(solution)/shard_map/ppermute | solution.py:28
  152.5 3.8 %collective-permute-start.28 = (bf16[192,512]{1,0:T(8,128)(2,1)S(1)}, bf16[192,512]{1,0:T(8,128)(2,1)S(1)}, u32[]{:S(2)}, u32[]{:S(2)}) collective-permute-start(bf16[192,512]{1,0:T(8,128)(2,1)S(1)} %get-tuple-element.21), channel_id=1, source_target_pairs={{0,6},{1,7},{2,0},{3,1},{4,2},{5,3},{6,4},{7,5},{8,14},{9,15},{10,... | collective-permute-start | bytes 589832 | tf_op jit(solution)/shard_map/ppermute | solution.py:28
  156.3 2.6 %collective-permute-start.29 = (bf16[192,512]{1,0:T(8,128)(2,1)S(1)}, bf16[192,512]{1,0:T(8,128)(2,1)S(1)}, u32[]{:S(2)}, u32[]{:S(2)}) collective-permute-start(bf16[192,512]{1,0:T(8,128)(2,1)S(1)} %get-tuple-element.20), channel_id=1, source_target_pairs={{0,4},{1,5},{2,6},{3,7},{4,0},{5,1},{6,2},{7,3},{8,12},{9,13},{10,... | collective-permute-start | bytes 589832 | tf_op jit(solution)/shard_map/ppermute | solution.py:28
  158.9 9.4 %collective-permute-done.27 = bf16[192,512]{1,0:T(8,128)(2,1)S(1)} collective-permute-done((bf16[192,512]{1,0:T(8,128)(2,1)S(1)}, bf16[192,512]{1,0:T(8,128)(2,1)S(1)}, u32[]{:S(2)}, u32[]{:S(2)}) %collective-permute-start.27) | collective-permute-done | bytes 196640 | tf_op jit(solution)/shard_map/ppermute | solution.py:28
  168.3 3.8 %collective-permute-done.29 = bf16[192,512]{1,0:T(8,128)(2,1)S(1)} collective-permute-done((bf16[192,512]{1,0:T(8,128)(2,1)S(1)}, bf16[192,512]{1,0:T(8,128)(2,1)S(1)}, u32[]{:S(2)}, u32[]{:S(2)}) %collective-permute-start.29) | collective-permute-done | bytes 196640 | tf_op jit(solution)/shard_map/ppermute | solution.py:28
  (133 shorter events, 50.5 us)
Async XLA Ops:
  6.5 84.3 %all-gather.5.cloned.1.call-start = ((), (), s32[]{:S(2)}) async-start(), calls=%async_computation.1 | async-start | bytes 7864320 | tf_op jit(solution)/shard_map/all_gather | solution.py:118
  14.1 129.8 %all-gather.3.cloned.1.call-start = ((), (), s32[]{:S(2)}) async-start(), calls=%async_computation | async-start | bytes 3932160 | tf_op jit(solution)/shard_map/all_gather | solution.py:136
  14.1 34.8 %collective-permute-start = (bf16[256,768]{1,0:T(8,128)(2,1)}, bf16[256,768]{1,0:T(8,128)(2,1)S(1)}, u32[]{:S(2)}, u32[]{:S(2)}) collective-permute-start(bf16[256,768]{1,0:T(8,128)(2,1)} %bitcast), channel_id=1, source_target_pairs={{0,0},{1,1},{2,2},{3,3},{4,4},{5,5},{6,6},{7,7},{8,64},{9,65},{10,... | collective-permute-start | bytes 1179656 | tf_op jit(solution)/shard_map/ppermute | solution.py:28
  17.6 31.4 %collective-permute-start.1 = (bf16[256,768]{1,0:T(8,128)(2,1)}, bf16[256,768]{1,0:T(8,128)(2,1)S(1)}, u32[]{:S(2)}, u32[]{:S(2)}) collective-permute-start(bf16[256,768]{1,0:T(8,128)(2,1)} %bitcast), channel_id=1, source_target_pairs={{16,0},{17,1},{18,2},{19,3},{20,4},{21,5},{22,6},{23,7},{24,64},{2... | collective-permute-start | bytes 1179656 | tf_op jit(solution)/shard_map/ppermute | solution.py:28
  19.0 11.5 %collective-permute-start.4 = (bf16[192,512]{1,0:T(8,128)(2,1)S(1)}, bf16[192,512]{1,0:T(8,128)(2,1)S(1)}, u32[]{:S(2)}, u32[]{:S(2)}) collective-permute-start(bf16[192,512]{1,0:T(8,128)(2,1)S(1)} %collective-permute-done.3), channel_id=1, source_target_pairs={{0,2},{1,3},{2,4},{3,5},{4,6},{5,7},{6,0},{7,1},{8,10},{9,11},{10,... | collective-permute-start | bytes 589832 | tf_op jit(solution)/shard_map/ppermute | solution.py:28
  22.4 8.9 %collective-permute-start.5 = (bf16[192,512]{1,0:T(8,128)(2,1)S(1)}, bf16[192,512]{1,0:T(8,128)(2,1)S(1)}, u32[]{:S(2)}, u32[]{:S(2)}) collective-permute-start(bf16[192,512]{1,0:T(8,128)(2,1)S(1)} %collective-permute-done.3), channel_id=1, source_target_pairs={{0,6},{1,7},{2,0},{3,1},{4,2},{5,3},{6,4},{7,5},{8,14},{9,15},{10,... | collective-permute-start | bytes 589832 | tf_op jit(solution)/shard_map/ppermute | solution.py:28
  25.5 15.3 %collective-permute-start.6 = (bf16[192,512]{1,0:T(8,128)(2,1)S(1)}, bf16[192,512]{1,0:T(8,128)(2,1)S(1)}, u32[]{:S(2)}, u32[]{:S(2)}) collective-permute-start(bf16[192,512]{1,0:T(8,128)(2,1)S(1)} %collective-permute-done.3), channel_id=1, source_target_pairs={{0,4},{1,5},{2,6},{3,7},{4,0},{5,1},{6,2},{7,3},{8,12},{9,13},{10,... | collective-permute-start | bytes 589832 | tf_op jit(solution)/shard_map/ppermute | solution.py:28
  40.8 25.7 %collective-permute-start.8 = (bf16[4,192,512]{2,1,0:T(8,128)(2,1)S(1)}, bf16[4,192,512]{2,1,0:T(8,128)(2,1)S(1)}, u32[]{:S(2)}, u32[]{:S(2)}) collective-permute-start(bf16[4,192,512]{2,1,0:T(8,128)(2,1)S(1)} %bitcast_dynamic-update-slice_fusion), channel_id=1, source_target_pairs={{0,8},{1,9},{2,10},{3,11},{4,12},{5,13},{6,14},{7,15},{8,16},{9,17... | collective-permute-start | bytes 2359304 | tf_op jit(solution)/shard_map/ppermute | solution.py:28
  40.9 25.6 %collective-permute-start.10 = (bf16[4,192,512]{2,1,0:T(8,128)(2,1)S(1)}, bf16[4,192,512]{2,1,0:T(8,128)(2,1)S(1)}, u32[]{:S(2)}, u32[]{:S(2)}) collective-permute-start(bf16[4,192,512]{2,1,0:T(8,128)(2,1)S(1)} %bitcast_dynamic-update-slice_fusion), channel_id=1, source_target_pairs={{0,24},{1,25},{2,26},{3,27},{4,28},{5,29},{6,30},{7,31},{8,0},{9,1... | collective-permute-start | bytes 2359304 | tf_op jit(solution)/shard_map/ppermute | solution.py:28
  48.9 20.8 %collective-permute-start.7 = (bf16[4,192,512]{2,1,0:T(8,128)(2,1)S(1)}, bf16[4,192,512]{2,1,0:T(8,128)(2,1)S(1)}, u32[]{:S(2)}, u32[]{:S(2)}) collective-permute-start(bf16[4,192,512]{2,1,0:T(8,128)(2,1)S(1)} %bitcast_dynamic-update-slice_fusion), channel_id=1, source_target_pairs={{0,1},{1,0},{2,3},{3,2},{4,5},{5,4},{6,7},{7,6},{8,9},{9,8},{10,11... | collective-permute-start | bytes 2359304 | tf_op jit(solution)/shard_map/ppermute | solution.py:28
  49.1 24.4 %collective-permute-start.2 = (bf16[2,256,768]{2,1,0:T(8,128)(2,1)S(1)}, bf16[2,256,768]{2,1,0:T(8,128)(2,1)S(1)}, u32[]{:S(2)}, u32[]{:S(2)}) collective-permute-start(bf16[2,256,768]{2,1,0:T(8,128)(2,1)S(1)} %pad_maximum_fusion.1), channel_id=1, source_target_pairs={{0,128},{1,129},{2,130},{3,131},{4,132},{5,133},{6,134},{7,135},{8... | collective-permute-start | bytes 2359304 | tf_op jit(solution)/shard_map/ppermute | solution.py:28
  66.5 16.0 %collective-permute-start.9 = (bf16[4,192,512]{2,1,0:T(8,128)(2,1)S(1)}, bf16[4,192,512]{2,1,0:T(8,128)(2,1)}, u32[]{:S(2)}, u32[]{:S(2)}) collective-permute-start(bf16[4,192,512]{2,1,0:T(8,128)(2,1)S(1)} %collective-permute-done.8), channel_id=1, source_target_pairs={{0,1},{1,0},{2,3},{3,2},{4,5},{5,4},{6,7},{7,6},{8,9},{9,8},{10,11... | collective-permute-start | bytes 2359304 | tf_op jit(solution)/shard_map/ppermute | solution.py:28
  66.5 17.4 %collective-permute-start.11 = (bf16[4,192,512]{2,1,0:T(8,128)(2,1)S(1)}, bf16[4,192,512]{2,1,0:T(8,128)(2,1)}, u32[]{:S(2)}, u32[]{:S(2)}) collective-permute-start(bf16[4,192,512]{2,1,0:T(8,128)(2,1)S(1)} %collective-permute-done.10), channel_id=1, source_target_pairs={{0,1},{1,0},{2,3},{3,2},{4,5},{5,4},{6,7},{7,6},{8,9},{9,8},{10,11... | collective-permute-start | bytes 2359304 | tf_op jit(solution)/shard_map/ppermute | solution.py:28
  67.8 12.6 %collective-permute-start.12 = (bf16[2,192,512]{2,1,0:T(8,128)(2,1)}, bf16[2,192,512]{2,1,0:T(8,128)(2,1)}, u32[]{:S(2)}, u32[]{:S(2)}) collective-permute-start(bf16[2,192,512]{2,1,0:T(8,128)(2,1)} %slice_add_fusion.3), channel_id=1, source_target_pairs={{0,8},{1,9},{2,10},{3,11},{4,12},{5,13},{6,14},{7,15},{8,16},{9,17... | collective-permute-start | bytes 1179656 | tf_op jit(solution)/shard_map/ppermute | solution.py:28
  69.7 12.1 %collective-permute-start.14 = (bf16[2,192,512]{2,1,0:T(8,128)(2,1)S(1)}, bf16[2,192,512]{2,1,0:T(8,128)(2,1)}, u32[]{:S(2)}, u32[]{:S(2)}) collective-permute-start(bf16[2,192,512]{2,1,0:T(8,128)(2,1)S(1)} %slice.143), channel_id=1, source_target_pairs={{0,24},{1,25},{2,26},{3,27},{4,28},{5,29},{6,30},{7,31},{8,0},{9,1... | collective-permute-start | bytes 1179656 | tf_op jit(solution)/shard_map/ppermute | solution.py:28
  96.4 14.9 %collective-permute-start.16 = (bf16[512,512]{1,0:T(8,128)(2,1)S(1)}, bf16[512,512]{1,0:T(8,128)(2,1)S(1)}, u32[]{:S(2)}, u32[]{:S(2)}) collective-permute-start(bf16[512,512]{1,0:T(8,128)(2,1)S(1)} %fusion.7), channel_id=1, source_target_pairs={{0,128},{1,129},{2,130},{3,131},{4,132},{5,133},{6,134},{7,135},{8... | collective-permute-start | bytes 1572872 | tf_op jit(solution)/shard_map/ppermute | solution.py:28
  99.9 26.3 %collective-permute-start.17 = (bf16[256,512]{1,0:T(8,128)(2,1)S(1)}, bf16[256,512]{1,0:T(8,128)(2,1)S(1)}, u32[]{:S(2)}, u32[]{:S(2)}) collective-permute-start(bf16[256,512]{1,0:T(8,128)(2,1)S(1)} %get-tuple-element.22), channel_id=1, source_target_pairs={{0,128},{1,129},{2,130},{3,131},{4,132},{5,133},{6,134},{7,135},{8... | collective-permute-start | bytes 786440 | tf_op jit(solution)/shard_map/ppermute | solution.py:28
  100.5 25.7 %collective-permute-start.22 = (bf16[256,512]{1,0:T(8,128)(2,1)S(1)}, bf16[256,512]{1,0:T(8,128)(2,1)S(1)}, u32[]{:S(2)}, u32[]{:S(2)}) collective-permute-start(bf16[256,512]{1,0:T(8,128)(2,1)S(1)} %get-tuple-element.23), channel_id=1, source_target_pairs={{0,128},{1,129},{2,130},{3,131},{4,132},{5,133},{6,134},{7,135},{8... | collective-permute-start | bytes 786440 | tf_op jit(solution)/shard_map/ppermute | solution.py:28
  132.2 10.5 %collective-permute-start.23 = (bf16[256,512]{1,0:T(8,128)(2,1)S(1)}, bf16[256,512]{1,0:T(8,128)(2,1)S(1)}, u32[]{:S(2)}, u32[]{:S(2)}) collective-permute-start(bf16[256,512]{1,0:T(8,128)(2,1)S(1)} %bitcast.152), channel_id=1, source_target_pairs={{0,8},{1,9},{2,10},{3,11},{4,12},{5,13},{6,14},{7,15},{8,16},{9,17... | collective-permute-start | bytes 786440 | tf_op jit(solution)/shard_map/ppermute | solution.py:28
  132.9 13.1 %collective-permute-start.24 = (bf16[256,512]{1,0:T(8,128)(2,1)S(1)}, bf16[256,512]{1,0:T(8,128)(2,1)S(1)}, u32[]{:S(2)}, u32[]{:S(2)}) collective-permute-start(bf16[256,512]{1,0:T(8,128)(2,1)S(1)} %bitcast.153), channel_id=1, source_target_pairs={{0,24},{1,25},{2,26},{3,27},{4,28},{5,29},{6,30},{7,31},{8,0},{9,1... | collective-permute-start | bytes 786440 | tf_op jit(solution)/shard_map/ppermute | solution.py:28
  135.5 10.7 %collective-permute-start.25 = (bf16[256,512]{1,0:T(8,128)(2,1)S(1)}, bf16[256,512]{1,0:T(8,128)(2,1)S(1)}, u32[]{:S(2)}, u32[]{:S(2)}) collective-permute-start(bf16[256,512]{1,0:T(8,128)(2,1)S(1)} %bitcast.154), channel_id=1, source_target_pairs={{0,16},{1,17},{2,18},{3,19},{4,20},{5,21},{6,22},{7,23},{8,24},{9,... | collective-permute-start | bytes 786440 | tf_op jit(solution)/shard_map/ppermute | solution.py:28
  152.1 16.3 %collective-permute-start.27 = (bf16[192,512]{1,0:T(8,128)(2,1)S(1)}, bf16[192,512]{1,0:T(8,128)(2,1)S(1)}, u32[]{:S(2)}, u32[]{:S(2)}) collective-permute-start(bf16[192,512]{1,0:T(8,128)(2,1)S(1)} %get-tuple-element.19), channel_id=1, source_target_pairs={{0,2},{1,3},{2,4},{3,5},{4,6},{5,7},{6,0},{7,1},{8,10},{9,11},{10,... | collective-permute-start | bytes 589832 | tf_op jit(solution)/shard_map/ppermute | solution.py:28
  152.5 15.8 %collective-permute-start.28 = (bf16[192,512]{1,0:T(8,128)(2,1)S(1)}, bf16[192,512]{1,0:T(8,128)(2,1)S(1)}, u32[]{:S(2)}, u32[]{:S(2)}) collective-permute-start(bf16[192,512]{1,0:T(8,128)(2,1)S(1)} %get-tuple-element.21), channel_id=1, source_target_pairs={{0,6},{1,7},{2,0},{3,1},{4,2},{5,3},{6,4},{7,5},{8,14},{9,15},{10,... | collective-permute-start | bytes 589832 | tf_op jit(solution)/shard_map/ppermute | solution.py:28
  156.3 15.9 %collective-permute-start.29 = (bf16[192,512]{1,0:T(8,128)(2,1)S(1)}, bf16[192,512]{1,0:T(8,128)(2,1)S(1)}, u32[]{:S(2)}, u32[]{:S(2)}) collective-permute-start(bf16[192,512]{1,0:T(8,128)(2,1)S(1)} %get-tuple-element.20), channel_id=1, source_target_pairs={{0,4},{1,5},{2,6},{3,7},{4,0},{5,1},{6,2},{7,3},{8,12},{9,13},{10,... | collective-permute-start | bytes 589832 | tf_op jit(solution)/shard_map/ppermute | solution.py:28
  (21 other events, 204.7 us)
Sparse Core Ops, SparseCore 0:
  14.2 76.6 all-gather.4
  92.7 45.0 all-gather.2

commit v7 on v6

--- a/solution.py
+++ b/solution.py
@@ -102,9 +102,6 @@
     zh = lax.axis_index("zh")
     y = lax.axis_index("y")
 
-    w_out_block = w_out.reshape(heads * size, -1)
-    w_out_moved = jnp.stack([send(w_out_block, w_out_to_columns(high)) for high in range(2)])
-
     moved = send(tokens.T, tokens_to_half)
     w_block = w_qkvg.reshape(2, 2, tokens.shape[1], -1)
     kv_cuts = [(4 * h + 1, 4 * h + 3) for h in range(heads)]
@@ -123,6 +120,9 @@
     for step in (1, 3, 2):
         piece = send(moved, along_zh(step))
         stacked = lax.dynamic_update_slice(stacked, piece[None], ((zh + 4 - step) % 4, 0, 0))
+    w_out_block = w_out.reshape(heads * size, -1)
+    w_out_moved = jnp.stack([send(w_out_block, w_out_to_columns(high)) for high in range(2)])
+
     gathered = jnp.zeros((4, 4, 2, depth, across), BF)
     swapped = []
     for piece, start, place in gather_ring(stacked, "y", along_y, 2, w_out_moved):

time: 183 us -> 183 us (level)
  no operation moved by 1% of the time
where the time goes in v7:
time: 183 us; the launch traced here: 180 us
  waiting for transfers between devices  60.3 us (33%)
  starting transfers between devices  58.7 us (32%)
  other arithmetic  20.1 us (11%)
  between operations  17.5 us (10%)
  matrix products  12.9 us (7%)
  local copies, waits for them, and re-layouts  10.4 us (6%)
    ppermute x30, waiting for transfers between devices, send(): return lax.ppermute(array, AXES, moves(target))  59.1 us
    ppermute x30, starting transfers between devices, send(): return lax.ppermute(array, AXES, moves(target))  58.6 us
    dot_general x7, matrix products, columns_first(): lax.dot_general(weights, rows_last, (((0,), (0,)), ((), ())), preferred_e...  9.46 us
    add x4, other arithmetic, after(): return array + other[(0,) * other.ndim] * jnp.zeros((), array.dtype)  7.49 us
    dynamic_update_slice x5, other arithmetic, local(): lax.dynamic_update_slice(gathered, both[None], (place, start, 0, 0, 0))  4.97 us
  transfers between devices with their start and end apart: 32, of which 13 were waited for; matrix products, arithmetic and copies ran while one was open for 20% of the time, Pallas kernels for 0%

profile of v7, /device:TPU:4, one launch (start us, length us, event | category | flops | bytes accessed | tf_op | source)
XLA Modules:
  0.0 179.8 jit_solution(13873201226014119129)
XLA Ops:
  8.1 2.8 %reshape.162 = bf16[2,2,192,1024]{3,2,1,0:T(8,128)(2,1)S(1)} reshape(bf16[768,2,512]{2,1,0:T(2,128)(2,1)} %param.6) | data formatting | bytes 3145728 | tf_op jit(solution)/shard_map/reshape | solution.py:106
  14.1 3.4 %collective-permute-start = (bf16[256,768]{1,0:T(8,128)(2,1)}, bf16[256,768]{1,0:T(8,128)(2,1)S(1)}, u32[]{:S(2)}, u32[]{:S(2)}) collective-permute-start(bf16[256,768]{1,0:T(8,128)(2,1)} %bitcast), channel_id=1, source_target_pairs={{0,0},{1,1},{2,2},{3,3},{4,4},{5,5},{6,6},{7,7},{8,64},{9,65},{10,... | collective-permute-start | bytes 1179656 | tf_op jit(solution)/shard_map/ppermute | solution.py:28
  19.0 3.3 %collective-permute-start.4 = (bf16[192,512]{1,0:T(8,128)(2,1)S(1)}, bf16[192,512]{1,0:T(8,128)(2,1)S(1)}, u32[]{:S(2)}, u32[]{:S(2)}) collective-permute-start(bf16[192,512]{1,0:T(8,128)(2,1)S(1)} %collective-permute-done.3), channel_id=1, source_target_pairs={{0,2},{1,3},{2,4},{3,5},{4,6},{5,7},{6,0},{7,1},{8,10},{9,11},{10,... | collective-permute-start | bytes 589832 | tf_op jit(solution)/shard_map/ppermute | solution.py:28
  22.4 3.1 %collective-permute-start.5 = (bf16[192,512]{1,0:T(8,128)(2,1)S(1)}, bf16[192,512]{1,0:T(8,128)(2,1)S(1)}, u32[]{:S(2)}, u32[]{:S(2)}) collective-permute-start(bf16[192,512]{1,0:T(8,128)(2,1)S(1)} %collective-permute-done.3), channel_id=1, source_target_pairs={{0,6},{1,7},{2,0},{3,1},{4,2},{5,3},{6,4},{7,5},{8,14},{9,15},{10,... | collective-permute-start | bytes 589832 | tf_op jit(solution)/shard_map/ppermute | solution.py:28
  25.5 4.9 %collective-permute-start.6 = (bf16[192,512]{1,0:T(8,128)(2,1)S(1)}, bf16[192,512]{1,0:T(8,128)(2,1)S(1)}, u32[]{:S(2)}, u32[]{:S(2)}) collective-permute-start(bf16[192,512]{1,0:T(8,128)(2,1)S(1)} %collective-permute-done.3), channel_id=1, source_target_pairs={{0,4},{1,5},{2,6},{3,7},{4,0},{5,1},{6,2},{7,3},{8,12},{9,13},{10,... | collective-permute-start | bytes 589832 | tf_op jit(solution)/shard_map/ppermute | solution.py:28
  31.3 9.5 %collective-permute-done.6 = bf16[192,512]{1,0:T(8,128)(2,1)S(1)} collective-permute-done((bf16[192,512]{1,0:T(8,128)(2,1)S(1)}, bf16[192,512]{1,0:T(8,128)(2,1)S(1)}, u32[]{:S(2)}, u32[]{:S(2)}) %collective-permute-start.6) | collective-permute-done | bytes 196640 | tf_op jit(solution)/shard_map/ppermute | solution.py:28
  40.9 7.9 %collective-permute-start.10 = (bf16[4,192,512]{2,1,0:T(8,128)(2,1)S(1)}, bf16[4,192,512]{2,1,0:T(8,128)(2,1)S(1)}, u32[]{:S(2)}, u32[]{:S(2)}) collective-permute-start(bf16[4,192,512]{2,1,0:T(8,128)(2,1)S(1)} %bitcast_dynamic-update-slice_fusion), channel_id=1, source_target_pairs={{0,24},{1,25},{2,26},{3,27},{4,28},{5,29},{6,30},{7,31},{8,0},{9,1... | collective-permute-start | bytes 2359304 | tf_op jit(solution)/shard_map/ppermute | solution.py:28
  49.1 5.5 %collective-permute-start.2 = (bf16[2,256,768]{2,1,0:T(8,128)(2,1)S(1)}, bf16[2,256,768]{2,1,0:T(8,128)(2,1)S(1)}, u32[]{:S(2)}, u32[]{:S(2)}) collective-permute-start(bf16[2,256,768]{2,1,0:T(8,128)(2,1)S(1)} %pad_maximum_fusion.1), channel_id=1, source_target_pairs={{0,128},{1,129},{2,130},{3,131},{4,132},{5,133},{6,134},{7,135},{8... | collective-permute-start | bytes 2359304 | tf_op jit(solution)/shard_map/ppermute | solution.py:28
  56.5 10.0 %collective-permute-done.8 = bf16[4,192,512]{2,1,0:T(8,128)(2,1)S(1)} collective-permute-done((bf16[4,192,512]{2,1,0:T(8,128)(2,1)S(1)}, bf16[4,192,512]{2,1,0:T(8,128)(2,1)S(1)}, u32[]{:S(2)}, u32[]{:S(2)}) %collective-permute-start.8) | collective-permute-done | bytes 786464 | tf_op jit(solution)/shard_map/ppermute | solution.py:28
  69.7 2.7 %collective-permute-start.14 = (bf16[2,192,512]{2,1,0:T(8,128)(2,1)S(1)}, bf16[2,192,512]{2,1,0:T(8,128)(2,1)}, u32[]{:S(2)}, u32[]{:S(2)}) collective-permute-start(bf16[2,192,512]{2,1,0:T(8,128)(2,1)S(1)} %slice.143), channel_id=1, source_target_pairs={{0,24},{1,25},{2,26},{3,27},{4,28},{5,29},{6,30},{7,31},{8,0},{9,1... | collective-permute-start | bytes 1179656 | tf_op jit(solution)/shard_map/ppermute | solution.py:28
  74.5 5.9 %collective-permute-done.12 = bf16[2,192,512]{2,1,0:T(8,128)(2,1)} collective-permute-done((bf16[2,192,512]{2,1,0:T(8,128)(2,1)}, bf16[2,192,512]{2,1,0:T(8,128)(2,1)}, u32[]{:S(2)}, u32[]{:S(2)}) %collective-permute-start.12) | collective-permute-done | bytes 393248 | tf_op jit(solution)/shard_map/ppermute | solution.py:28
  90.9 3.3 %broadcast_add_fusion = bf16[3072,1024]{1,0:T(8,128)(2,1)S(1)} fusion(bf16[3072,1024]{1,0:T(8,128)(2,1)} %all-gather.5.cloned.1.call-done, bf16[]{:T(256)} %bitcast.10), kind=kLoop, calls=%fused_computation.5 | loop fusion | flops 3145728 | bytes 12582914 | tf_op jit(solution)/shard_map/add | solution.py:87
  102.0 3.4 %fusion.67 = f32[1024,512]{1,0:T(8,128)S(1)} fusion(bf16[3072,1024]{1,0:T(8,128)(2,1)S(1)} %broadcast_add_fusion, bf16[3072,512]{1,0:T(8,128)(2,1)S(1)} %bitcast.136), kind=kOutput, calls=%fused_computation.130 | convolution fusion | flops 3221225472 | bytes 11534336 | tf_op jit(solution)/shard_map/dot_general | solution.py:140
  105.5 5.8 %collective-permute-done.16 = bf16[512,512]{1,0:T(8,128)(2,1)S(1)} collective-permute-done((bf16[512,512]{1,0:T(8,128)(2,1)S(1)}, bf16[512,512]{1,0:T(8,128)(2,1)S(1)}, u32[]{:S(2)}, u32[]{:S(2)}) %collective-permute-start.16) | collective-permute-done | bytes 524320 | tf_op jit(solution)/shard_map/ppermute | solution.py:28
  113.1 2.4 %collective-permute-start.19 = (bf16[2,128,128]{2,1,0:T(8,128)(2,1)S(1)}, bf16[2,128,128]{2,1,0:T(8,128)(2,1)S(1)}, u32[]{:S(2)}, u32[]{:S(2)}) collective-permute-start(bf16[2,128,128]{2,1,0:T(8,128)(2,1)S(1)} %convolution_convert_fusion), channel_id=1, source_target_pairs={{0,32},{1,33},{2,34},{3,35},{4,36},{5,37},{6,38},{7,39},{8,40},{9,... | collective-permute-start | bytes 196616 | tf_op jit(solution)/shard_map/ppermute | solution.py:28
  119.5 2.5 %collective-permute-done.20 = bf16[2,128,128]{2,1,0:T(8,128)(2,1)S(1)} collective-permute-done((bf16[2,128,128]{2,1,0:T(8,128)(2,1)S(1)}, bf16[2,128,128]{2,1,0:T(8,128)(2,1)S(1)}, u32[]{:S(2)}, u32[]{:S(2)}) %collective-permute-start.20) | collective-permute-done | bytes 65568 | tf_op jit(solution)/shard_map/ppermute | solution.py:28
  122.2 4.0 %collective-permute-start.21 = (bf16[2,128,128]{2,1,0:T(8,128)(2,1)S(1)}, bf16[2,128,128]{2,1,0:T(8,128)(2,1)S(1)}, u32[]{:S(2)}, u32[]{:S(2)}) collective-permute-start(bf16[2,128,128]{2,1,0:T(8,128)(2,1)S(1)} %fusion.50), channel_id=1, source_target_pairs={{0,128},{1,129},{2,130},{3,131},{4,132},{5,133},{6,134},{7,135},{8... | collective-permute-start | bytes 196616 | tf_op jit(solution)/shard_map/ppermute | solution.py:28
  128.2 2.8 %multiply_reduce_fusion = (f32[2,512]{1,0:T(2,128)S(1)}, f32[2,128,512]{2,1,0:T(8,128)}) fusion(f32[2,128,512]{2,1,0:T(8,128)S(1)} %convolution_multiply_fusion, bf16[2,128,512]{2,1,0:T(8,128)(2,1)S(1)} %bitcast.151, f32[512,512]{1,0:T(8,128)S(1)} %copy-done.1, f32[2]{0:T(128)S(1)} %get-tuple-element.8, pred[512,512]{1,0:T(8,128)(4,1)} %fusion.22, ...), kind=kOutput, calls=%fused_computation.57 | convolution fusion | flops 270924800 | bytes 3412480 | tf_op jit(solution)/shard_map/hts,hes->het/dot_general | solution.py:188
  132.9 2.6 %collective-permute-start.24 = (bf16[256,512]{1,0:T(8,128)(2,1)S(1)}, bf16[256,512]{1,0:T(8,128)(2,1)S(1)}, u32[]{:S(2)}, u32[]{:S(2)}) collective-permute-start(bf16[256,512]{1,0:T(8,128)(2,1)S(1)} %bitcast.153), channel_id=1, source_target_pairs={{0,24},{1,25},{2,26},{3,27},{4,28},{5,29},{6,30},{7,31},{8,0},{9,1... | collective-permute-start | bytes 786440 | tf_op jit(solution)/shard_map/ppermute | solution.py:28
  136.6 6.0 %collective-permute-done.23 = bf16[256,512]{1,0:T(8,128)(2,1)S(1)} collective-permute-done((bf16[256,512]{1,0:T(8,128)(2,1)S(1)}, bf16[256,512]{1,0:T(8,128)(2,1)S(1)}, u32[]{:S(2)}, u32[]{:S(2)}) %collective-permute-start.23) | collective-permute-done | bytes 262176 | tf_op jit(solution)/shard_map/ppermute | solution.py:28
  152.5 3.8 %collective-permute-start.28 = (bf16[192,512]{1,0:T(8,128)(2,1)S(1)}, bf16[192,512]{1,0:T(8,128)(2,1)S(1)}, u32[]{:S(2)}, u32[]{:S(2)}) collective-permute-start(bf16[192,512]{1,0:T(8,128)(2,1)S(1)} %get-tuple-element.21), channel_id=1, source_target_pairs={{0,6},{1,7},{2,0},{3,1},{4,2},{5,3},{6,4},{7,5},{8,14},{9,15},{10,... | collective-permute-start | bytes 589832 | tf_op jit(solution)/shard_map/ppermute | solution.py:28
  156.3 2.6 %collective-permute-start.29 = (bf16[192,512]{1,0:T(8,128)(2,1)S(1)}, bf16[192,512]{1,0:T(8,128)(2,1)S(1)}, u32[]{:S(2)}, u32[]{:S(2)}) collective-permute-start(bf16[192,512]{1,0:T(8,128)(2,1)S(1)} %get-tuple-element.20), channel_id=1, source_target_pairs={{0,4},{1,5},{2,6},{3,7},{4,0},{5,1},{6,2},{7,3},{8,12},{9,13},{10,... | collective-permute-start | bytes 589832 | tf_op jit(solution)/shard_map/ppermute | solution.py:28
  158.9 9.4 %collective-permute-done.27 = bf16[192,512]{1,0:T(8,128)(2,1)S(1)} collective-permute-done((bf16[192,512]{1,0:T(8,128)(2,1)S(1)}, bf16[192,512]{1,0:T(8,128)(2,1)S(1)}, u32[]{:S(2)}, u32[]{:S(2)}) %collective-permute-start.27) | collective-permute-done | bytes 196640 | tf_op jit(solution)/shard_map/ppermute | solution.py:28
  168.3 3.8 %collective-permute-done.29 = bf16[192,512]{1,0:T(8,128)(2,1)S(1)} collective-permute-done((bf16[192,512]{1,0:T(8,128)(2,1)S(1)}, bf16[192,512]{1,0:T(8,128)(2,1)S(1)}, u32[]{:S(2)}, u32[]{:S(2)}) %collective-permute-start.29) | collective-permute-done | bytes 196640 | tf_op jit(solution)/shard_map/ppermute | solution.py:28
  (133 shorter events, 50.5 us)
Async XLA Ops:
  6.5 84.3 %all-gather.5.cloned.1.call-start = ((), (), s32[]{:S(2)}) async-start(), calls=%async_computation.1 | async-start | bytes 7864320 | tf_op jit(solution)/shard_map/all_gather | solution.py:115
  14.1 129.8 %all-gather.3.cloned.1.call-start = ((), (), s32[]{:S(2)}) async-start(), calls=%async_computation | async-start | bytes 3932160 | tf_op jit(solution)/shard_map/all_gather | solution.py:136
  14.1 34.8 %collective-permute-start = (bf16[256,768]{1,0:T(8,128)(2,1)}, bf16[256,768]{1,0:T(8,128)(2,1)S(1)}, u32[]{:S(2)}, u32[]{:S(2)}) collective-permute-start(bf16[256,768]{1,0:T(8,128)(2,1)} %bitcast), channel_id=1, source_target_pairs={{0,0},{1,1},{2,2},{3,3},{4,4},{5,5},{6,6},{7,7},{8,64},{9,65},{10,... | collective-permute-start | bytes 1179656 | tf_op jit(solution)/shard_map/ppermute | solution.py:28
  17.6 31.4 %collective-permute-start.1 = (bf16[256,768]{1,0:T(8,128)(2,1)}, bf16[256,768]{1,0:T(8,128)(2,1)S(1)}, u32[]{:S(2)}, u32[]{:S(2)}) collective-permute-start(bf16[256,768]{1,0:T(8,128)(2,1)} %bitcast), channel_id=1, source_target_pairs={{16,0},{17,1},{18,2},{19,3},{20,4},{21,5},{22,6},{23,7},{24,64},{2... | collective-permute-start | bytes 1179656 | tf_op jit(solution)/shard_map/ppermute | solution.py:28
  19.0 11.5 %collective-permute-start.4 = (bf16[192,512]{1,0:T(8,128)(2,1)S(1)}, bf16[192,512]{1,0:T(8,128)(2,1)S(1)}, u32[]{:S(2)}, u32[]{:S(2)}) collective-permute-start(bf16[192,512]{1,0:T(8,128)(2,1)S(1)} %collective-permute-done.3), channel_id=1, source_target_pairs={{0,2},{1,3},{2,4},{3,5},{4,6},{5,7},{6,0},{7,1},{8,10},{9,11},{10,... | collective-permute-start | bytes 589832 | tf_op jit(solution)/shard_map/ppermute | solution.py:28
  22.4 8.9 %collective-permute-start.5 = (bf16[192,512]{1,0:T(8,128)(2,1)S(1)}, bf16[192,512]{1,0:T(8,128)(2,1)S(1)}, u32[]{:S(2)}, u32[]{:S(2)}) collective-permute-start(bf16[192,512]{1,0:T(8,128)(2,1)S(1)} %collective-permute-done.3), channel_id=1, source_target_pairs={{0,6},{1,7},{2,0},{3,1},{4,2},{5,3},{6,4},{7,5},{8,14},{9,15},{10,... | collective-permute-start | bytes 589832 | tf_op jit(solution)/shard_map/ppermute | solution.py:28
  25.5 15.3 %collective-permute-start.6 = (bf16[192,512]{1,0:T(8,128)(2,1)S(1)}, bf16[192,512]{1,0:T(8,128)(2,1)S(1)}, u32[]{:S(2)}, u32[]{:S(2)}) collective-permute-start(bf16[192,512]{1,0:T(8,128)(2,1)S(1)} %collective-permute-done.3), channel_id=1, source_target_pairs={{0,4},{1,5},{2,6},{3,7},{4,0},{5,1},{6,2},{7,3},{8,12},{9,13},{10,... | collective-permute-start | bytes 589832 | tf_op jit(solution)/shard_map/ppermute | solution.py:28
  40.8 25.7 %collective-permute-start.8 = (bf16[4,192,512]{2,1,0:T(8,128)(2,1)S(1)}, bf16[4,192,512]{2,1,0:T(8,128)(2,1)S(1)}, u32[]{:S(2)}, u32[]{:S(2)}) collective-permute-start(bf16[4,192,512]{2,1,0:T(8,128)(2,1)S(1)} %bitcast_dynamic-update-slice_fusion), channel_id=1, source_target_pairs={{0,8},{1,9},{2,10},{3,11},{4,12},{5,13},{6,14},{7,15},{8,16},{9,17... | collective-permute-start | bytes 2359304 | tf_op jit(solution)/shard_map/ppermute | solution.py:28
  40.9 25.6 %collective-permute-start.10 = (bf16[4,192,512]{2,1,0:T(8,128)(2,1)S(1)}, bf16[4,192,512]{2,1,0:T(8,128)(2,1)S(1)}, u32[]{:S(2)}, u32[]{:S(2)}) collective-permute-start(bf16[4,192,512]{2,1,0:T(8,128)(2,1)S(1)} %bitcast_dynamic-update-slice_fusion), channel_id=1, source_target_pairs={{0,24},{1,25},{2,26},{3,27},{4,28},{5,29},{6,30},{7,31},{8,0},{9,1... | collective-permute-start | bytes 2359304 | tf_op jit(solution)/shard_map/ppermute | solution.py:28
  48.9 20.8 %collective-permute-start.7 = (bf16[4,192,512]{2,1,0:T(8,128)(2,1)S(1)}, bf16[4,192,512]{2,1,0:T(8,128)(2,1)S(1)}, u32[]{:S(2)}, u32[]{:S(2)}) collective-permute-start(bf16[4,192,512]{2,1,0:T(8,128)(2,1)S(1)} %bitcast_dynamic-update-slice_fusion), channel_id=1, source_target_pairs={{0,1},{1,0},{2,3},{3,2},{4,5},{5,4},{6,7},{7,6},{8,9},{9,8},{10,11... | collective-permute-start | bytes 2359304 | tf_op jit(solution)/shard_map/ppermute | solution.py:28
  49.1 24.4 %collective-permute-start.2 = (bf16[2,256,768]{2,1,0:T(8,128)(2,1)S(1)}, bf16[2,256,768]{2,1,0:T(8,128)(2,1)S(1)}, u32[]{:S(2)}, u32[]{:S(2)}) collective-permute-start(bf16[2,256,768]{2,1,0:T(8,128)(2,1)S(1)} %pad_maximum_fusion.1), channel_id=1, source_target_pairs={{0,128},{1,129},{2,130},{3,131},{4,132},{5,133},{6,134},{7,135},{8... | collective-permute-start | bytes 2359304 | tf_op jit(solution)/shard_map/ppermute | solution.py:28
  66.5 16.0 %collective-permute-start.9 = (bf16[4,192,512]{2,1,0:T(8,128)(2,1)S(1)}, bf16[4,192,512]{2,1,0:T(8,128)(2,1)}, u32[]{:S(2)}, u32[]{:S(2)}) collective-permute-start(bf16[4,192,512]{2,1,0:T(8,128)(2,1)S(1)} %collective-permute-done.8), channel_id=1, source_target_pairs={{0,1},{1,0},{2,3},{3,2},{4,5},{5,4},{6,7},{7,6},{8,9},{9,8},{10,11... | collective-permute-start | bytes 2359304 | tf_op jit(solution)/shard_map/ppermute | solution.py:28
  66.5 17.4 %collective-permute-start.11 = (bf16[4,192,512]{2,1,0:T(8,128)(2,1)S(1)}, bf16[4,192,512]{2,1,0:T(8,128)(2,1)}, u32[]{:S(2)}, u32[]{:S(2)}) collective-permute-start(bf16[4,192,512]{2,1,0:T(8,128)(2,1)S(1)} %collective-permute-done.10), channel_id=1, source_target_pairs={{0,1},{1,0},{2,3},{3,2},{4,5},{5,4},{6,7},{7,6},{8,9},{9,8},{10,11... | collective-permute-start | bytes 2359304 | tf_op jit(solution)/shard_map/ppermute | solution.py:28
  67.8 12.6 %collective-permute-start.12 = (bf16[2,192,512]{2,1,0:T(8,128)(2,1)}, bf16[2,192,512]{2,1,0:T(8,128)(2,1)}, u32[]{:S(2)}, u32[]{:S(2)}) collective-permute-start(bf16[2,192,512]{2,1,0:T(8,128)(2,1)} %slice_add_fusion.3), channel_id=1, source_target_pairs={{0,8},{1,9},{2,10},{3,11},{4,12},{5,13},{6,14},{7,15},{8,16},{9,17... | collective-permute-start | bytes 1179656 | tf_op jit(solution)/shard_map/ppermute | solution.py:28
  69.7 12.1 %collective-permute-start.14 = (bf16[2,192,512]{2,1,0:T(8,128)(2,1)S(1)}, bf16[2,192,512]{2,1,0:T(8,128)(2,1)}, u32[]{:S(2)}, u32[]{:S(2)}) collective-permute-start(bf16[2,192,512]{2,1,0:T(8,128)(2,1)S(1)} %slice.143), channel_id=1, source_target_pairs={{0,24},{1,25},{2,26},{3,27},{4,28},{5,29},{6,30},{7,31},{8,0},{9,1... | collective-permute-start | bytes 1179656 | tf_op jit(solution)/shard_map/ppermute | solution.py:28
  96.4 14.9 %collective-permute-start.16 = (bf16[512,512]{1,0:T(8,128)(2,1)S(1)}, bf16[512,512]{1,0:T(8,128)(2,1)S(1)}, u32[]{:S(2)}, u32[]{:S(2)}) collective-permute-start(bf16[512,512]{1,0:T(8,128)(2,1)S(1)} %fusion.7), channel_id=1, source_target_pairs={{0,128},{1,129},{2,130},{3,131},{4,132},{5,133},{6,134},{7,135},{8... | collective-permute-start | bytes 1572872 | tf_op jit(solution)/shard_map/ppermute | solution.py:28
  99.9 26.3 %collective-permute-start.17 = (bf16[256,512]{1,0:T(8,128)(2,1)S(1)}, bf16[256,512]{1,0:T(8,128)(2,1)S(1)}, u32[]{:S(2)}, u32[]{:S(2)}) collective-permute-start(bf16[256,512]{1,0:T(8,128)(2,1)S(1)} %get-tuple-element.22), channel_id=1, source_target_pairs={{0,128},{1,129},{2,130},{3,131},{4,132},{5,133},{6,134},{7,135},{8... | collective-permute-start | bytes 786440 | tf_op jit(solution)/shard_map/ppermute | solution.py:28
  100.5 25.7 %collective-permute-start.22 = (bf16[256,512]{1,0:T(8,128)(2,1)S(1)}, bf16[256,512]{1,0:T(8,128)(2,1)S(1)}, u32[]{:S(2)}, u32[]{:S(2)}) collective-permute-start(bf16[256,512]{1,0:T(8,128)(2,1)S(1)} %get-tuple-element.23), channel_id=1, source_target_pairs={{0,128},{1,129},{2,130},{3,131},{4,132},{5,133},{6,134},{7,135},{8... | collective-permute-start | bytes 786440 | tf_op jit(solution)/shard_map/ppermute | solution.py:28
  132.2 10.5 %collective-permute-start.23 = (bf16[256,512]{1,0:T(8,128)(2,1)S(1)}, bf16[256,512]{1,0:T(8,128)(2,1)S(1)}, u32[]{:S(2)}, u32[]{:S(2)}) collective-permute-start(bf16[256,512]{1,0:T(8,128)(2,1)S(1)} %bitcast.152), channel_id=1, source_target_pairs={{0,8},{1,9},{2,10},{3,11},{4,12},{5,13},{6,14},{7,15},{8,16},{9,17... | collective-permute-start | bytes 786440 | tf_op jit(solution)/shard_map/ppermute | solution.py:28
  132.9 13.1 %collective-permute-start.24 = (bf16[256,512]{1,0:T(8,128)(2,1)S(1)}, bf16[256,512]{1,0:T(8,128)(2,1)S(1)}, u32[]{:S(2)}, u32[]{:S(2)}) collective-permute-start(bf16[256,512]{1,0:T(8,128)(2,1)S(1)} %bitcast.153), channel_id=1, source_target_pairs={{0,24},{1,25},{2,26},{3,27},{4,28},{5,29},{6,30},{7,31},{8,0},{9,1... | collective-permute-start | bytes 786440 | tf_op jit(solution)/shard_map/ppermute | solution.py:28
  135.5 10.7 %collective-permute-start.25 = (bf16[256,512]{1,0:T(8,128)(2,1)S(1)}, bf16[256,512]{1,0:T(8,128)(2,1)S(1)}, u32[]{:S(2)}, u32[]{:S(2)}) collective-permute-start(bf16[256,512]{1,0:T(8,128)(2,1)S(1)} %bitcast.154), channel_id=1, source_target_pairs={{0,16},{1,17},{2,18},{3,19},{4,20},{5,21},{6,22},{7,23},{8,24},{9,... | collective-permute-start | bytes 786440 | tf_op jit(solution)/shard_map/ppermute | solution.py:28
  152.1 16.3 %collective-permute-start.27 = (bf16[192,512]{1,0:T(8,128)(2,1)S(1)}, bf16[192,512]{1,0:T(8,128)(2,1)S(1)}, u32[]{:S(2)}, u32[]{:S(2)}) collective-permute-start(bf16[192,512]{1,0:T(8,128)(2,1)S(1)} %get-tuple-element.19), channel_id=1, source_target_pairs={{0,2},{1,3},{2,4},{3,5},{4,6},{5,7},{6,0},{7,1},{8,10},{9,11},{10,... | collective-permute-start | bytes 589832 | tf_op jit(solution)/shard_map/ppermute | solution.py:28
  152.5 15.8 %collective-permute-start.28 = (bf16[192,512]{1,0:T(8,128)(2,1)S(1)}, bf16[192,512]{1,0:T(8,128)(2,1)S(1)}, u32[]{:S(2)}, u32[]{:S(2)}) collective-permute-start(bf16[192,512]{1,0:T(8,128)(2,1)S(1)} %get-tuple-element.21), channel_id=1, source_target_pairs={{0,6},{1,7},{2,0},{3,1},{4,2},{5,3},{6,4},{7,5},{8,14},{9,15},{10,... | collective-permute-start | bytes 589832 | tf_op jit(solution)/shard_map/ppermute | solution.py:28
  156.3 15.9 %collective-permute-start.29 = (bf16[192,512]{1,0:T(8,128)(2,1)S(1)}, bf16[192,512]{1,0:T(8,128)(2,1)S(1)}, u32[]{:S(2)}, u32[]{:S(2)}) collective-permute-start(bf16[192,512]{1,0:T(8,128)(2,1)S(1)} %get-tuple-element.20), channel_id=1, source_target_pairs={{0,4},{1,5},{2,6},{3,7},{4,0},{5,1},{6,2},{7,3},{8,12},{9,13},{10,... | collective-permute-start | bytes 589832 | tf_op jit(solution)/shard_map/ppermute | solution.py:28
  (21 other events, 204.7 us)
Sparse Core Ops, SparseCore 0:
  14.2 76.6 all-gather.4
  92.7 45.0 all-gather.2
